TPU v7x, 32 devices: a whole 2x2x4 slice. The times are simulated.
32 devices in a mesh: ctx: 8 (over y, x, core), head: 4 (over z).
Axes of the slice: x: 2, y: 2, z: 4, core: 2. Of those that a mesh axis runs over, the one named last changes fastest.
Arguments:
- mixed_in: bfloat16 [2048, 8192], P(('ctx', 'head')), may hold values from -6 to 6
- conv_weight: float32 [4, 8192], P(None, 'head'), may hold values from -3 to 3
- write_strength_logit: float32 [32, 2048], P('head', 'ctx'), may hold values from -10.5 to 2.2, as said below
- decay_log: float32 [32, 2048], P('head', 'ctx'), may hold values from -0.7 to 0, as said below
- initial_state: float32 [32, 128, 128], P('head'), may hold values from -6 to 6
- final_state_grad: float32 [32, 128, 128], P('head'), may hold values from -6 to 6
- grad_out: bfloat16 [2048, 4096], P('ctx', 'head'), may hold values from -6 to 6
Outputs:
- grad_mixed: bfloat16 [2048, 8192], P(('ctx', 'head'))
- grad_conv: float32 [4, 8192], P(None, 'head')
- grad_beta_logit: float32 [32, 2048], P('head', 'ctx')
- grad_decay_log: float32 [32, 2048], P('head', 'ctx')
Inputs may be any that keep to these rules, and one draw needn't show every extreme that they name: `write_strength_logit`: each value head's write strengths and decays vary from token to token. `decay_log`: every entry is negative.
All inputs are finite; a program needn't handle non-finite values.
Results may differ from a plain program's by a relative error of at most 0.001.
Values may be sent and summed in bfloat16 or wider, within the bound.
No kernel may reach another device: no remote copies, remote signals or barrier semaphores. Data moves between devices by JAX's collectives and lax.ppermute only.
A program may use at most 128 MiB of HBM per device.

v0:
```python
import jax
import jax.numpy as jnp
from jax import lax
from jax.sharding import PartitionSpec as P

HK = 16
VALUE_HEADS = 32
DK = 128
DV = 128
KW = 4
BLOCK = 64


highest = lax.Precision.HIGHEST
norm_eps = 1e-06


def from_behind(value, axis, by):
    devices = lax.axis_size(axis)
    pairs = [(i, i + by) for i in range(devices) if 0 <= i + by < devices]
    return lax.ppermute(value, axis, pairs)


def prefix(value, axis, combine, identity, reverse):
    devices, mine = (lax.axis_size(axis), lax.axis_index(axis))
    everything = jax.tree.map(lambda part: lax.all_gather(part, axis), value)
    start = jax.tree.map(
        lambda part, zero: jnp.broadcast_to(jnp.asarray(zero, part.dtype), part.shape),
        value,
        identity,
    )

    def step(k, before):
        at = devices - 1 - k if reverse else k
        reached = at > mine if reverse else at < mine
        new = combine(before, jax.tree.map(lambda part: part[at], everything))
        return jax.tree.map(lambda a, b: jnp.where(reached, a, b), new, before)

    return lax.fori_loop(0, devices, step, start)


def block_step(carried, pieces):
    state, transit = carried
    queries, key_feats, values, beta_gate, log_decay = pieces
    block_size = log_decay.shape[0]
    cumulative = jnp.cumsum(log_decay)
    row_ids = lax.broadcasted_iota(jnp.int32, (block_size, block_size), 0)
    col_ids = lax.broadcasted_iota(jnp.int32, (block_size, block_size), 1)
    causal = col_ids <= row_ids
    differ = jnp.where(causal, cumulative[:, None] - cumulative[None, :], 0.0)
    ratios = jnp.where(causal, jnp.exp(differ), 0.0)
    key_gram = jnp.dot(key_feats, key_feats.T, precision=highest)
    lower_part = jnp.where(col_ids < row_ids, beta_gate[:, None] * ratios * key_gram, 0.0)
    system = lower_part + jnp.eye(block_size, dtype=jnp.float32)
    decays = jnp.exp(cumulative)
    right_sides = jnp.concatenate(
        [beta_gate[:, None] * values, (beta_gate * decays)[:, None] * key_feats], axis=1
    )
    solved = jax.scipy.linalg.solve_triangular(system, right_sides, lower=True)
    width_v = values.shape[1]
    base_update = solved[:, :width_v]
    weights = solved[:, width_v:]
    update = base_update - jnp.dot(weights, state, precision=highest)
    scores = ratios * jnp.dot(queries, key_feats.T, precision=highest)
    output = decays[:, None] * jnp.dot(queries, state, precision=highest) + jnp.dot(
        scores, update, precision=highest
    )
    total_decay = jnp.exp(cumulative[-1])
    tail_keys = jnp.exp(cumulative[-1] - cumulative)[:, None] * key_feats
    new_state = total_decay * state + jnp.dot(tail_keys.T, update, precision=highest)
    step_map = total_decay * jnp.eye(key_feats.shape[1], dtype=jnp.float32) - jnp.dot(
        tail_keys.T, weights, precision=highest
    )
    new_transit = jnp.dot(step_map, transit, precision=highest)
    return ((new_state, new_transit), output)


def run_head(state, queries, key_feats, values, beta_gate, log_decay):
    blocks = queries.shape[0] // BLOCK
    pieces = (
        queries.reshape(blocks, BLOCK, -1),
        key_feats.reshape(blocks, BLOCK, -1),
        values.reshape(blocks, BLOCK, -1),
        beta_gate.reshape(blocks, BLOCK),
        log_decay.reshape(blocks, BLOCK),
    )
    start = (state, jnp.eye(key_feats.shape[1], dtype=jnp.float32))
    (state_end, transit), outputs = lax.scan(block_step, start, pieces)
    return (outputs.reshape(-1, values.shape[1]), state_end, transit)


def normalize(feats, factor):
    return feats * lax.rsqrt(jnp.sum(feats * feats, axis=-1, keepdims=True) + norm_eps) * factor


def mix_layer(state_in, extended, conv_weight, write_strength_logit, decay_log):
    row_count = extended.shape[0] - (KW - 1)
    filtered_signal = conv_weight[0] * extended[0:row_count]
    for tap in range(1, KW):
        filtered_signal = filtered_signal + conv_weight[tap] * extended[tap : tap + row_count]
    activated = jax.nn.silu(filtered_signal)
    ratio_heads = VALUE_HEADS // HK
    group_width = 2 * DK + ratio_heads * DV
    groups = activated.reshape(row_count, -1, group_width)
    key_heads = groups.shape[1]
    queries = normalize(groups[:, :, :DK], DK ** (-0.5))
    key_feats = normalize(groups[:, :, DK : 2 * DK], 1.0)
    values = (
        groups[:, :, 2 * DK :].reshape(row_count, key_heads * ratio_heads, DV).transpose(1, 0, 2)
    )
    queries = jnp.repeat(queries.transpose(1, 0, 2), ratio_heads, axis=0)
    key_feats = jnp.repeat(key_feats.transpose(1, 0, 2), ratio_heads, axis=0)
    beta_gate = jax.nn.sigmoid(write_strength_logit)
    outputs, state_out, transit = jax.vmap(run_head)(
        state_in, queries, key_feats, values, beta_gate, decay_log
    )
    result = outputs.transpose(1, 0, 2).reshape(row_count, -1)
    return ((result, state_out), transit)


def compose(earlier, later):
    matrix = jnp.einsum("hij,hjk->hik", later[0], earlier[0], precision=highest)
    offset = jnp.einsum("hij,hjk->hik", later[0], earlier[1], precision=highest) + later[1]
    return (matrix, offset)


def advance(maps, state):
    return jnp.einsum("hij,hjk->hik", maps[0], state, precision=highest) + maps[1]


def on_device(
    mixed_in,
    conv_weight,
    write_strength_logit,
    decay_log,
    initial_state,
    final_state_grad,
    grad_out,
):
    local_in = lax.all_to_all(mixed_in, "head", split_axis=1, concat_axis=0, tiled=True)
    edge_rows = from_behind(local_in[-(KW - 1) :], "ctx", 1)
    extended = jnp.concatenate([edge_rows, local_in], axis=0).astype(jnp.float32)
    cotangent = grad_out.astype(jnp.float32)
    zeros_state = jnp.zeros_like(initial_state)

    def from_state(state):
        return mix_layer(state, extended, conv_weight, write_strength_logit, decay_log)

    primal, pull_state, transit = jax.vjp(from_state, zeros_state, has_aux=True)
    offset = primal[1]
    local_grad = pull_state((cotangent, jnp.zeros_like(offset)))[0]
    flipped = jnp.swapaxes(transit, 1, 2)
    identity = (
        jnp.broadcast_to(jnp.eye(transit.shape[1], dtype=jnp.float32), transit.shape),
        jnp.zeros_like(offset),
    )
    earlier_map = prefix((transit, offset), "ctx", compose, identity, False)
    later_map = prefix((flipped, local_grad), "ctx", compose, identity, True)
    state_in = advance(earlier_map, initial_state)
    state_grad = advance(later_map, final_state_grad)

    def forward(ext_rows, weight_taps, logits, decay_logs):
        return mix_layer(state_in, ext_rows, weight_taps, logits, decay_logs)

    unused, pull_all, unused_transit = jax.vjp(
        forward, extended, conv_weight, write_strength_logit, decay_log, has_aux=True
    )
    grad_ext, grad_weight, grad_beta, grad_decay = pull_all((cotangent, state_grad))
    spilled = from_behind(grad_ext[: KW - 1], "ctx", -1)
    own_grad = grad_ext[KW - 1 :]
    own_grad = jnp.concatenate([own_grad[: -(KW - 1)], own_grad[-(KW - 1) :] + spilled], axis=0)
    returned = lax.all_to_all(
        own_grad.astype(jnp.bfloat16), "head", split_axis=0, concat_axis=1, tiled=True
    )
    weight_total = lax.psum(grad_weight, "ctx")
    return (returned, weight_total, grad_beta, grad_decay)


def solution(mesh):
    in_specs = (
        P(("ctx", "head"), None),
        P(None, "head"),
        P("head", "ctx"),
        P("head", "ctx"),
        P("head", None, None),
        P("head", None, None),
        P("ctx", "head"),
    )
    out_specs = (P(("ctx", "head"), None), P(None, "head"), P("head", "ctx"), P("head", "ctx"))
    return jax.shard_map(
        on_device, mesh=mesh, in_specs=in_specs, out_specs=out_specs, check_vma=False
    )
```

profile of v0, /device:TPU:28, one launch (start us, length us, event | category | flops | bytes accessed | tf_op | source)
XLA Modules:
  0.0 1085.1 jit_solution(12561949842308954976)
XLA Ops:
  9.6 5.1 all-to-all-start
  14.8 23.2 %all-to-all-done = bf16[64,4,2048]{2,0,1:T(8,128)(2,1)S(1)} async-done(((bf16[64,4,2048]{2,0,1:T(8,128)(2,1)}), bf16[64,4,2048]{2,0,1:T(8,128)(2,1)S(1)}, u32[]{:S(2)}, u32[]{:S(2)}) %all-to-all-start) | async-done | bytes 1048608 | tf_op jit(solution)/shard_map/all_to_all | solution.py:140
  40.2 3.8 collective-permute-done
  44.3 3.2 fusion.223
  64.2 213.3 %while.169 = (s32[]{:T(128)}, f32[8,128,128]{2,1,0:T(8,128)}, f32[8,128,128]{2,1,0:T(8,128)}, f32[4,8,64,128]{3,2,1,0:T(8,128)}, f32[4,8,64,1]{2,1,3,0:T(8,128)S...) while((s32[]{:T(128)}, f32[8,128,128]{2,1,0:T(8,128)}, ...), condition=%wide.region_4.6_spmd.clone.clone, body=%wide.region_2.5_spmd.clone.clone.sunk | while | flops 706425344 | bytes 11293616 | solution.py:88
  65.3 39.3 %custom-call.35 = f32[8,1,64,64]{2,3,1,0:T(8,128)S(1)} custom-call(f32[8,1,64,64]{3,2,1,0:T(8,128)S(1)} %fusion.414), custom_call_target="InvertDiagBlocksLowerTriangular" | custom-call | tf_op jit(solution)/shard_map/jvp(vmap())/while/body/eval_jaxpr/jit(_solve_triangular)/triangular_solve/custom-call.1 | solution.py:59
  117.1 39.3 %custom-call.35 = f32[8,1,64,64]{2,3,1,0:T(8,128)S(1)} custom-call(f32[8,1,64,64]{3,2,1,0:T(8,128)S(1)} %fusion.414), custom_call_target="InvertDiagBlocksLowerTriangular" | custom-call | tf_op jit(solution)/shard_map/jvp(vmap())/while/body/eval_jaxpr/jit(_solve_triangular)/triangular_solve/custom-call.1 | solution.py:59
  164.2 3.0 convolution_add_fusion.31
  170.9 39.3 %custom-call.35 = f32[8,1,64,64]{2,3,1,0:T(8,128)S(1)} custom-call(f32[8,1,64,64]{3,2,1,0:T(8,128)S(1)} %fusion.414), custom_call_target="InvertDiagBlocksLowerTriangular" | custom-call | tf_op jit(solution)/shard_map/jvp(vmap())/while/body/eval_jaxpr/jit(_solve_triangular)/triangular_solve/custom-call.1 | solution.py:59
  218.1 3.0 convolution_add_fusion.31
  224.8 39.3 %custom-call.35 = f32[8,1,64,64]{2,3,1,0:T(8,128)S(1)} custom-call(f32[8,1,64,64]{3,2,1,0:T(8,128)S(1)} %fusion.414), custom_call_target="InvertDiagBlocksLowerTriangular" | custom-call | tf_op jit(solution)/shard_map/jvp(vmap())/while/body/eval_jaxpr/jit(_solve_triangular)/triangular_solve/custom-call.1 | solution.py:59
  271.9 3.0 convolution_add_fusion.31
  286.7 31.1 %while.166 = (s32[]{:T(128)}, f32[8,128,128]{2,1,0:T(8,128)S(1)}, f32[4,8,1,1]{1,3,2,0:T(1,128)}, f32[4,8,64,128]{3,2,1,0:T(8,128)}, f32[4,8,64,1]{2,1,3,0:T(8,1...) while((s32[]{:T(128)}, f32[8,128,128]{2,1,0:T(8,128)S(1)}, ...), condition=%wide.region_6.8_spmd.clone, body=%wide.region_5.7_spmd.clone.sunk | while | flops 353173504 | bytes 5254363 | solution.py:88
  320.9 32.0 %all-gather.15.cloned.1.call-done = f32[64,128,128]{2,1,0:T(8,128)} async-done(((f32[8,128,128]{2,1,0:T(8,128)}), f32[64,128,128]{2,1,0:T(8,128)}) %all-gather.15.cloned.1.call-update) | async-done | bytes 4194320 | tf_op jit(solution)/shard_map/all_gather | solution.py:26
  353.8 50.9 %while.168 = (s32[]{:T(128)}, f32[8,128,128]{2,1,0:T(8,128)}, f32[8,128,128]{2,1,0:T(8,128)}, s32[]{:T(128)}, f32[8,8,128,128]{3,2,1,0:T(8,128)}, /*index=5*/f32[8,8,128,128]{3,2,1,0:T(8,128)}, s32[]{:T(128)}, s32[]{:T(128)}) while((s32[]{:T(128)}, f32[8,128,128]{2,1,0:T(8,128)}, f32[8,128,128]{2,1,0:T(8,128)}, s32[]{:T(128)}, ...), condition=%wide.region_10.12_spmd.clone, body=%wide.region_9.11_spmd.clone.sunk | while | flops 403308544 | bytes 8916100 | solution.py:39
  361.2 2.7 fusion.402
  386.7 2.7 fusion.402
  399.4 2.7 fusion.402
  420.0 221.0 %while.164 = (s32[]{:T(128)}, f32[8,128,128]{2,1,0:T(8,128)S(1)}, f32[4,8,64,64]{3,2,1,0:T(8,128)}, f32[4,8,128,64]{2,3,1,0:T(8,128)}, f32[4,8,64,64]{3,2,1,0:T(...) while((s32[]{:T(128)}, f32[8,128,128]{2,1,0:T(8,128)S(1)}, ...), condition=%wide.region_13.15_spmd.clone.clone, body=%wide.region_11.14_spmd.clone.clone.sunk | while | flops 504739840 | bytes 12791885 | solution.py:88
  421.8 2.7 bitcast_dynamic-update-slice_fusion.26
  424.7 39.3 %custom-call.33 = f32[8,1,64,64]{2,3,1,0:T(8,128)S(1)} custom-call(f32[8,1,64,64]{3,2,1,0:T(8,128)S(1)} %select_bitcast_fusion.4), custom_call_target="InvertDiagBlocksLowerTriangular" | custom-call | tf_op jit(solution)/shard_map/jvp(vmap())/while/body/eval_jaxpr/jit(_solve_triangular)/triangular_solve/custom-call.1 | solution.py:59
  477.0 2.7 bitcast_dynamic-update-slice_fusion.26
  480.0 39.3 %custom-call.33 = f32[8,1,64,64]{2,3,1,0:T(8,128)S(1)} custom-call(f32[8,1,64,64]{3,2,1,0:T(8,128)S(1)} %select_bitcast_fusion.4), custom_call_target="InvertDiagBlocksLowerTriangular" | custom-call | tf_op jit(solution)/shard_map/jvp(vmap())/while/body/eval_jaxpr/jit(_solve_triangular)/triangular_solve/custom-call.1 | solution.py:59
  532.3 2.7 bitcast_dynamic-update-slice_fusion.26
  535.2 39.3 %custom-call.33 = f32[8,1,64,64]{2,3,1,0:T(8,128)S(1)} custom-call(f32[8,1,64,64]{3,2,1,0:T(8,128)S(1)} %select_bitcast_fusion.4), custom_call_target="InvertDiagBlocksLowerTriangular" | custom-call | tf_op jit(solution)/shard_map/jvp(vmap())/while/body/eval_jaxpr/jit(_solve_triangular)/triangular_solve/custom-call.1 | solution.py:59
  590.4 39.3 %custom-call.33 = f32[8,1,64,64]{2,3,1,0:T(8,128)S(1)} custom-call(f32[8,1,64,64]{3,2,1,0:T(8,128)S(1)} %select_bitcast_fusion.4), custom_call_target="InvertDiagBlocksLowerTriangular" | custom-call | tf_op jit(solution)/shard_map/jvp(vmap())/while/body/eval_jaxpr/jit(_solve_triangular)/triangular_solve/custom-call.1 | solution.py:59
  641.7 43.8 %while.167 = (s32[]{:T(128)}, f32[8,128,128]{2,1,0:T(8,128)S(1)}, f32[8,128,128]{2,1,0:T(8,128)}, s32[]{:T(128)}, f32[8,8,128,128]{3,2,1,0:T(8,128)}, /*index=5*...) while((s32[]{:T(128)}, f32[8,128,128]{2,1,0:T(8,128)S(1)}, ...), condition=%wide.region_8.10_spmd.clone, body=%wide.region_7.9_spmd.clone.sunk | while | flops 403308544 | bytes 6818474 | solution.py:39
  642.8 2.7 fusion.397
  648.3 2.7 fusion.397
  653.7 2.7 fusion.397
  659.2 2.7 fusion.397
  664.7 2.7 fusion.397
  670.2 2.7 fusion.397
  675.6 2.7 fusion.397
  692.2 328.8 %while.165 = (s32[]{:T(128)}, f32[8,128,128]{2,1,0:T(8,128)S(1)}, f32[4,8,64,128]{3,2,0,1:T(8,128)}, f32[4,8,64,128]{3,2,0,1:T(8,128)}, f32[4,8,64,128]{3,2,0,1:...) while((s32[]{:T(128)}, f32[8,128,128]{2,1,0:T(8,128)S(1)}, ...), condition=%wide.region_25.27_spmd.clone.clone, body=%wide.region_14.26_spmd.clone.clone.sunk | while | flops 1135419392 | bytes 23078908 | solution.py:88
  708.9 40.0 %custom-call.34 = f32[8,1,64,64]{2,3,1,0:T(8,128)} custom-call(f32[8,1,64,64]{3,2,1,0:T(8,128)S(1)} %select_bitcast_fusion.5), custom_call_target="InvertDiagBlocksLowerTriangular" | custom-call | tf_op jit(solution)/shard_map/transpose(jvp(vmap()))/while/body/eval_jaxpr/jit(_solve_triangular)/triangular_solve | solution.py:59
  755.2 3.1 fusion.373
  789.0 40.0 %custom-call.34 = f32[8,1,64,64]{2,3,1,0:T(8,128)} custom-call(f32[8,1,64,64]{3,2,1,0:T(8,128)S(1)} %select_bitcast_fusion.5), custom_call_target="InvertDiagBlocksLowerTriangular" | custom-call | tf_op jit(solution)/shard_map/transpose(jvp(vmap()))/while/body/eval_jaxpr/jit(_solve_triangular)/triangular_solve | solution.py:59
  835.4 3.1 fusion.373
  869.2 40.0 %custom-call.34 = f32[8,1,64,64]{2,3,1,0:T(8,128)} custom-call(f32[8,1,64,64]{3,2,1,0:T(8,128)S(1)} %select_bitcast_fusion.5), custom_call_target="InvertDiagBlocksLowerTriangular" | custom-call | tf_op jit(solution)/shard_map/transpose(jvp(vmap()))/while/body/eval_jaxpr/jit(_solve_triangular)/triangular_solve | solution.py:59
  915.5 3.1 fusion.373
  949.4 40.0 %custom-call.34 = f32[8,1,64,64]{2,3,1,0:T(8,128)} custom-call(f32[8,1,64,64]{3,2,1,0:T(8,128)S(1)} %select_bitcast_fusion.5), custom_call_target="InvertDiagBlocksLowerTriangular" | custom-call | tf_op jit(solution)/shard_map/transpose(jvp(vmap()))/while/body/eval_jaxpr/jit(_solve_triangular)/triangular_solve | solution.py:59
  995.7 3.1 fusion.373
  1031.2 3.1 copy.201
  1034.3 3.3 multiply_reduce_fusion.3
  1038.8 3.3 collective-permute-start.1
  1044.9 5.2 all-to-all-start.1
  1050.9 25.7 %psum.7 = f32[4,2048]{1,0:T(4,128)} all-reduce(f32[4,2048]{1,0:T(4,128)S(1)} %pad_add_fusion.6), channel_id=1, replica_groups=mesh['ctx'=8,'head'=4] {'ctx'}, use_global_device_ids=true, to_apply=%region_34.36 | all-reduce | flops 8192 | bytes 65536 | tf_op jit(solution)/shard_map/psum | solution.py:175
  (600 shorter events, 422.1 us)
Async XLA Ops:
  7.2 397.5 %copy-start = (f32[8,128,128]{2,1,0:T(8,128)S(1)}, f32[8,128,128]{2,1,0:T(8,128)}, u32[]{:S(2)}) copy-start(f32[8,128,128]{2,1,0:T(8,128)} %param.25) | copy-start | bytes 1572868
  7.2 7.5 copy-start.37
  7.2 7.5 copy-start.39
  7.2 32.9 %copy-start.40 = (f32[8,256]{1,0:T(8,128)S(1)}, f32[8,256]{1,0:T(8,128)}, u32[]{:S(2)}) copy-start(f32[8,256]{1,0:T(8,128)} %param.24) | copy-start | bytes 24580
  9.6 28.5 %all-to-all-start = ((bf16[64,4,2048]{2,0,1:T(8,128)(2,1)}), bf16[64,4,2048]{2,0,1:T(8,128)(2,1)S(1)}, u32[]{:S(2)}, u32[]{:S(2)}) async-start(bf16[64,4,2048]{2,0,1:T(8,128)(2,1)} %bitcast.443), calls=%async_computation | async-start | bytes 2097152 | tf_op jit(solution)/shard_map/all_to_all | solution.py:140
  14.7 306.2 %all-gather.13.cloned.1.call-start = ((), (), s32[]{:S(2)}) async-start(), calls=%async_computation.4 | async-start | bytes 4718592 | tf_op jit(solution)/shard_map/all_gather | solution.py:26
  14.7 32.8 %copy-start.22 = (f32[1,2048]{1,0:T(1,128)}, f32[1,2048]{1,0:T(1,128)S(1)}, u32[]{:S(2)}) copy-start(f32[1,2048]{1,0:T(1,128)S(1)} %get-tuple-element.3235) | copy-start | bytes 24580
  14.8 32.8 %copy-start.24 = (f32[1,2048]{1,0:T(1,128)}, f32[1,2048]{1,0:T(1,128)S(1)}, u32[]{:S(2)}) copy-start(f32[1,2048]{1,0:T(1,128)S(1)} %get-tuple-element.3236) | copy-start | bytes 24580
  14.8 32.7 %copy-start.26 = (f32[1,2048]{1,0:T(1,128)}, f32[1,2048]{1,0:T(1,128)S(1)}, u32[]{:S(2)}) copy-start(f32[1,2048]{1,0:T(1,128)S(1)} %get-tuple-element.3237) | copy-start | bytes 24580
  14.8 32.7 %copy-start.28 = (f32[1,2048]{1,0:T(1,128)}, f32[1,2048]{1,0:T(1,128)S(1)}, u32[]{:S(2)}) copy-start(f32[1,2048]{1,0:T(1,128)S(1)} %get-tuple-element.3238) | copy-start | bytes 24580
  38.0 6.0 collective-permute-start
  44.3 3.2 copy-start.2
  277.5 7.8 copy-start.4
  277.5 7.8 copy-start.17
  277.5 75.4 %all-gather.15.cloned.1.call-start = ((), (), s32[]{:S(2)}) async-start(), calls=%async_computation.5 | async-start | bytes 4718592 | tf_op jit(solution)/shard_map/all_gather | solution.py:26
  278.3 362.8 %all-gather.11.cloned.1.call-start = ((), (), s32[]{:S(2)}) async-start(), calls=%async_computation.3 | async-start | bytes 4718592 | tf_op jit(solution)/shard_map/all_gather | solution.py:26
  318.7 322.4 %all-gather.9.cloned.1.call-start = ((), (), s32[]{:S(2)}) async-start(), calls=%async_computation.2 | async-start | bytes 4718592 | tf_op jit(solution)/shard_map/all_gather | solution.py:26
  353.8 3.8 copy-start.9
  360.1 3.8 copy-start.9
  366.5 3.8 copy-start.9
  372.8 3.8 copy-start.9
  379.2 3.8 copy-start.9
  385.6 3.8 copy-start.9
  391.9 3.8 copy-start.9
  398.3 3.8 copy-start.9
  748.8 5.0 copy-start.7
  755.2 8.9 copy-start.6
  829.0 5.0 copy-start.7
  835.4 8.9 copy-start.6
  909.2 5.0 copy-start.7
  915.5 8.9 copy-start.6
  989.3 5.0 copy-start.7
  995.7 8.9 copy-start.6
  1021.1 2.8 copy-start.34
  1021.1 2.8 copy-start.13
  1021.1 2.8 copy-start.32
  1021.1 3.9 copy-start.15
  1025.0 2.9 copy-start.14
  1031.2 3.1 copy-start.3
  1034.3 3.4 copy-start.23
  1034.3 3.4 copy-start.25
  1034.3 3.4 copy-start.27
  1034.3 3.4 copy-start.29
  1038.8 4.9 collective-permute-start.1
  1043.7 6.4 copy-start.30
  1043.7 32.9 %copy-start.38 = (f32[8,256]{1,0:T(8,128)S(1)}, f32[8,256]{1,0:T(8,128)}, u32[]{:S(2)}) copy-start(f32[8,256]{1,0:T(8,128)} %param.23) | copy-start | bytes 24580
  1044.9 33.4 %copy-start.1 = (f32[8,128,128]{2,1,0:T(8,128)S(1)}, f32[8,128,128]{2,1,0:T(8,128)}, u32[]{:S(2)}) copy-start(f32[8,128,128]{2,1,0:T(8,128)} %param.25) | copy-start | bytes 1572868
  1044.9 32.4 %all-to-all-start.1 = ((bf16[4,64,2048]{2,1,0:T(8,128)(2,1)}), bf16[4,64,2048]{2,1,0:T(8,128)(2,1)S(1)}, u32[]{:S(2)}, u32[]{:S(2)}) async-start(bf16[4,64,2048]{2,1,0:T(8,128)(2,1)} %bitcast.43), calls=%async_computation.1 | async-start | bytes 2097152 | tf_op jit(solution)/shard_map/all_to_all | solution.py:172
  (15 other events, 13.0 us)
Sparse Core Ops, SparseCore 0:
  277.7 36.5 all-gather.12
  316.2 36.7 all-gather.14
  354.8 36.7 all-gather.10
  393.3 36.7 all-gather.8
where the time goes:
time: 1100 us; the launch traced here: 1090 us
  other arithmetic  539 us (49%)
  matrix products  303 us (28%)
  local copies, waits for them, and re-layouts  117 us (11%)
  waiting for transfers between devices  60.2 us (5%)
  blocking collectives  25.7 us (2%)
  starting transfers between devices  15.9 us (1%)
  between operations  14.8 us (1%)
    another operation x32, other arithmetic, block_step(): solved = jax.scipy.linalg.solve_triangular(system, right_sides, lower=True)  479 us
    dot_general x16, matrix products, compose(): jnp.einsum('hij,hjk->hik', later[0], earlier[1], precision=highest)  42.8 us
    dot_general x20, matrix products, block_step(): jnp.dot(tail_keys.T, update, precision=highest)  40.3 us
    dot_general x20, matrix products, block_step(): update = base_update - jnp.dot(weights, state, precision=highest)  35 us
    dot_general x16, matrix products, block_step(): jnp.dot(queries, state, precision=highest)  34.1 us
    dot_general x16, matrix products, compose(): matrix = jnp.einsum('hij,hjk->hik', later[0], earlier[0], precision=highest)  33.8 us
    all_gather x4, waiting for transfers between devices, prefix(): everything = jax.tree.map(lambda part: lax.all_gather(part, axis), value)  32.1 us
    dot_general x16, matrix products, block_step(): scores = ratios * jnp.dot(queries, key_feats.T, precision=highest)  31.6 us
  transfers between devices with their start and end apart: 8, of which 4 were waited for; matrix products, arithmetic and copies ran while one was open for 31% of the time, Pallas kernels for 0%

commit v1 on v0

v1 whole, which is shorter than its diff:
```python
import functools
import jax
import jax.numpy as jnp
from jax import lax
from jax.experimental import pallas as pl
from jax.experimental.pallas import tpu as pltpu
from jax.sharding import PartitionSpec as P

HK = 16
VALUE_HEADS = 32
DK = 128
DV = 128
KW = 4
RATIO = VALUE_HEADS // HK
GROUP = 2 * DK + RATIO * DV
TILE = 128
BASE = 8
HALO = 16
EDGE = 8

norm_eps = 1e-06
f32 = jnp.float32
bf16 = jnp.bfloat16
NN = (((1,), (0,)), ((), ()))
NT = (((1,), (1,)), ((), ()))


def split(a):
    high = a.astype(bf16)
    return (high, (a - high.astype(f32)).astype(bf16))


def mm(a, b, dims=NN):
    total = lax.dot_general(a[0], b[0], dims, preferred_element_type=f32)
    if len(b) > 1:
        total += lax.dot_general(a[0], b[1], dims, preferred_element_type=f32)
    if len(a) > 1:
        total += lax.dot_general(a[1], b[0], dims, preferred_element_type=f32)
    return total


def iotas(rows, cols):
    return (
        lax.broadcasted_iota(jnp.int32, (rows, cols), 0),
        lax.broadcasted_iota(jnp.int32, (rows, cols), 1),
    )


def tile_inverses(lowers):
    row, col = iotas(TILE, TILE)
    eye = jnp.where(row == col, 1.0, 0.0).astype(f32)
    width = BASE
    same = row // width == col // width
    powers = [jnp.where(same, -low, 0.0) for low in lowers]
    inverses = [eye + p for p in powers]
    reach = 2
    while reach < BASE:
        parts = [split(p) for p in powers]
        powers = [mm(p, p) for p in parts]
        parts = [split(p) for p in powers]
        inverses = [inv + mm(split(inv), p) for inv, p in zip(inverses, parts)]
        reach *= 2
    while width < TILE:
        same = row // width == col // width
        wider = row // (2 * width) == col // (2 * width)
        between = wider & jnp.logical_not(same)
        parts = [split(inv) for inv in inverses]
        inner = [
            mm(split(jnp.where(between, low, 0.0)), inv) for low, inv in zip(lowers, parts)
        ]
        inverses = [inv - mm(p, split(i)) for inv, p, i in zip(inverses, parts, inner)]
        width *= 2
    return inverses


def unit_lower_inverses(lowers):
    size = lowers[0].shape[0]
    if size == TILE:
        return tile_inverses(lowers)
    half = size // 2
    inverses = unit_lower_inverses(
        [low[:half, :half] for low in lowers] + [low[half:, half:] for low in lowers]
    )
    first, second = (inverses[: len(lowers)], inverses[len(lowers) :])
    inner = [mm(split(low[half:, :half]), split(inv)) for low, inv in zip(lowers, first)]
    below = [-mm(split(inv), split(i)) for inv, i in zip(second, inner)]
    zero = jnp.zeros((half, half), f32)
    return [
        jnp.concatenate(
            [jnp.concatenate([a, zero], axis=1), jnp.concatenate([c, b], axis=1)], axis=0
        )
        for a, b, c in zip(first, second, below)
    ]


def sigmoid(a):
    return 1.0 / (1.0 + jnp.exp(-a))


def unit_rows(a):
    scale = lax.rsqrt(jnp.sum(a * a, axis=-1, keepdims=True) + norm_eps)
    return (a * scale, scale)


def local_kernel(x_ref, halo_ref, w_ref, rows_ref, cols_ref, do_ref, conv_ref, saved_ref, maps_ref, ext):
    tokens = x_ref.shape[0]
    ext[:HALO] = halo_ref[...].astype(f32)
    ext[HALO:] = x_ref[...].astype(f32)
    start = HALO - (KW - 1)
    conv = w_ref[0:1] * ext[start : start + tokens]
    for tap in range(1, KW):
        conv += w_ref[tap : tap + 1] * ext[start + tap : start + tap + tokens]
    conv_ref[...] = conv
    act = conv * sigmoid(conv)
    q = unit_rows(act[:, :DK])[0] * DK**-0.5
    k = unit_rows(act[:, DK : 2 * DK])[0]
    qs, ks = (split(q), split(k))
    gram = mm(ks, ks, NT)
    kq = mm(ks, qs, NT)
    qt = split(q.T)
    kt = split(k.T)
    row, col = iotas(tokens, tokens)
    lowers = []
    for h in range(RATIO):
        cum_r, cum_c = (rows_ref[0, h : h + 1], cols_ref[0, :, h : h + 1])
        beta = cols_ref[0, :, RATIO + h : RATIO + h + 1]
        ratio = jnp.exp(jnp.minimum(cum_c - cum_r, 0.0))
        lowers.append(jnp.where(col < row, beta * ratio * gram, 0.0))
    inverses = unit_lower_inverses(lowers)
    for h in range(RATIO):
        cum_r, cum_c = (rows_ref[0, h : h + 1], cols_ref[0, :, h : h + 1])
        beta = cols_ref[0, :, RATIO + h : RATIO + h + 1]
        gamma = jnp.exp(cum_c)
        total = cum_c[tokens - 1 :]
        tail = jnp.exp(total - cum_c)
        v = act[:, 2 * DK + h * DV : 2 * DK + (h + 1) * DV]
        do = do_ref[:, h * DV : (h + 1) * DV]
        right = jnp.concatenate([beta * v, (beta * gamma) * k], axis=1)
        solved = mm(split(inverses[h]), split(right))
        scores_t = jnp.where(col >= row, jnp.exp(jnp.minimum(cum_r - cum_c, 0.0)) * kq, 0.0)
        du = mm(split(scores_t), (do,))
        pulled = mm(split(inverses[h].T), split(jnp.concatenate([du, tail * k], axis=1)))
        saved_ref[h, :, : DV + DK] = solved
        saved_ref[h, :, DV + DK :] = pulled
        packed = jnp.concatenate([tail * solved, (beta * gamma) * pulled[:, :DV]], axis=1)
        moved = mm(kt, split(packed))
        drow, dcol = iotas(DK, DK)
        maps_ref[h, 0] = jnp.where(drow == dcol, jnp.exp(total), 0.0) - moved[:, DV : DV + DK]
        maps_ref[h, 1] = moved[:, :DV]
        maps_ref[h, 2] = mm(qt, split(gamma * do.astype(f32))) - moved[:, DV + DK :]


def scan_kernel(maps_ref, first_ref, last_ref, out_ref):
    count = maps_ref.shape[0]
    state, adjoint = (first_ref[0], last_ref[0])
    for step in range(count):
        back = count - 1 - step
        out_ref[step, 0, 0] = state
        out_ref[back, 0, 1] = adjoint
        if step < count - 1:
            state = mm(split(maps_ref[step, 0, 0]), split(state)) + maps_ref[step, 0, 1]
            adjoint = mm(split(maps_ref[back, 0, 0].T), split(adjoint)) + maps_ref[back, 0, 2]


def grad_kernel(
    x_ref, halo_ref, w_ref, rows_ref, cols_ref, do_ref, conv_ref, saved_ref, ends_ref,
    own_ref, edge_ref, spill_ref, dw_ref, drows_ref, dcols_ref, ext, dext,
):
    tokens = x_ref.shape[0]
    conv = conv_ref[...]
    gate = sigmoid(conv)
    act = conv * gate
    qn, q_scale = unit_rows(act[:, :DK])
    q = qn * DK**-0.5
    k, k_scale = unit_rows(act[:, DK : 2 * DK])
    qs, ks = (split(q), split(k))
    gram = mm(ks, ks, NT)
    scores = mm(qs, ks, NT)
    row, col = iotas(tokens, tokens)
    dq, dk = (jnp.zeros((tokens, DK), f32), jnp.zeros((tokens, DK), f32))
    dscores, dgram = (jnp.zeros((tokens, tokens), f32), jnp.zeros((tokens, tokens), f32))
    dvs = []
    drows, dcols = ([], [])
    for h in range(RATIO):
        cum_r, cum_c = (rows_ref[0, h : h + 1], cols_ref[0, :, h : h + 1])
        beta = cols_ref[0, :, RATIO + h : RATIO + h + 1]
        gamma = jnp.exp(cum_c)
        total = cum_c[tokens - 1 :]
        tail = jnp.exp(total - cum_c)
        ratio = jnp.exp(jnp.minimum(cum_c - cum_r, 0.0))
        v = act[:, 2 * DK + h * DV : 2 * DK + (h + 1) * DV]
        do = (do_ref[:, h * DV : (h + 1) * DV],)
        state, adjoint = (ends_ref[h, 0], ends_ref[h, 1])
        ss, ds = (split(state), split(adjoint))
        u = saved_ref[h, :, :DV] - mm(split(saved_ref[h, :, DV : DV + DK]), ss)
        z = saved_ref[h, :, DV + DK : 2 * DV + DK] + mm(
            split(saved_ref[h, :, 2 * DV + DK :]), ds
        )
        us, zs = (split(u), split(z))
        dq_in = mm(do, ss, NT)
        dk_in = -mm(zs, ss, NT)
        dk_out = mm(us, ds, NT)
        score_part = jnp.where(col <= row, mm(do, us, NT) * ratio, 0.0)
        gram_part = jnp.where(col < row, mm(zs, us, NT) * -ratio, 0.0)
        gram_term = gram_part * gram
        dscores += score_part
        dgram += beta * gram_part
        both = beta * gram_term + score_part * scores
        gate_in = gamma * jnp.sum(dk_in * k, axis=1, keepdims=True)
        dbeta = jnp.sum(gram_term, axis=1, keepdims=True) + gate_in
        dbeta += jnp.sum(z * v, axis=1, keepdims=True)
        dvs.append(beta * z)
        dq += gamma * dq_in
        dk += (beta * gamma) * dk_in + tail * dk_out
        left = tail * jnp.sum(dk_out * k, axis=1, keepdims=True)
        dcum = jnp.sum(both, axis=1, keepdims=True) - left + beta * gate_in
        dcum += gamma * jnp.sum(dq_in * q, axis=1, keepdims=True)
        at_end = jnp.sum(left, axis=0, keepdims=True) + jnp.exp(total) * jnp.sum(
            jnp.sum(state * adjoint, axis=1, keepdims=True), axis=0, keepdims=True
        )
        last = lax.broadcasted_iota(jnp.int32, (tokens, 1), 0) == tokens - 1
        dcum += jnp.where(last, at_end, 0.0)
        dcols.append((dcum, dbeta))
        drows.append(jnp.sum(both, axis=0, keepdims=True))
    dss, dgs = (split(dscores), split(dgram + dgram.T))
    dq += mm(dss, ks)
    dk += mm(split(dscores.T), qs) + mm(dgs, ks)
    lane = lax.broadcasted_iota(jnp.int32, (tokens, 8), 1)
    packed = jnp.zeros((tokens, 8), f32)
    for h in range(RATIO):
        packed = jnp.where(lane == h, dcols[h][0], packed)
        packed = jnp.where(lane == RATIO + h, dcols[h][1], packed)
    dcols_ref[0] = packed
    drows_ref[0] = jnp.concatenate(drows + [jnp.zeros((8 - RATIO, tokens), f32)], axis=0)
    dqn = dq * DK**-0.5
    dq_raw = q_scale * (dqn - qn * jnp.sum(qn * dqn, axis=1, keepdims=True))
    dk_raw = k_scale * (dk - k * jnp.sum(k * dk, axis=1, keepdims=True))
    dact = jnp.concatenate([dq_raw, dk_raw] + dvs, axis=1)
    dconv = dact * (gate * (1.0 + conv * (1.0 - gate)))
    ext[:HALO] = halo_ref[...].astype(f32)
    ext[HALO:] = x_ref[...].astype(f32)
    start = HALO - (KW - 1)
    for tap in range(KW):
        dw_ref[tap : tap + 1] = jnp.sum(
            dconv * ext[start + tap : start + tap + tokens], axis=0, keepdims=True
        )
    zero = jnp.zeros((EDGE, GROUP), f32)
    dext[:EDGE] = zero
    dext[EDGE : EDGE + tokens] = dconv
    dext[EDGE + tokens :] = zero
    own = jnp.zeros((tokens, GROUP), f32)
    spill = jnp.zeros((EDGE, GROUP), f32)
    for tap in range(KW):
        begin = EDGE + KW - 1 - tap
        own += w_ref[tap : tap + 1] * dext[begin : begin + tokens]
        begin = KW - 1 - tap
        spill += w_ref[tap : tap + 1] * dext[begin : begin + EDGE]
    own_ref[...] = own.astype(bf16)
    edge_ref[...] = own[tokens - EDGE :]
    spill_ref[...] = spill


def params():
    return pltpu.CompilerParams(vmem_limit_bytes=48 * 1024 * 1024)


def from_behind(value, axis, by):
    devices = lax.axis_size(axis)
    pairs = [(i, i + by) for i in range(devices) if 0 <= i + by < devices]
    return lax.ppermute(value, axis, pairs)


def shape(*dims, dtype=f32):
    return jax.ShapeDtypeStruct(dims, dtype)


def local_pass(x, halo, weight, rows, cols, do):
    tokens, feats = x.shape
    groups = feats // GROUP
    heads = groups * RATIO
    width = 2 * (DV + DK)
    return pl.pallas_call(
        local_kernel,
        grid=(groups,),
        in_specs=[
            pl.BlockSpec((tokens, GROUP), lambda g: (0, g)),
            pl.BlockSpec((HALO, GROUP), lambda g: (0, g)),
            pl.BlockSpec((KW, GROUP), lambda g: (0, g)),
            pl.BlockSpec((1, 8, tokens), lambda g: (g, 0, 0)),
            pl.BlockSpec((1, tokens, 8), lambda g: (g, 0, 0)),
            pl.BlockSpec((tokens, RATIO * DV), lambda g: (0, g)),
        ],
        out_specs=[
            pl.BlockSpec((tokens, GROUP), lambda g: (0, g)),
            pl.BlockSpec((RATIO, tokens, width), lambda g: (g, 0, 0)),
            pl.BlockSpec((RATIO, 3, DK, DV), lambda g: (g, 0, 0, 0)),
        ],
        out_shape=[
            shape(tokens, feats),
            shape(heads, tokens, width),
            shape(heads, 3, DK, DV),
        ],
        scratch_shapes=[pltpu.VMEM((HALO + tokens, GROUP), f32)],
        compiler_params=params(),
        name="local_pass",
    )(x, halo, weight, rows, cols, do)


def scan_pass(maps, first, last):
    count, heads = maps.shape[:2]
    return pl.pallas_call(
        scan_kernel,
        grid=(heads,),
        in_specs=[
            pl.BlockSpec((count, 1, 3, DK, DV), lambda h: (0, h, 0, 0, 0)),
            pl.BlockSpec((1, DK, DV), lambda h: (h, 0, 0)),
            pl.BlockSpec((1, DK, DV), lambda h: (h, 0, 0)),
        ],
        out_specs=pl.BlockSpec((count, 1, 2, DK, DV), lambda h: (0, h, 0, 0, 0)),
        out_shape=shape(count, heads, 2, DK, DV),
        compiler_params=params(),
        name="scan_pass",
    )(maps, first, last)


def grad_pass(x, halo, weight, rows, cols, do, conv, saved, ends):
    tokens, feats = x.shape
    groups = feats // GROUP
    width = saved.shape[-1]
    return pl.pallas_call(
        grad_kernel,
        grid=(groups,),
        in_specs=[
            pl.BlockSpec((tokens, GROUP), lambda g: (0, g)),
            pl.BlockSpec((HALO, GROUP), lambda g: (0, g)),
            pl.BlockSpec((KW, GROUP), lambda g: (0, g)),
            pl.BlockSpec((1, 8, tokens), lambda g: (g, 0, 0)),
            pl.BlockSpec((1, tokens, 8), lambda g: (g, 0, 0)),
            pl.BlockSpec((tokens, RATIO * DV), lambda g: (0, g)),
            pl.BlockSpec((tokens, GROUP), lambda g: (0, g)),
            pl.BlockSpec((RATIO, tokens, width), lambda g: (g, 0, 0)),
            pl.BlockSpec((RATIO, 2, DK, DV), lambda g: (g, 0, 0, 0)),
        ],
        out_specs=[
            pl.BlockSpec((tokens, GROUP), lambda g: (0, g)),
            pl.BlockSpec((EDGE, GROUP), lambda g: (0, g)),
            pl.BlockSpec((EDGE, GROUP), lambda g: (0, g)),
            pl.BlockSpec((KW, GROUP), lambda g: (0, g)),
            pl.BlockSpec((1, 8, tokens), lambda g: (g, 0, 0)),
            pl.BlockSpec((1, tokens, 8), lambda g: (g, 0, 0)),
        ],
        out_shape=[
            shape(tokens, feats, dtype=bf16),
            shape(EDGE, feats),
            shape(EDGE, feats),
            shape(KW, feats),
            shape(groups, 8, tokens),
            shape(groups, tokens, 8),
        ],
        scratch_shapes=[
            pltpu.VMEM((HALO + tokens, GROUP), f32),
            pltpu.VMEM((tokens + 2 * EDGE, GROUP), f32),
        ],
        compiler_params=params(),
        name="grad_pass",
    )(x, halo, weight, rows, cols, do, conv, saved, ends)


def cross_blocks(maps, first, last):
    devices, mine = (lax.axis_size("ctx"), lax.axis_index("ctx"))
    heads = maps.shape[0]
    if heads % devices == 0:
        share = heads // devices
        maps = lax.all_to_all(maps, "ctx", split_axis=0, concat_axis=0, tiled=True)
        maps = maps.reshape(devices, share, 3, DK, DV)
        first = lax.dynamic_slice_in_dim(first, mine * share, share, 0)
        last = lax.dynamic_slice_in_dim(last, mine * share, share, 0)
        ends = scan_pass(maps, first, last).reshape(heads, 2, DK, DV)
        return lax.all_to_all(ends, "ctx", split_axis=0, concat_axis=0, tiled=True)
    ends = scan_pass(lax.all_gather(maps, "ctx"), first, last)
    return lax.dynamic_index_in_dim(ends, mine, 0, keepdims=False)


def on_device(
    mixed_in,
    conv_weight,
    write_strength_logit,
    decay_log,
    initial_state,
    final_state_grad,
    grad_out,
):
    heads, tokens = decay_log.shape
    groups = heads // RATIO
    beta = jax.nn.sigmoid(write_strength_logit)
    cumulative = jnp.cumsum(decay_log, axis=1)
    rows = jnp.concatenate(
        [
            cumulative.reshape(groups, RATIO, tokens),
            beta.reshape(groups, RATIO, tokens),
            jnp.zeros((groups, 8 - 2 * RATIO, tokens), f32),
        ],
        axis=1,
    )
    cols = rows.transpose(0, 2, 1)
    x = lax.all_to_all(mixed_in, "head", split_axis=1, concat_axis=0, tiled=True)
    halo = from_behind(x[-HALO:], "ctx", 1)
    conv, saved, maps = local_pass(x, halo, conv_weight, rows, cols, grad_out)
    ends = cross_blocks(maps, initial_state, final_state_grad)
    own, edge, spill, dweight, drows, dcols = grad_pass(
        x, halo, conv_weight, rows, cols, grad_out, conv, saved, ends
    )
    spilled = from_behind(spill[EDGE - (KW - 1) :], "ctx", -1)
    last_rows = (edge[EDGE - (KW - 1) :] + spilled).astype(bf16)
    own = jnp.concatenate([own[: -(KW - 1)], last_rows], axis=0)
    returned = lax.all_to_all(own, "head", split_axis=0, concat_axis=1, tiled=True)
    weight_total = lax.psum(dweight, "ctx")
    dcum = dcols[:, :, :RATIO].transpose(0, 2, 1) - drows[:, :RATIO]
    dcum = dcum.reshape(heads, tokens)
    grad_decay = lax.cumsum(dcum, axis=1, reverse=True)
    dbeta = dcols[:, :, RATIO : 2 * RATIO].transpose(0, 2, 1).reshape(heads, tokens)
    grad_beta = dbeta * beta * (1.0 - beta)
    return (returned, weight_total, grad_beta, grad_decay)


def solution(mesh):
    in_specs = (
        P(("ctx", "head"), None),
        P(None, "head"),
        P("head", "ctx"),
        P("head", "ctx"),
        P("head", None, None),
        P("head", None, None),
        P("ctx", "head"),
    )
    out_specs = (P(("ctx", "head"), None), P(None, "head"), P("head", "ctx"), P("head", "ctx"))
    return jax.shard_map(
        on_device, mesh=mesh, in_specs=in_specs, out_specs=out_specs, check_vma=False
    )
```

time: 1100 us -> 162 us (0.15); the launches traced: 1090 us -> 161 us
  other arithmetic: 539 us -> 5.76 us
  matrix products: 303 us -> 0 us
  local copies, waits for them, and re-layouts: 117 us -> 8.21 us
  Pallas kernels: 0 us -> 36.7 us
  blocking collectives: 25.7 us -> 43.8 us
  between operations: 14.8 us -> 0.82 us
  waiting for transfers between devices: 60.2 us -> 46.7 us
    another operation x49 -> x6, other arithmetic: 483 us -> 3.9 us  [the longest x32 479 us: block_step(): solved = jax.scipy.linalg.solve_triangular(system, right_sides, lower=True)]
    dot_general x146 -> x0, matrix products: 283 us -> none  [the longest x16 42.8 us: compose(): jnp.einsum('hij,hjk->hik', later[0], earlier[1], precision=highest)]
    pallas_call x0 -> x3, Pallas kernels: none -> 36.7 us  [the longest x1 21.1 us: local_pass(): pl.pallas_call(local_kernel, grid=(groups,), in_specs=[pl.BlockSpec((toke...]
    all_gather x4 -> x0, waiting for transfers between devices: 32.1 us -> none  [prefix(): everything = jax.tree.map(lambda part: lax.all_gather(part, axis), value)]
    while x69 -> x0, local copies, waits for them, and re-layouts: 24 us -> none
    another operation x29 -> x7, local copies, waits for them, and re-layouts: 21.3 us -> 0.16 us
    another operation x16 -> x0, matrix products: 20.5 us -> none  [block_step(): solved = jax.scipy.linalg.solve_triangular(system, right_sides, lower=True)]
    all_to_all x1 -> x2, waiting for transfers between devices: 0.01 us -> 18.5 us  [the longest x1 18.5 us: cross_blocks(): maps = lax.all_to_all(maps, 'ctx', split_axis=0, concat_axis=0, tiled=True)]
  transfers between devices with their start and end apart: 8 -> 5, of which waited for: 4 -> 4; matrix products, arithmetic and copies ran while one was open for 31% -> 4% of each run, Pallas kernels for 0% -> 0%
where the time goes in v1:
time: 162 us; the launch traced here: 161 us
  waiting for transfers between devices  46.7 us (29%)
  blocking collectives  43.8 us (27%)
  Pallas kernels  36.7 us (23%)
  starting transfers between devices  19.3 us (12%)
  local copies, waits for them, and re-layouts  8.21 us (5%)
  other arithmetic  5.76 us (4%)
    psum x1, blocking collectives, on_device(): weight_total = lax.psum(dweight, 'ctx')  26 us
    all_to_all x1, waiting for transfers between devices, on_device(): lax.all_to_all(mixed_in, 'head', split_axis=1, concat_axis=0, tiled=True)  22.3 us
    pallas_call x1, Pallas kernels, local_pass(): pl.pallas_call(local_kernel, grid=(groups,), in_specs=[pl.BlockSpec((toke...  21.1 us
    all_to_all x1, waiting for transfers between devices, cross_blocks(): maps = lax.all_to_all(maps, 'ctx', split_axis=0, concat_axis=0, tiled=True)  18.5 us
    all_to_all x1, blocking collectives, cross_blocks(): return lax.all_to_all(ends, 'ctx', split_axis=0, concat_axis=0, tiled=True)  17.8 us
    pallas_call x1, Pallas kernels, grad_pass(): pl.pallas_call(grad_kernel, grid=(groups,), in_specs=[pl.BlockSpec((token...  14.4 us
    ppermute x2, waiting for transfers between devices, from_behind(): return lax.ppermute(value, axis, pairs)  5.85 us
    all_to_all x1, starting transfers between devices, on_device(): lax.all_to_all(own, 'head', split_axis=0, concat_axis=1, tiled=True)  5.85 us
  transfers between devices with their start and end apart: 5, of which 4 were waited for; matrix products, arithmetic and copies ran while one was open for 4% of the time, Pallas kernels for 0%

profile of v1, /device:TPU:28, one launch (start us, length us, event | category | flops | bytes accessed | tf_op | source)
XLA Modules:
  0.0 161.2 jit_solution(1499254557771902125)
XLA Ops:
  0.6 0.0 copy-start.5
  0.6 0.0 copy-start.6
  0.7 0.0 copy-start
  0.7 0.0 copy-start.4
  0.7 2.4 %copy.46 = bf16[8,4,8,2048]{3,2,0,1:T(8,128)(2,1)} copy(bf16[8,4,8,2048]{3,2,1,0:T(8,128)(2,1)} %bitcast.31) | data formatting | bytes 2097152 | tf_op jit(solution)/shard_map/all_to_all | solution.py:406
  3.0 5.1 %all-to-all-start = ((bf16[64,4,2048]{2,0,1:T(8,128)(2,1)}), bf16[64,4,2048]{2,0,1:T(8,128)(2,1)S(1)}, u32[]{:S(2)}, u32[]{:S(2)}) async-start(bf16[64,4,2048]{2,0,1:T(8,128)(2,1)} %bitcast.20), calls=%async_computation | async-start | bytes 2097152 | tf_op jit(solution)/shard_map/all_to_all | solution.py:406
  8.1 0.0 copy-done.5
  8.2 0.0 copy-done.6
  8.2 0.6 reduce-window.14
  8.8 0.2 slice_reduce_fusion.1
  9.0 0.1 broadcast_add_fusion
  9.1 0.1 pad.4.clone
  9.1 22.3 %all-to-all-done = bf16[64,4,2048]{2,0,1:T(8,128)(2,1)S(1)} async-done(((bf16[64,4,2048]{2,0,1:T(8,128)(2,1)}), bf16[64,4,2048]{2,0,1:T(8,128)(2,1)S(1)}, u32[]{:S(2)}, u32[]{:S(2)}) %all-to-all-start) | async-done | bytes 1048608 | tf_op jit(solution)/shard_map/all_to_all | solution.py:406
  31.5 1.9 %collective-permute-start = (bf16[16,2048]{1,0:T(8,128)(2,1)S(1)}, bf16[16,2048]{1,0:T(8,128)(2,1)S(1)}, u32[]{:S(2)}, u32[]{:S(2)}) collective-permute-start(bf16[16,2048]{1,0:T(8,128)(2,1)S(1)} %slice.44), channel_id=1, source_target_pairs={{0,4},{4,8},{8,12},{12,16},{16,20},{20,24},{24,28},{1,5},{5,9},{9,... | collective-permute-start | bytes 196616 | tf_op jit(solution)/shard_map/ppermute | solution.py:270
  33.4 0.1 maximum_maximum_fusion.rows_ref
  33.5 0.2 copy.37
  33.7 4.3 %collective-permute-done.halo_ref = bf16[16,2048]{1,0:T(8,128)(2,1)S(1)} collective-permute-done((bf16[16,2048]{1,0:T(8,128)(2,1)S(1)}, bf16[16,2048]{1,0:T(8,128)(2,1)S(1)}, u32[]{:S(2)}, u32[]{:S(2)}) %collective-permute-start) | collective-permute-done | bytes 65568 | tf_op jit(solution)/shard_map/ppermute | solution.py:270
  38.0 0.0 copy-done
  38.0 0.0 copy-done.4
  38.0 21.1 %local_pass.1 = (f32[256,2048]{1,0:T(8,128)S(1)}, f32[8,256,512]{2,1,0:T(8,128)}, f32[8,3,128,128]{3,2,1,0:T(8,128)S(1)}) custom-call(bf16[256,2048]{1,0:T(8,128)(2,1)S(1)} %bitcast.23, bf16[16,2048]{1,0:T(8,128)(2,1)S(1)} %collective-permute-done.halo_ref, f32[4,2048]{1,0:T(4,128)S(1)} %copy-done.4, f32[4,8,256]{2,1,0:T(8,128)S(1)} %maximum_maximum_fusion.rows_ref, ...), custom_call_target="tpu_custom_call" | custom-call | tf_op jit(solution)/shard_map/local_pass/pallas_call | solution.py:282
  59.0 0.0 copy-start.2
  59.0 1.3 copy-done.2
  60.4 0.0 copy-start.3
  60.4 1.1 copy-done.3
  61.5 3.5 %all-to-all-start.1 = ((f32[8,3,128,128]{3,2,1,0:T(8,128)}), f32[8,3,128,128]{3,2,1,0:T(8,128)S(1)}, u32[]{:S(2)}, u32[]{:S(2)}) async-start(f32[8,3,128,128]{3,2,1,0:T(8,128)} %copy-done.3), calls=%async_computation.1 | async-start | bytes 3145728 | tf_op jit(solution)/shard_map/all_to_all | solution.py:374
  65.0 0.9 constant_dynamic-slice_fusion
  65.9 18.5 %all-to-all-done.1 = f32[8,3,128,128]{3,2,1,0:T(8,128)S(1)} async-done(((f32[8,3,128,128]{3,2,1,0:T(8,128)}), f32[8,3,128,128]{3,2,1,0:T(8,128)S(1)}, u32[]{:S(2)}, u32[]{:S(2)}) %all-to-all-start.1) | async-done | bytes 1572896 | tf_op jit(solution)/shard_map/all_to_all | solution.py:374
  84.4 0.0 copy-start.1
  84.4 1.3 scan_pass.1
  85.7 17.8 %all_to_all.48.ends_ref = f32[8,2,128,128]{3,2,1,0:T(8,128)S(1)} all-to-all(f32[8,2,128,128]{3,2,1,0:T(8,128)S(1)} %bitcast.28), channel_id=1, replica_groups=mesh['ctx'=8,'head'=4] {'ctx'}, dimensions={0} | all-to-all | bytes 2097152 | tf_op jit(solution)/shard_map/all_to_all | solution.py:379
  103.5 0.0 copy-done.1
  103.5 14.4 %grad_pass.1 = (bf16[256,2048]{1,0:T(8,128)(2,1)S(1)}, f32[8,2048]{1,0:T(8,128)S(1)}, f32[8,2048]{1,0:T(8,128)S(1)}, f32[4,2048]{1,0:T(4,128)S(1)}, f32[4,8,256]{2,1,0:T(8,128)S(1)}, /*index=5*/f32[4,256,8]{2,1,0:T(8,128)S(1)}) custom-call(bf16[256,2048]{1,0:T(8,128)(2,1)S(1)} %bitcast.24, bf16[16,2048]{1,0:T(8,128)(2,1)S(1)} %collective-permute-done.halo_ref, ...), custom_call_target="tpu_custom_call" | custom-call | tf_op jit(solution)/shard_map/grad_pass/pallas_call | solution.py:330
  117.9 2.9 %collective-permute-start.1 = (f32[3,2048]{1,0:T(4,128)S(1)}, f32[3,2048]{1,0:T(4,128)S(1)}, u32[]{:S(2)}, u32[]{:S(2)}) collective-permute-start(f32[3,2048]{1,0:T(4,128)S(1)} %slice.38), channel_id=1, source_target_pairs={{4,0},{8,4},{12,8},{16,12},{20,16},{24,20},{28,24},{5,1},{9,5},{13... | collective-permute-start | bytes 73736 | tf_op jit(solution)/shard_map/ppermute | solution.py:270
  120.8 1.6 collective-permute-done.1
  122.4 1.1 pad_maximum_fusion
  123.5 5.8 %all-to-all-start.3 = ((bf16[4,64,2048]{2,1,0:T(8,128)(2,1)}), bf16[4,64,2048]{2,1,0:T(8,128)(2,1)S(1)}, u32[]{:S(2)}, u32[]{:S(2)}) async-start(bf16[4,64,2048]{2,1,0:T(8,128)(2,1)} %bitcast.7), calls=%async_computation.3 | async-start | bytes 2097152 | tf_op jit(solution)/shard_map/all_to_all | solution.py:416
  129.3 0.2 slice_bitcast_fusion
  129.5 0.2 copy.39
  129.7 0.2 copy.40
  130.0 0.1 bitcast_subtract_fusion
  130.0 0.2 copy.41
  130.3 2.5 %reduce-window.16 = f32[8,2,128]{2,0,1:T(8,128)S(1)} reduce-window(f32[8,2,128]{2,0,1:T(8,128)S(1)} %copy.42, f32[]{:T(128)} %constant.6.clone.1), window={size=1x1x128 pad=0_0x0_0x0_127}, to_apply=%region_3.4 | reduce-window | flops 260096 | bytes 16388 | tf_op jit(solution)/shard_map/reduce-window.2
  132.8 0.1 slice_reduce_fusion
  132.9 26.0 %psum.7 = f32[4,2048]{1,0:T(4,128)} all-reduce(f32[4,2048]{1,0:T(4,128)S(1)} %get-tuple-element.19), channel_id=1, replica_groups=mesh['ctx'=8,'head'=4] {'ctx'}, use_global_device_ids=true, to_apply=%region_2.3 | all-reduce | flops 8192 | bytes 65536 | tf_op jit(solution)/shard_map/psum | solution.py:417
  158.9 0.7 add_bitcast_fusion
  159.6 0.6 subtract_multiply_fusion
  160.2 0.0 all-to-all-done.3
  160.2 1.0 copy.44
  (16 shorter events, 0.2 us)
Async XLA Ops:
  0.6 7.5 %copy-start.5 = (f32[8,256]{1,0:T(8,128)S(1)}, f32[8,256]{1,0:T(8,128)}, u32[]{:S(2)}) copy-start(f32[8,256]{1,0:T(8,128)} %param.9) | copy-start | bytes 24580
  0.6 7.5 %copy-start.6 = (f32[8,256]{1,0:T(8,128)S(1)}, f32[8,256]{1,0:T(8,128)}, u32[]{:S(2)}) copy-start(f32[8,256]{1,0:T(8,128)} %param.10) | copy-start | bytes 24580
  0.7 37.3 %copy-start = (bf16[256,1024]{1,0:T(8,128)(2,1)S(1)}, bf16[256,1024]{1,0:T(8,128)(2,1)}, u32[]{:S(2)}) copy-start(bf16[256,1024]{1,0:T(8,128)(2,1)} %do_ref.3) | copy-start | bytes 1572868
  0.7 37.3 %copy-start.4 = (f32[4,2048]{1,0:T(4,128)S(1)}, f32[4,2048]{1,0:T(4,128)}, u32[]{:S(2)}) copy-start(f32[4,2048]{1,0:T(4,128)} %w_ref.3) | copy-start | bytes 98308
  3.0 28.5 %all-to-all-start = ((bf16[64,4,2048]{2,0,1:T(8,128)(2,1)}), bf16[64,4,2048]{2,0,1:T(8,128)(2,1)S(1)}, u32[]{:S(2)}, u32[]{:S(2)}) async-start(bf16[64,4,2048]{2,0,1:T(8,128)(2,1)} %bitcast.20), calls=%async_computation | async-start | bytes 2097152 | tf_op jit(solution)/shard_map/all_to_all | solution.py:406
  31.5 6.5 %collective-permute-start = (bf16[16,2048]{1,0:T(8,128)(2,1)S(1)}, bf16[16,2048]{1,0:T(8,128)(2,1)S(1)}, u32[]{:S(2)}, u32[]{:S(2)}) collective-permute-start(bf16[16,2048]{1,0:T(8,128)(2,1)S(1)} %slice.44), channel_id=1, source_target_pairs={{0,4},{4,8},{8,12},{12,16},{16,20},{20,24},{24,28},{1,5},{5,9},{9,... | collective-permute-start | bytes 196616 | tf_op jit(solution)/shard_map/ppermute | solution.py:270
  59.0 1.3 copy-start.2
  60.4 1.1 copy-start.3
  61.5 22.9 %all-to-all-start.1 = ((f32[8,3,128,128]{3,2,1,0:T(8,128)}), f32[8,3,128,128]{3,2,1,0:T(8,128)S(1)}, u32[]{:S(2)}, u32[]{:S(2)}) async-start(f32[8,3,128,128]{3,2,1,0:T(8,128)} %copy-done.3), calls=%async_computation.1 | async-start | bytes 3145728 | tf_op jit(solution)/shard_map/all_to_all | solution.py:374
  84.4 19.1 %copy-start.1 = (bf16[256,1024]{1,0:T(8,128)(2,1)S(1)}, bf16[256,1024]{1,0:T(8,128)(2,1)}, u32[]{:S(2)}) copy-start(bf16[256,1024]{1,0:T(8,128)(2,1)} %do_ref.3) | copy-start | bytes 1572868
  117.9 4.5 %collective-permute-start.1 = (f32[3,2048]{1,0:T(4,128)S(1)}, f32[3,2048]{1,0:T(4,128)S(1)}, u32[]{:S(2)}, u32[]{:S(2)}) collective-permute-start(f32[3,2048]{1,0:T(4,128)S(1)} %slice.38), channel_id=1, source_target_pairs={{4,0},{8,4},{12,8},{16,12},{20,16},{24,20},{28,24},{5,1},{9,5},{13... | collective-permute-start | bytes 73736 | tf_op jit(solution)/shard_map/ppermute | solution.py:270
  123.5 36.7 %all-to-all-start.3 = ((bf16[4,64,2048]{2,1,0:T(8,128)(2,1)}), bf16[4,64,2048]{2,1,0:T(8,128)(2,1)S(1)}, u32[]{:S(2)}, u32[]{:S(2)}) async-start(bf16[4,64,2048]{2,1,0:T(8,128)(2,1)} %bitcast.7), calls=%async_computation.3 | async-start | bytes 2097152 | tf_op jit(solution)/shard_map/all_to_all | solution.py:416

commit v2 on v1

v2 whole, which is shorter than its diff:
```python
import functools
import jax
import jax.numpy as jnp
from jax import lax
from jax.experimental import pallas as pl
from jax.experimental.pallas import tpu as pltpu
from jax.sharding import PartitionSpec as P

HK = 16
VALUE_HEADS = 32
DK = 128
DV = 128
KW = 4
RATIO = VALUE_HEADS // HK
GROUP = 2 * DK + RATIO * DV
TILE = 128
BASE = 2
EDGE = 16
VMEM_BYTES = 24 * 1024 * 1024

norm_eps = 1e-06
f32 = jnp.float32
bf16 = jnp.bfloat16
NN = (((1,), (0,)), ((), ()))
NT = (((1,), (1,)), ((), ()))


def split(a):
    high = a.astype(bf16)
    return (high, (a - high.astype(f32)).astype(bf16))


def dot(a, b, dims):
    return lax.dot_general(a, b, dims, preferred_element_type=f32)


def mm(a, b, dims=NN):
    inner_axis = dims[0][1][0]
    inner, outer = (b[0].shape[inner_axis], b[0].shape[1 - inner_axis])
    if len(b) == 1:
        return dot(a[0], b[0], dims) + dot(a[1], b[0], dims)
    high, low = b
    exact = len(a) == 1
    if outer <= TILE:
        wide = jnp.concatenate([high, low], axis=1 - inner_axis)
        if exact:
            total = dot(a[0], wide, dims)
        elif inner <= TILE:
            both = jnp.concatenate([wide, wide], axis=inner_axis)
            total = dot(jnp.concatenate(a, axis=1), both, dims)
        else:
            total = dot(a[0], wide, dims) + dot(a[1], wide, dims)
        return total[:, :outer] + total[:, outer:]
    if inner <= TILE:
        if exact:
            deep = jnp.concatenate([high, low], axis=inner_axis)
            return dot(jnp.concatenate([a[0], a[0]], axis=1), deep, dims)
        deep = jnp.concatenate([high, high], axis=inner_axis)
        return dot(jnp.concatenate(a, axis=1), deep, dims) + dot(a[0], low, dims)
    total = dot(a[0], high, dims) + dot(a[0], low, dims)
    return total if exact else total + dot(a[1], high, dims)


def iotas(rows, cols):
    return (
        lax.broadcasted_iota(jnp.int32, (rows, cols), 0),
        lax.broadcasted_iota(jnp.int32, (rows, cols), 1),
    )


def tile_inverses(lowers):
    row, col = iotas(TILE, TILE)
    eye = jnp.where(row == col, 1.0, 0.0).astype(f32)
    width = BASE
    same = row // width == col // width
    inverses = [eye - jnp.where(same, low, 0.0) for low in lowers]
    while width < TILE:
        same = row // width == col // width
        wider = row // (2 * width) == col // (2 * width)
        between = wider & jnp.logical_not(same)
        parts = [split(inv) for inv in inverses]
        inner = [
            mm(split(jnp.where(between, low, 0.0)), inv) for low, inv in zip(lowers, parts)
        ]
        inverses = [inv - mm(p, split(i)) for inv, p, i in zip(inverses, parts, inner)]
        width *= 2
    return inverses


def unit_lower_inverses(lowers):
    size = lowers[0].shape[0]
    if size == TILE:
        return tile_inverses(lowers)
    half = size // 2
    inverses = unit_lower_inverses(
        [low[:half, :half] for low in lowers] + [low[half:, half:] for low in lowers]
    )
    first, second = (inverses[: len(lowers)], inverses[len(lowers) :])
    inner = [mm(split(low[half:, :half]), split(inv)) for low, inv in zip(lowers, first)]
    below = [-mm(split(inv), split(i)) for inv, i in zip(second, inner)]
    zero = jnp.zeros((half, half), f32)
    return [
        jnp.concatenate(
            [jnp.concatenate([a, zero], axis=1), jnp.concatenate([c, b], axis=1)], axis=0
        )
        for a, b, c in zip(first, second, below)
    ]


def sigmoid(a):
    return 1.0 / (1.0 + jnp.exp(-a))


def unit_rows(a):
    scale = lax.rsqrt(jnp.sum(a * a, axis=-1, keepdims=True) + norm_eps)
    return (a * scale, scale)


def prefix_sums(a):
    count, size = a.shape
    high, low = split(a)
    rest = (a - high.astype(f32) - low.astype(f32)).astype(bf16)
    row, col = iotas(size, size)
    parts = dot(
        jnp.concatenate([high, low, rest], axis=0), jnp.where(row <= col, 1.0, 0.0).astype(bf16), NN
    )
    return parts[:count] + parts[count : 2 * count] + parts[2 * count :]


def gates_kernel(logit_ref, decay_ref, causal_ref, gates_ref, beta_ref):
    heads, tokens = decay_ref.shape
    row, col = iotas(tokens, tokens)
    cum = prefix_sums(decay_ref[...])
    beta = sigmoid(logit_ref[...])
    beta_ref[...] = beta
    cols = jnp.concatenate([cum, beta], axis=0).T
    for g in range(heads // RATIO):
        first = g * RATIO
        for h in range(first, first + RATIO):
            ratio = jnp.exp(jnp.minimum(cols[:, h : h + 1] - cum[h : h + 1], 0.0))
            causal_ref[h] = jnp.where(col <= row, ratio, 0.0)
        cum_c = cols[:, first : first + RATIO]
        gates_ref[g, :, :RATIO] = cols[:, heads + first : heads + first + RATIO]
        gates_ref[g, :, RATIO : 2 * RATIO] = jnp.exp(cum_c)
        gates_ref[g, :, 2 * RATIO : 3 * RATIO] = jnp.exp(cum_c[tokens - 1 :] - cum_c)


def wide_gates(gates_ref, group, h):
    tokens = gates_ref.shape[1]
    cols = [gates_ref[group, :, i * RATIO + h : i * RATIO + h + 1] for i in range(3)]
    return [jnp.broadcast_to(c, (tokens, DK)) for c in cols]


def group_at(place_ref, slot):
    first, flip = slot
    return first if flip is None else first + ((place_ref[1] & 1) ^ flip)


def lanes(start, size):
    return pl.ds(start if isinstance(start, int) else pl.multiple_of(start, size), size)


def local_kernel(slots, place_ref, mixed_ref, *refs):
    each = len(slots)
    outs, exts = (refs[-6 * each : -each], refs[-each:])
    groups = [group_at(place_ref, slot) for slot in slots]
    lowers = []
    for at, group in enumerate(groups):
        lowers += group_system(
            group, place_ref, mixed_ref, refs[: -6 * each], *outs[at : 3 * each : each], exts[at]
        )
    inverses = unit_lower_inverses(lowers)
    for at, group in enumerate(groups):
        group_maps(
            group, inverses[at * RATIO : (at + 1) * RATIO], refs[: -6 * each], *outs[each + at :: each]
        )


def group_system(group, place_ref, mixed_ref, refs, x_out, act_ref, slope_ref, ext):
    *piece_refs, halo_ref, w_ref, causal_ref, gates_in, do_ref = refs
    mine = place_ref[0]
    here = lanes(group * GROUP, GROUP)
    count = mixed_ref.shape[0]
    pieces = len(piece_refs) + 1
    tokens = pieces * count
    feats = mixed_ref.shape[1] // pieces
    ext[:EDGE] = halo_ref[:, here].astype(f32)
    x_out[:EDGE] = halo_ref[:, here]
    for s in range(pieces):
        if s == 0:
            piece = mixed_ref[:, pl.ds(pl.multiple_of(mine * feats + group * GROUP, GROUP), GROUP)]
        else:
            piece = piece_refs[s - 1][:, here]
        begin = pl.multiple_of(EDGE + (mine ^ s) * count, EDGE)
        ext[pl.ds(begin, count)] = piece.astype(f32)
        x_out[pl.ds(begin, count)] = piece
    start = EDGE - (KW - 1)
    conv = w_ref[0:1, here] * ext[start : start + tokens]
    for tap in range(1, KW):
        conv += w_ref[tap : tap + 1, here] * ext[start + tap : start + tap + tokens]
    gate = sigmoid(conv)
    act = conv * gate
    slope = gate + act * (1.0 - gate)
    qn, q_scale = unit_rows(act[:, :DK])
    k, k_scale = unit_rows(act[:, DK : 2 * DK])
    act_ref[:, :DK] = qn
    act_ref[:, DK : 2 * DK] = k
    act_ref[:, 2 * DK :] = act[:, 2 * DK :]
    slope_ref[:, :DK] = slope[:, :DK] * q_scale
    slope_ref[:, DK : 2 * DK] = slope[:, DK : 2 * DK] * k_scale
    slope_ref[:, 2 * DK :] = slope[:, 2 * DK :]
    ks = split(k)
    gram = mm(ks, ks, NT)
    row, col = iotas(tokens, tokens)
    gram = jnp.where(col < row, gram, 0.0)
    lowers = []
    for h in range(RATIO):
        beta = wide_gates(gates_in, group, h)[0]
        wide = jnp.concatenate([beta] * (tokens // DK), axis=1)
        lowers.append(causal_ref[group * RATIO + h] * gram * wide)
    return lowers


def group_maps(group, inverses, refs, act_ref, slope_ref, saved_ref, maps_ref):
    *_, causal_ref, gates_in, do_ref = refs
    tokens = act_ref.shape[0]
    q = act_ref[:, :DK] * DK**-0.5
    k = act_ref[:, DK : 2 * DK]
    scores = mm(split(q), split(k), NT)
    qt = split(q.T)
    kt = split(k.T)
    for h in range(RATIO):
        head = group * RATIO + h
        beta, gamma, tail = wide_gates(gates_in, group, h)
        beta_gamma = beta * gamma
        v = act_ref[:, 2 * DK + h * DV : 2 * DK + (h + 1) * DV]
        do = do_ref[:, lanes(head * DV, DV)]
        solved = mm(split(inverses[h]), split(jnp.concatenate([beta * v, beta_gamma * k], axis=1)))
        du = mm(split((causal_ref[head] * scores).T), (do,))
        pulled = mm(split(inverses[h].T), split(jnp.concatenate([du, tail * k], axis=1)))
        saved_ref[h, :, : DV + DK] = solved
        saved_ref[h, :, DV + DK :] = pulled
        packed = [tail * solved[:, :DV], tail * solved[:, DV:], beta_gamma * pulled[:, :DV]]
        moved = mm(kt, split(jnp.concatenate(packed, axis=1)))
        drow, dcol = iotas(DK, DK)
        total = gamma[tokens - 1 :]
        maps_ref[h, 0] = jnp.where(drow == dcol, total, 0.0) - moved[:, DV : DV + DK]
        maps_ref[h, 1] = moved[:, :DV]
        maps_ref[h, 2] = mm(qt, split(gamma * do.astype(f32))) - moved[:, DV + DK :]


def ordered(core, own, other):
    return (jnp.where(core == 0, own, other), jnp.where(core == 0, other, own))


def compose_kernel(parts, place_ref, *refs):
    keeps, others, outs, held = (refs[:parts], refs[parts : 2 * parts], refs[2 * parts : -1], refs[-1])
    core, chip = (place_ref[1] & 1, place_ref[1] >> 1)
    share = keeps[0].shape[0]
    for p in range(parts):
        for i in range(share):
            maps0, maps1 = ordered(core, keeps[p][i], others[p][i])
            later = mm(split(maps1[0]), split(jnp.concatenate([maps0[0], maps0[1]], axis=1)))
            held[p * share + i, 0] = later[:, :DK]
            held[p * share + i, 1] = later[:, DK:] + maps1[1]
            held[p * share + i, 2] = mm(split(maps0[0].T), split(maps1[2])) + maps0[2]
    for s, out in enumerate(outs):
        out[...] = held[chip ^ s]


def chips_kernel(chips, place_ref, *refs):
    maps_refs, first_ref, last_ref, outs, held, ends = (
        refs[:chips], refs[chips], refs[chips + 1], refs[chips + 2 : -2], refs[-2], refs[-1],
    )
    chip = place_ref[1] >> 1
    for s, maps_ref in enumerate(maps_refs):
        held[chip ^ s] = maps_ref[...]
    share = RATIO
    head = (chip // share * 2 + (place_ref[1] & 1)) * share + chip % share
    state, adjoint = (first_ref[head], last_ref[head])
    for step in range(chips):
        back = chips - 1 - step
        ends[step, 0] = state
        ends[back, 1] = adjoint
        if step < chips - 1:
            state = mm(split(held[step, 0]), split(state)) + held[step, 1]
            adjoint = mm(split(held[back, 0].T), split(adjoint)) + held[back, 2]
    for s, out in enumerate(outs):
        out[...] = ends[chip ^ s]


def expand_kernel(chips, place_ref, *refs):
    ends_refs, refs = (refs[:chips], refs[chips:])
    *maps_refs, own_out, give_out, ends = refs
    parts = len(maps_refs) // 2
    keeps, others = (maps_refs[:parts], maps_refs[parts:])
    core, chip = (place_ref[1] & 1, place_ref[1] >> 1)
    for s, ends_ref in enumerate(ends_refs):
        ends[chip ^ s] = ends_ref[...]
    share = keeps[0].shape[0]
    for p in range(parts):
        for i in range(share):
            head = p * share + i
            state, adjoint = (ends[head, 0], ends[head, 1])
            maps0, maps1 = ordered(core, keeps[p][i], others[p][i])
            state1 = mm(split(maps0[0]), split(state)) + maps0[1]
            adjoint0 = mm(split(maps1[0].T), split(adjoint)) + maps1[2]
            own_out[head, 0], give_out[head, 0] = ordered(core, state, state1)
            own_out[head, 1], give_out[head, 1] = ordered(core, adjoint0, adjoint)


def scan_kernel(maps_ref, first_ref, last_ref, out_ref):
    count = maps_ref.shape[0]
    state, adjoint = (first_ref[0], last_ref[0])
    for step in range(count):
        back = count - 1 - step
        out_ref[step, 0, 0] = state
        out_ref[back, 0, 1] = adjoint
        if step < count - 1:
            state = mm(split(maps_ref[step, 0, 0]), split(state)) + maps_ref[step, 0, 1]
            adjoint = mm(split(maps_ref[back, 0, 0].T), split(adjoint)) + maps_ref[back, 0, 2]


def row_sums(a):
    return dot(jnp.ones((8, 2 * DK), bf16), jnp.concatenate(split(a), axis=1), NT)[:1]


def wide_row_sums(a):
    return dot(jnp.concatenate(split(a), axis=1), jnp.ones((2 * DK, DK), bf16), NN)


def grad_kernel(slots, sides, place_ref, *refs):
    each = len(slots)
    w_ref, beta_ref, causal_ref, gates_in, do_ref, *refs = refs
    ends_refs, refs = (refs[:sides], refs[sides:])
    kept, (*out_refs, extra_ref, gates_ref, dext, ext) = (refs[: 4 * each], refs[4 * each :])
    for at, slot in enumerate(slots):
        side, first = divmod(at * RATIO, each * RATIO // sides)
        group_grads(
            group_at(place_ref, slot), at, place_ref[0], *kept[4 * at : 4 * at + 4], w_ref, beta_ref,
            causal_ref, gates_in, do_ref, ends_refs[side].at[pl.ds(first, RATIO)], out_refs,
            extra_ref, gates_ref, dext, ext,
        )


def group_grads(
    group, at, mine, x_ref, act_ref, slope_ref, saved_ref, w_ref, beta_ref, causal_ref, gates_in,
    do_ref, ends_ref, out_refs, extra_ref, gates_ref, dext, ext,
):
    tokens = act_ref.shape[0]
    here = lanes(group * GROUP, GROUP)
    there = slice(at * GROUP, (at + 1) * GROUP)
    qn = act_ref[:, :DK]
    q = qn * DK**-0.5
    k = act_ref[:, DK : 2 * DK]
    qs, ks = (split(q), split(k))
    gram = mm(ks, ks, NT)
    scores = mm(qs, ks, NT)
    row, col = iotas(tokens, tokens)
    below = col < row
    suffix = jnp.where(row >= col, 1.0, 0.0).astype(bf16)
    dq, dk = (jnp.zeros((tokens, DK), f32), jnp.zeros((tokens, DK), f32))
    dscores, dgram = (jnp.zeros((tokens, tokens), f32), jnp.zeros((tokens, tokens), f32))
    dvs = []
    for h in range(RATIO):
        head = group * RATIO + h
        beta, gamma, tail = wide_gates(gates_in, group, h)
        v = act_ref[:, 2 * DK + h * DV : 2 * DK + (h + 1) * DV]
        do = (do_ref[:, lanes(head * DV, DV)],)
        state, adjoint = (ends_ref[h, 0], ends_ref[h, 1])
        ss, ds = (split(state), split(adjoint))
        u = saved_ref[h, :, :DV] - mm(split(saved_ref[h, :, DV : DV + DK]), ss)
        z = saved_ref[h, :, DV + DK : 2 * DV + DK] + mm(
            split(saved_ref[h, :, 2 * DV + DK :]), ds
        )
        dv = beta * z
        us, zs = (split(u), split(dv))
        dq_in = gamma * mm(do, ss, NT)
        dk_in = gamma * mm(zs, ss, NT)
        dk_out = tail * mm(us, ds, NT)
        causal = causal_ref[head]
        score_part = mm(do, us, NT) * causal
        gram_part = jnp.where(below, mm(zs, us, NT) * causal, 0.0)
        dscores += score_part
        dgram -= gram_part
        gram_term = gram_part * gram
        both = score_part * scores - gram_term
        dvs.append(dv)
        dq += dq_in
        dk += dk_out - dk_in
        key_in = dk_in * k
        left = dk_out * k
        parts = both[:, :DK]
        terms = gram_term[:, :DK]
        for begin in range(DK, tokens, DK):
            parts += both[:, begin : begin + DK]
            terms += gram_term[:, begin : begin + DK]
        dcum = row_sums(parts + dq_in * q - key_in - left) - jnp.sum(both, axis=0, keepdims=True)
        high, low = split(dcum)
        rest = (dcum - high.astype(f32) - low.astype(f32)).astype(bf16)
        stack = [high, low, rest, high, low, rest, high, low]
        summed = dot(jnp.concatenate(stack, axis=0), suffix, NN)
        at_end = jnp.sum(left, axis=0, keepdims=True) + gamma[tokens - 1 :] * jnp.sum(
            state * adjoint, axis=0, keepdims=True
        )
        gates_ref[at, h : h + 1] = (
            summed[0:1] + summed[1:2] + summed[2:3] + jnp.sum(at_end, axis=1, keepdims=True)
        )
        closed = 1.0 - beta_ref[pl.ds(head, 1)]
        gates_ref[at, RATIO + h : RATIO + h + 1] = closed * row_sums(dv * v - terms - key_in)
    dss, dgs = (split(dscores), split(dgram + dgram.T))
    dq += mm(dss, ks)
    dk += mm(split(dscores.T), qs) + mm(dgs, ks)
    dq *= DK**-0.5
    dconv = jnp.concatenate(
        [dq - qn * wide_row_sums(qn * dq), dk - k * wide_row_sums(k * dk)] + dvs, axis=1
    )
    dconv *= slope_ref[...]
    ext[...] = x_ref[...].astype(f32)
    start = EDGE - (KW - 1)
    for tap in range(KW):
        extra_ref[2 * EDGE + tap : 2 * EDGE + tap + 1, there] = jnp.sum(
            dconv * ext[start + tap : start + tap + tokens], axis=0, keepdims=True
        )
    zero = jnp.zeros((EDGE, GROUP), f32)
    dext[:EDGE] = zero
    dext[EDGE : EDGE + tokens] = dconv
    dext[EDGE + tokens :] = zero
    own = jnp.zeros((tokens, GROUP), f32)
    spill = jnp.zeros((EDGE, GROUP), f32)
    for tap in range(KW):
        begin = EDGE + KW - 1 - tap
        own += w_ref[tap : tap + 1, here] * dext[begin : begin + tokens]
        begin = KW - 1 - tap
        spill += w_ref[tap : tap + 1, here] * dext[begin : begin + EDGE]
    ext[:tokens] = own
    count = tokens // len(out_refs)
    for s, out_ref in enumerate(out_refs):
        begin = pl.multiple_of((mine ^ s) * count, EDGE)
        out_ref[:, there] = ext[pl.ds(begin, count)].astype(bf16)
    extra_ref[:EDGE, there] = own[tokens - EDGE :]
    extra_ref[EDGE : 2 * EDGE, there] = spill


def finish_kernel(slots, place_ref, extra_ref, gates_ref, *outs):
    edge_ref, spill_ref, dw_ref, decay_ref, beta_ref = outs
    for at, slot in enumerate(slots):
        group = group_at(place_ref, slot)
        here = lanes(group * GROUP, GROUP)
        there = slice(at * GROUP, (at + 1) * GROUP)
        edge_ref[:, here] = extra_ref[:EDGE, there]
        spill_ref[:, here] = extra_ref[EDGE : 2 * EDGE, there]
        dw_ref[:, here] = extra_ref[2 * EDGE :, there]
        for h in range(RATIO):
            decay_ref[pl.ds(group * RATIO + h, 1)] = gates_ref[at, h : h + 1]
            beta_ref[pl.ds(group * RATIO + h, 1)] = gates_ref[at, RATIO + h : RATIO + h + 1]


def pack_kernel(place_ref, mixed_ref, *outs):
    feats = mixed_ref.shape[1] // (len(outs) + 1)
    for s, out in enumerate(outs):
        out[...] = mixed_ref[:, lanes((place_ref[0] ^ (s + 1)) * feats, feats)]


def assemble_kernel(slots, place_ref, *refs):
    *refs, out_ref = refs
    pieces = len(refs) // 2
    rows = out_ref.shape[0]
    feats = out_ref.shape[1] // pieces
    for at, slot in enumerate(slots):
        for s in range(pieces):
            begin = (place_ref[0] ^ s) * feats + group_at(place_ref, slot) * GROUP
            out_ref[:, lanes(begin, GROUP)] = refs[s][:, at * GROUP : (at + 1) * GROUP]

    @pl.when(place_ref[0] == pieces - 1)
    def fix():
        for s in range(pieces):
            out_ref[rows - EDGE :, s * feats : (s + 1) * feats] = refs[pieces + s][...]


def shape(*dims, dtype=f32):
    return jax.ShapeDtypeStruct(dims, dtype)


def call(kernel, name, out_shape, place, args, scratch=(), flops=0):
    in_specs = [pl.BlockSpec(memory_space=pltpu.VMEM)] * len(args)
    if place is not None:
        in_specs = [pl.BlockSpec(memory_space=pltpu.SMEM)] + in_specs
        args = [place, *args]
    return pl.pallas_call(
        kernel,
        in_specs=in_specs,
        out_specs=jax.tree.map(lambda _: pl.BlockSpec(memory_space=pltpu.VMEM), out_shape),
        out_shape=out_shape,
        scratch_shapes=scratch,
        compiler_params=pltpu.CompilerParams(vmem_limit_bytes=VMEM_BYTES),
        cost_estimate=pl.CostEstimate(flops=flops, bytes_accessed=1 << 20, transcendentals=0),
        name=name,
    )(*args)


def from_behind(value, axis, by):
    devices = lax.axis_size(axis)
    pairs = [(i, i + by) for i in range(devices) if 0 <= i + by < devices]
    return lax.ppermute(value, axis, pairs)


def across(value, axis, by):
    return lax.ppermute(value, axis, [(i, i ^ by) for i in range(lax.axis_size(axis))])


def local_pass(place, slots, mixed_in, received, halo, weight, gates, do):
    tokens = gates[0].shape[1]
    each = len(slots)
    outs = call(
        functools.partial(local_kernel, slots),
        "local_pass",
        [shape(EDGE + tokens, GROUP, dtype=bf16)] * each
        + [shape(tokens, GROUP)] * (2 * each)
        + [shape(RATIO, tokens, 2 * (DV + DK))] * each
        + [shape(RATIO, 3, DK, DV)] * each,
        place,
        [mixed_in, *received, halo, weight, *gates, do],
        [pltpu.VMEM((EDGE + tokens, GROUP), f32)] * each,
        flops=each * 6 * 10**9,
    )
    kept = [outs[at : 4 * each : each] for at in range(each)]
    return (kept, outs[4 * each :])


def grad_pass(place, slots, kept, ends, weight, beta, gates, do, pieces):
    tokens = do.shape[0]
    each = len(slots)
    outs = call(
        functools.partial(grad_kernel, slots, len(ends)),
        "grad_pass",
        [shape(tokens // pieces, each * GROUP, dtype=bf16)] * pieces
        + [shape(2 * EDGE + KW, each * GROUP), shape(each, 2 * RATIO, tokens)],
        place,
        [weight, beta, *gates, do, *ends, *[a for part in kept for a in part]],
        [pltpu.VMEM((tokens + 2 * EDGE, GROUP), f32), pltpu.VMEM((tokens + EDGE, GROUP), f32)],
        flops=each * 4 * 10**9,
    )
    return (outs[:pieces], *outs[pieces:])


def scan_pass(maps, first, last):
    count, heads = maps.shape[:2]
    return pl.pallas_call(
        scan_kernel,
        grid=(heads,),
        in_specs=[
            pl.BlockSpec((count, 1, 3, DK, DV), lambda h: (0, h, 0, 0, 0)),
            pl.BlockSpec((1, DK, DV), lambda h: (h, 0, 0)),
            pl.BlockSpec((1, DK, DV), lambda h: (h, 0, 0)),
        ],
        out_specs=pl.BlockSpec((count, 1, 2, DK, DV), lambda h: (0, h, 0, 0, 0)),
        out_shape=shape(count, heads, 2, DK, DV),
        compiler_params=pltpu.CompilerParams(vmem_limit_bytes=4 * VMEM_BYTES),
        name="scan_pass",
    )(maps, first, last)


def cross_chips(place, keeps, others, initial_state, final_state_grad):
    parts = len(keeps)
    chips = parts * keeps[0].shape[0]
    joined = call(
        functools.partial(compose_kernel, parts),
        "join_cores",
        [shape(3, DK, DV)] * chips,
        place,
        [*keeps, *others],
        [pltpu.VMEM((chips, 3, DK, DV), f32)],
    )
    held = [joined[0]] + [across(joined[s], "ctx", 2 * s) for s in range(1, chips)]
    ends = call(
        functools.partial(chips_kernel, chips),
        "over_chips",
        [shape(2, DK, DV)] * chips,
        place,
        [*held, initial_state, final_state_grad],
        [pltpu.VMEM((chips, 3, DK, DV), f32), pltpu.VMEM((chips, 2, DK, DV), f32)],
    )
    ends = [ends[0]] + [across(ends[s], "ctx", 2 * s) for s in range(1, chips)]
    own, give = call(
        functools.partial(expand_kernel, chips),
        "within_chip",
        [shape(chips, 2, DK, DV)] * 2,
        place,
        [*ends, *keeps, *others],
        [pltpu.VMEM((chips, 2, DK, DV), f32)],
    )
    return (own, across(give, "ctx", 1))


def on_device(
    mixed_in,
    conv_weight,
    write_strength_logit,
    decay_log,
    initial_state,
    final_state_grad,
    grad_out,
):
    devices, pieces = (lax.axis_size("ctx"), lax.axis_size("head"))
    heads, tokens = decay_log.shape
    groups = heads // RATIO
    feats = groups * GROUP
    paired = heads == devices and groups == 4
    slots = tuple((g, None) for g in range(groups))
    if paired:
        slots = tuple((g, flip) for flip in (1, 0) for g in range(0, groups, 2))
    place = jnp.stack([lax.axis_index("head"), lax.axis_index("ctx")]).astype(jnp.int32)
    packed = call(
        pack_kernel,
        "pack",
        [shape(mixed_in.shape[0], feats, dtype=bf16)] * (pieces - 1),
        place,
        [mixed_in],
    )
    arrived = [across(piece, "head", s + 1) for s, piece in enumerate(packed)]
    mine = lax.axis_index("head")
    edge_rows = mixed_in[mixed_in.shape[0] - EDGE :, feats * (pieces - 1) :]
    for s, piece in enumerate(arrived):
        edge_rows = jnp.where((mine ^ (s + 1)) == pieces - 1, piece[piece.shape[0] - EDGE :], edge_rows)
    halo = from_behind(edge_rows, "ctx", 1)
    *gates, beta = call(
        gates_kernel,
        "gates_pass",
        [shape(heads, tokens, tokens), shape(groups, tokens, 8), shape(heads, tokens)],
        None,
        [write_strength_logit, decay_log],
    )
    kept, maps = local_pass(
        place, slots, mixed_in, arrived, halo, conv_weight, gates, grad_out
    )
    if paired:
        others = [across(part, "ctx", 1) for part in maps[: groups // 2]]
        own_ends, other_ends = cross_chips(
            place, maps[groups // 2 :], others, initial_state, final_state_grad
        )
        ends = [other_ends, own_ends]
    else:
        gathered = lax.all_gather(jnp.concatenate(maps), "ctx")
        gathered = scan_pass(gathered, initial_state, final_state_grad)
        ends = [lax.dynamic_index_in_dim(gathered, lax.axis_index("ctx"), 0, keepdims=False)]
    out_pieces, extra, gate_grad = grad_pass(
        place, slots, kept, ends, conv_weight, beta, gates, grad_out, pieces
    )
    received = [out_pieces[0]] + [across(out_pieces[s], "head", s) for s in range(1, pieces)]
    edge, spill, dweight, grad_decay, grad_beta = call(
        functools.partial(finish_kernel, slots),
        "finish",
        [
            shape(EDGE, feats),
            shape(EDGE, feats),
            shape(KW, feats),
            shape(heads, tokens),
            shape(heads, tokens),
        ],
        place,
        [extra, gate_grad],
    )
    last = (edge + from_behind(spill, "ctx", -1)).astype(bf16)
    last_rows = [
        lax.ppermute(
            last, ("ctx", "head"), [(c * pieces + h, (c + 1) * pieces - 1) for c in range(devices)]
        )
        for h in range(pieces - 1)
    ] + [last]
    returned = call(
        functools.partial(assemble_kernel, slots),
        "assemble",
        shape(mixed_in.shape[0], feats * pieces, dtype=bf16),
        place,
        [*received, *last_rows],
    )
    if devices & (devices - 1) == 0:
        by = 1
        while by < devices:
            dweight = dweight + across(dweight, "ctx", by)
            by *= 2
    else:
        dweight = lax.psum(dweight, "ctx")
    return (returned, dweight, grad_beta, grad_decay)


def solution(mesh):
    in_specs = (
        P(("ctx", "head"), None),
        P(None, "head"),
        P("head", "ctx"),
        P("head", "ctx"),
        P("head", None, None),
        P("head", None, None),
        P("ctx", "head"),
    )
    out_specs = (P(("ctx", "head"), None), P(None, "head"), P("head", "ctx"), P("head", "ctx"))
    return jax.shard_map(
        on_device, mesh=mesh, in_specs=in_specs, out_specs=out_specs, check_vma=False
    )
```

time: 162 us -> 127 us (0.78)
  blocking collectives: 43.8 us -> 0 us
  waiting for transfers between devices: 46.7 us -> 57.4 us
  starting transfers between devices: 19.3 us -> 29.2 us
  Pallas kernels: 36.7 us -> 31.9 us
  other arithmetic: 5.76 us -> 1.59 us
  local copies, waits for them, and re-layouts: 8.21 us -> 5.66 us
    ppermute x0 -> x21, waiting for transfers between devices: none -> 55.2 us  [the longest x18 39.9 us: across(): lax.ppermute(value, axis, [(i, i ^ by) for i in range(lax.axis_size(axis))])]
    all_to_all x3 -> x0, waiting for transfers between devices: 40.8 us -> none  [the longest x1 22.3 us: on_device(): lax.all_to_all(mixed_in, 'head', split_axis=1, concat_axis=0, tiled=True)]
    psum x1 -> x0, blocking collectives: 26 us -> none  [on_device(): weight_total = lax.psum(dweight, 'ctx')]
    ppermute x0 -> x21, starting transfers between devices: none -> 24.4 us  [the longest x18 20.6 us: across(): lax.ppermute(value, axis, [(i, i ^ by) for i in range(lax.axis_size(axis))])]
    all_to_all x1 -> x0, blocking collectives: 17.8 us -> none  [cross_blocks(): return lax.all_to_all(ends, 'ctx', split_axis=0, concat_axis=0, tiled=True)]
    all_to_all x3 -> x0, starting transfers between devices: 14.5 us -> none  [the longest x1 5.85 us: on_device(): lax.all_to_all(own, 'head', split_axis=0, concat_axis=1, tiled=True)]
    pallas_call x3 -> x9, Pallas kernels: 36.7 us -> 31.9 us  [call(): pl.pallas_call(kernel, in_specs=in_specs, out_specs=jax.tree.map(lambda _...]
    another operation x6 -> x1, other arithmetic: 3.9 us -> 0.08 us  [on_device(): jnp.stack([lax.axis_index('head'), lax.axis_index('ctx')]).astype(jnp.int32)]
  transfers between devices with their start and end apart: 5 -> 23, of which waited for: 4 -> 14; matrix products, arithmetic and copies ran while one was open for 4% -> 1% of each run, Pallas kernels for 0% -> 1%
where the time goes in v2:
time: 127 us
  waiting for transfers between devices  57.4 us (45%)
  Pallas kernels  31.9 us (25%)
  starting transfers between devices  29.2 us (23%)
  local copies, waits for them, and re-layouts  5.66 us (4%)
  other arithmetic  1.59 us (1%)
    ppermute x18, waiting for transfers between devices, across(): lax.ppermute(value, axis, [(i, i ^ by) for i in range(lax.axis_size(axis))])  39.9 us
    pallas_call x9, Pallas kernels, call(): pl.pallas_call(kernel, in_specs=in_specs, out_specs=jax.tree.map(lambda _...  31.9 us
    ppermute x18, starting transfers between devices, across(): lax.ppermute(value, axis, [(i, i ^ by) for i in range(lax.axis_size(axis))])  20.6 us
    ppermute x3, waiting for transfers between devices, on_device(): lax.ppermute(last, ('ctx', 'head'), [(c * pieces + h, (c + 1) * pieces -...  15.4 us
    unnamed x20, local copies, waits for them, and re-layouts  5.66 us
    ppermute x2, starting transfers between devices, from_behind(): return lax.ppermute(value, axis, pairs)  4.79 us
    ppermute x3, starting transfers between devices, on_device(): lax.ppermute(last, ('ctx', 'head'), [(c * pieces + h, (c + 1) * pieces -...  3.85 us
  transfers between devices with their start and end apart: 23, of which 14 were waited for; matrix products, arithmetic and copies ran while one was open for 1% of the time, Pallas kernels for 1%

profile of v2, /device:TPU:28, one launch (start us, length us, event | category | flops | bytes accessed | tf_op | source)
XLA Modules:
  0.0 126.6 jit_solution(14493315902814908264)
XLA Ops:
  0.7 1.2 copy-done
  1.9 0.6 pack.1
  2.5 0.5 collective-permute-start
  3.1 0.3 collective-permute-start.1
  3.4 3.6 %collective-permute-start.2 = (bf16[64,2048]{1,0:T(8,128)(2,1)S(1)}, bf16[64,2048]{1,0:T(8,128)(2,1)S(1)}, u32[]{:S(2)}, u32[]{:S(2)}) collective-permute-start(bf16[64,2048]{1,0:T(8,128)(2,1)S(1)} %get-tuple-element.56), channel_id=1, source_target_pairs={{0,3},{1,2},{2,1},{3,0},{4,7},{5,6},{6,5},{7,4},{8,11},{9,10},{10,... | collective-permute-start | bytes 786440 | tf_op jit(solution)/shard_map/ppermute | solution.py:509
  7.0 7.9 %collective-permute-done.refs_0_ = bf16[64,2048]{1,0:T(8,128)(2,1)S(1)} collective-permute-done((bf16[64,2048]{1,0:T(8,128)(2,1)S(1)}, bf16[64,2048]{1,0:T(8,128)(2,1)S(1)}, u32[]{:S(2)}, u32[]{:S(2)}) %collective-permute-start) | collective-permute-done | bytes 262176 | tf_op jit(solution)/shard_map/ppermute | solution.py:509
  14.9 9.5 %collective-permute-done.1.refs_1_ = bf16[64,2048]{1,0:T(8,128)(2,1)S(1)} collective-permute-done((bf16[64,2048]{1,0:T(8,128)(2,1)S(1)}, bf16[64,2048]{1,0:T(8,128)(2,1)S(1)}, u32[]{:S(2)}, u32[]{:S(2)}) %collective-permute-start.1) | collective-permute-done | bytes 262176 | tf_op jit(solution)/shard_map/ppermute | solution.py:509
  24.4 0.9 fusion.1
  25.3 1.9 %collective-permute-start.3 = (bf16[16,2048]{1,0:T(8,128)(2,1)S(1)}, bf16[16,2048]{1,0:T(8,128)(2,1)S(1)}, u32[]{:S(2)}, u32[]{:S(2)}) collective-permute-start(bf16[16,2048]{1,0:T(8,128)(2,1)S(1)} %fusion.1), channel_id=1, source_target_pairs={{0,4},{4,8},{8,12},{12,16},{16,20},{20,24},{24,28},{1,5},{5,9},{9,... | collective-permute-start | bytes 196616 | tf_op jit(solution)/shard_map/ppermute | solution.py:505
  27.2 0.7 copy-done.4
  27.9 0.7 copy-done.5
  28.6 1.0 gates_pass.1
  29.6 2.2 %collective-permute-done.3.refs_3_ = bf16[16,2048]{1,0:T(8,128)(2,1)S(1)} collective-permute-done((bf16[16,2048]{1,0:T(8,128)(2,1)S(1)}, bf16[16,2048]{1,0:T(8,128)(2,1)S(1)}, u32[]{:S(2)}, u32[]{:S(2)}) %collective-permute-start.3) | collective-permute-done | bytes 65568 | tf_op jit(solution)/shard_map/ppermute | solution.py:505
  31.8 1.2 copy-done.1
  33.0 1.0 copy-done.6
  34.0 0.8 copy-done.8
  34.8 14.1 %local_pass.1 = (bf16[272,512]{1,0:T(8,128)(2,1)S(1)}, bf16[272,512]{1,0:T(8,128)(2,1)S(1)}, bf16[272,512]{1,0:T(8,128)(2,1)S(1)}, bf16[272,512]{1,0:T(8,128)(2,...) custom-call(s32[2]{0:T(128)S(1)} %pad_add_fusion.place_ref, ...), custom_call_target="tpu_custom_call" | custom-call | flops 24000000000 | bytes 1048576 | tf_op jit(solution)/shard_map/local_pass/pallas_call | solution.py:490
  49.0 0.5 collective-permute-start.5
  49.5 1.2 collective-permute-done.4.refs_2_.refs_6_
  50.7 0.6 collective-permute-done.5.refs_3_.refs_7_
  51.3 1.0 join_cores.1
  52.3 0.7 collective-permute-start.6
  53.0 0.5 collective-permute-start.7
  53.5 2.4 %collective-permute-start.8 = (f32[3,128,128]{2,1,0:T(8,128)S(1)}, f32[3,128,128]{2,1,0:T(8,128)S(1)}, u32[]{:S(2)}, u32[]{:S(2)}) collective-permute-start(f32[3,128,128]{2,1,0:T(8,128)S(1)} %get-tuple-element.64), channel_id=1, source_target_pairs={{0,24},{4,28},{8,16},{12,20},{16,8},{20,12},{24,0},{28,4},{1,25},{... | collective-permute-start | bytes 589832 | tf_op jit(solution)/shard_map/ppermute | solution.py:509
  55.9 4.3 %collective-permute-done.6.refs_1_ = f32[3,128,128]{2,1,0:T(8,128)S(1)} collective-permute-done((f32[3,128,128]{2,1,0:T(8,128)S(1)}, f32[3,128,128]{2,1,0:T(8,128)S(1)}, u32[]{:S(2)}, u32[]{:S(2)}) %collective-permute-start.6) | collective-permute-done | bytes 196640 | tf_op jit(solution)/shard_map/ppermute | solution.py:509
  60.1 3.7 %collective-permute-done.7.refs_2_ = f32[3,128,128]{2,1,0:T(8,128)S(1)} collective-permute-done((f32[3,128,128]{2,1,0:T(8,128)S(1)}, f32[3,128,128]{2,1,0:T(8,128)S(1)}, u32[]{:S(2)}, u32[]{:S(2)}) %collective-permute-start.7) | collective-permute-done | bytes 196640 | tf_op jit(solution)/shard_map/ppermute | solution.py:509
  63.9 1.2 over_chips.1
  65.1 1.5 %collective-permute-start.9 = (f32[2,128,128]{2,1,0:T(8,128)S(1)}, f32[2,128,128]{2,1,0:T(8,128)S(1)}, u32[]{:S(2)}, u32[]{:S(2)}) collective-permute-start(f32[2,128,128]{2,1,0:T(8,128)S(1)} %get-tuple-element.66), channel_id=1, source_target_pairs={{0,8},{4,12},{8,0},{12,4},{16,24},{20,28},{24,16},{28,20},{1,9},{5... | collective-permute-start | bytes 393224 | tf_op jit(solution)/shard_map/ppermute | solution.py:509
  66.9 1.8 %collective-permute-start.11 = (f32[2,128,128]{2,1,0:T(8,128)S(1)}, f32[2,128,128]{2,1,0:T(8,128)S(1)}, u32[]{:S(2)}, u32[]{:S(2)}) collective-permute-start(f32[2,128,128]{2,1,0:T(8,128)S(1)} %get-tuple-element.68), channel_id=1, source_target_pairs={{0,24},{4,28},{8,16},{12,20},{16,8},{20,12},{24,0},{28,4},{1,25},{... | collective-permute-start | bytes 393224 | tf_op jit(solution)/shard_map/ppermute | solution.py:509
  68.6 2.8 %collective-permute-done.9.refs_1_ = f32[2,128,128]{2,1,0:T(8,128)S(1)} collective-permute-done((f32[2,128,128]{2,1,0:T(8,128)S(1)}, f32[2,128,128]{2,1,0:T(8,128)S(1)}, u32[]{:S(2)}, u32[]{:S(2)}) %collective-permute-start.9) | collective-permute-done | bytes 131104 | tf_op jit(solution)/shard_map/ppermute | solution.py:509
  71.4 2.4 %collective-permute-done.10.refs_2_ = f32[2,128,128]{2,1,0:T(8,128)S(1)} collective-permute-done((f32[2,128,128]{2,1,0:T(8,128)S(1)}, f32[2,128,128]{2,1,0:T(8,128)S(1)}, u32[]{:S(2)}, u32[]{:S(2)}) %collective-permute-start.10) | collective-permute-done | bytes 131104 | tf_op jit(solution)/shard_map/ppermute | solution.py:509
  73.8 0.9 within_chip.1
  74.7 1.9 %collective-permute-done.12.refs_5_ = f32[4,2,128,128]{3,2,1,0:T(8,128)S(1)} collective-permute-done((f32[4,2,128,128]{3,2,1,0:T(8,128)S(1)}, f32[4,2,128,128]{3,2,1,0:T(8,128)S(1)}, u32[]{:S(2)}, u32[]{:S(2)}) %collective-permute-start.12) | collective-permute-done | bytes 524320 | tf_op jit(solution)/shard_map/ppermute | solution.py:509
  76.6 10.3 %grad_pass.1 = (bf16[64,2048]{1,0:T(8,128)(2,1)S(1)}, bf16[64,2048]{1,0:T(8,128)(2,1)S(1)}, bf16[64,2048]{1,0:T(8,128)(2,1)S(1)}, bf16[64,2048]{1,0:T(8,128)(2,1...) custom-call(s32[2]{0:T(128)S(1)} %pad_add_fusion.place_ref, f32[4,2048]{1,0:T(4,128)S(1)} %copy-done.9, ...), custom_call_target="tpu_custom_call" | custom-call | flops 16000000000 | bytes 1048576 | tf_op jit(solution)/shard_map/grad_pass/pallas_call | solution.py:490
  87.0 1.2 finish.1
  88.2 2.9 %collective-permute-start.16 = (f32[16,2048]{1,0:T(8,128)S(1)}, f32[16,2048]{1,0:T(8,128)S(1)}, u32[]{:S(2)}, u32[]{:S(2)}) collective-permute-start(f32[16,2048]{1,0:T(8,128)S(1)} %get-tuple-element.94), channel_id=1, source_target_pairs={{4,0},{8,4},{12,8},{16,12},{20,16},{24,20},{28,24},{5,1},{9,5},{13... | collective-permute-start | bytes 393224 | tf_op jit(solution)/shard_map/ppermute | solution.py:505
  91.1 4.8 %collective-permute-start.13 = (bf16[64,2048]{1,0:T(8,128)(2,1)S(1)}, bf16[64,2048]{1,0:T(8,128)(2,1)S(1)}, u32[]{:S(2)}, u32[]{:S(2)}) collective-permute-start(bf16[64,2048]{1,0:T(8,128)(2,1)S(1)} %get-tuple-element.88), channel_id=1, source_target_pairs={{0,1},{1,0},{2,3},{3,2},{4,5},{5,4},{6,7},{7,6},{8,9},{9,8},{10,11... | collective-permute-start | bytes 786440 | tf_op jit(solution)/shard_map/ppermute | solution.py:509
  96.0 2.4 %collective-permute-start.15 = (bf16[64,2048]{1,0:T(8,128)(2,1)S(1)}, bf16[64,2048]{1,0:T(8,128)(2,1)S(1)}, u32[]{:S(2)}, u32[]{:S(2)}) collective-permute-start(bf16[64,2048]{1,0:T(8,128)(2,1)S(1)} %get-tuple-element.90), channel_id=1, source_target_pairs={{0,3},{1,2},{2,1},{3,0},{4,7},{5,6},{6,5},{7,4},{8,11},{9,10},{10,... | collective-permute-start | bytes 786440 | tf_op jit(solution)/shard_map/ppermute | solution.py:509
  98.4 0.8 collective-permute-start.21
  99.3 1.3 %collective-permute-start.19 = (bf16[16,2048]{1,0:T(8,128)(2,1)S(1)}, bf16[16,2048]{1,0:T(8,128)(2,1)S(1)}, u32[]{:S(2)}, u32[]{:S(2)}) collective-permute-start(bf16[16,2048]{1,0:T(8,128)(2,1)S(1)} %add_convert_fusion.refs_7_), channel_id=1, source_target_pairs={{2,3},{6,7},{10,11},{14,15},{18,19},{22,23},{26,27},{30,31}} | collective-permute-start | bytes 196616 | tf_op jit(solution)/shard_map/ppermute | solution.py:666
  100.6 1.8 %collective-permute-done.21 = f32[4,2048]{1,0:T(4,128)S(1)} collective-permute-done((f32[4,2048]{1,0:T(4,128)S(1)}, f32[4,2048]{1,0:T(4,128)S(1)}, u32[]{:S(2)}, u32[]{:S(2)}) %collective-permute-start.21) | collective-permute-done | bytes 32800 | tf_op jit(solution)/shard_map/ppermute | solution.py:509
  102.6 3.8 %collective-permute-done.22 = f32[4,2048]{1,0:T(4,128)S(1)} collective-permute-done((f32[4,2048]{1,0:T(4,128)S(1)}, f32[4,2048]{1,0:T(4,128)S(1)}, u32[]{:S(2)}, u32[]{:S(2)}) %collective-permute-start.22) | collective-permute-done | bytes 32800 | tf_op jit(solution)/shard_map/ppermute | solution.py:509
  106.4 1.3 %collective-permute-start.18 = (bf16[16,2048]{1,0:T(8,128)(2,1)S(1)}, bf16[16,2048]{1,0:T(8,128)(2,1)S(1)}, u32[]{:S(2)}, u32[]{:S(2)}) collective-permute-start(bf16[16,2048]{1,0:T(8,128)(2,1)S(1)} %add_convert_fusion.refs_7_), channel_id=1, source_target_pairs={{1,3},{5,7},{9,11},{13,15},{17,19},{21,23},{25,27},{29,31}} | collective-permute-start | bytes 196616 | tf_op jit(solution)/shard_map/ppermute | solution.py:666
  107.7 0.9 collective-permute-done.19.refs_6_
  108.6 1.3 %collective-permute-start.17 = (bf16[16,2048]{1,0:T(8,128)(2,1)S(1)}, bf16[16,2048]{1,0:T(8,128)(2,1)S(1)}, u32[]{:S(2)}, u32[]{:S(2)}) collective-permute-start(bf16[16,2048]{1,0:T(8,128)(2,1)S(1)} %add_convert_fusion.refs_7_), channel_id=1, source_target_pairs={{0,3},{4,7},{8,11},{12,15},{16,19},{20,23},{24,27},{28,31}} | collective-permute-start | bytes 196616 | tf_op jit(solution)/shard_map/ppermute | solution.py:666
  109.9 0.6 add.15
  110.5 14.4 %collective-permute-done.18.refs_5_ = bf16[16,2048]{1,0:T(8,128)(2,1)S(1)} collective-permute-done((bf16[16,2048]{1,0:T(8,128)(2,1)S(1)}, bf16[16,2048]{1,0:T(8,128)(2,1)S(1)}, u32[]{:S(2)}, u32[]{:S(2)}) %collective-permute-start.18) | collective-permute-done | bytes 65568 | tf_op jit(solution)/shard_map/ppermute | solution.py:666
  125.0 1.6 %assemble.1 = bf16[64,8192]{1,0:T(8,128)(2,1)} custom-call(s32[2]{0:T(128)S(1)} %pad_add_fusion.place_ref, bf16[64,2048]{1,0:T(8,128)(2,1)S(1)} %get-tuple-element.87.refs_0_, bf16[64,2048]{1,0:T(8,128)(2,1)S(1)} %collective-permute-done.13.refs_1_, bf16[64,2048]{1,0:T(8,128)(2,1)S(1)} %collective-permute-done.14.refs_2_, ...), custom_call_target="tpu_custom_call" | custom-call | bytes 1048576 | tf_op jit(solution)/shard_map/assemble/pallas_call | solution.py:490
  (33 shorter events, 0.8 us)
Async XLA Ops:
  0.7 1.2 copy-start
  2.5 12.4 %collective-permute-start = (bf16[64,2048]{1,0:T(8,128)(2,1)S(1)}, bf16[64,2048]{1,0:T(8,128)(2,1)S(1)}, u32[]{:S(2)}, u32[]{:S(2)}) collective-permute-start(bf16[64,2048]{1,0:T(8,128)(2,1)S(1)} %get-tuple-element.54), channel_id=1, source_target_pairs={{0,1},{1,0},{2,3},{3,2},{4,5},{5,4},{6,7},{7,6},{8,9},{9,8},{10,11... | collective-permute-start | bytes 786440 | tf_op jit(solution)/shard_map/ppermute | solution.py:509
  3.1 21.4 %collective-permute-start.1 = (bf16[64,2048]{1,0:T(8,128)(2,1)S(1)}, bf16[64,2048]{1,0:T(8,128)(2,1)S(1)}, u32[]{:S(2)}, u32[]{:S(2)}) collective-permute-start(bf16[64,2048]{1,0:T(8,128)(2,1)S(1)} %get-tuple-element.55), channel_id=1, source_target_pairs={{0,2},{1,3},{2,0},{3,1},{4,6},{5,7},{6,4},{7,5},{8,10},{9,11},{10,... | collective-permute-start | bytes 786440 | tf_op jit(solution)/shard_map/ppermute | solution.py:509
  3.4 21.0 %collective-permute-start.2 = (bf16[64,2048]{1,0:T(8,128)(2,1)S(1)}, bf16[64,2048]{1,0:T(8,128)(2,1)S(1)}, u32[]{:S(2)}, u32[]{:S(2)}) collective-permute-start(bf16[64,2048]{1,0:T(8,128)(2,1)S(1)} %get-tuple-element.56), channel_id=1, source_target_pairs={{0,3},{1,2},{2,1},{3,0},{4,7},{5,6},{6,5},{7,4},{8,11},{9,10},{10,... | collective-permute-start | bytes 786440 | tf_op jit(solution)/shard_map/ppermute | solution.py:509
  25.3 6.5 %collective-permute-start.3 = (bf16[16,2048]{1,0:T(8,128)(2,1)S(1)}, bf16[16,2048]{1,0:T(8,128)(2,1)S(1)}, u32[]{:S(2)}, u32[]{:S(2)}) collective-permute-start(bf16[16,2048]{1,0:T(8,128)(2,1)S(1)} %fusion.1), channel_id=1, source_target_pairs={{0,4},{4,8},{8,12},{12,16},{16,20},{20,24},{24,28},{1,5},{5,9},{9,... | collective-permute-start | bytes 196616 | tf_op jit(solution)/shard_map/ppermute | solution.py:505
  27.2 0.7 copy-start.4
  27.9 0.7 copy-start.5
  31.8 1.2 copy-start.1
  33.0 1.0 copy-start.6
  34.0 0.8 copy-start.8
  34.8 29.1 %copy-start.2 = (f32[8,128,128]{2,1,0:T(8,128)S(1)}, f32[8,128,128]{2,1,0:T(8,128)}, u32[]{:S(2)}) copy-start(f32[8,128,128]{2,1,0:T(8,128)} %refs_4_.4) | copy-start | bytes 1572868
  34.8 29.1 %copy-start.3 = (f32[8,128,128]{2,1,0:T(8,128)S(1)}, f32[8,128,128]{2,1,0:T(8,128)}, u32[]{:S(2)}) copy-start(f32[8,128,128]{2,1,0:T(8,128)} %refs_5_.1) | copy-start | bytes 1572868
  48.9 1.8 %collective-permute-start.4 = (f32[2,3,128,128]{3,2,1,0:T(8,128)S(1)}, f32[2,3,128,128]{3,2,1,0:T(8,128)S(1)}, u32[]{:S(2)}, u32[]{:S(2)}) collective-permute-start(f32[2,3,128,128]{3,2,1,0:T(8,128)S(1)} %get-tuple-element.59), channel_id=1, source_target_pairs={{0,4},{4,0},{8,12},{12,8},{16,20},{20,16},{24,28},{28,24},{1,5},{5... | collective-permute-start | bytes 1179656 | tf_op jit(solution)/shard_map/ppermute | solution.py:509
  49.0 2.3 %collective-permute-start.5 = (f32[2,3,128,128]{3,2,1,0:T(8,128)S(1)}, f32[2,3,128,128]{3,2,1,0:T(8,128)S(1)}, u32[]{:S(2)}, u32[]{:S(2)}) collective-permute-start(f32[2,3,128,128]{3,2,1,0:T(8,128)S(1)} %get-tuple-element.60), channel_id=1, source_target_pairs={{0,4},{4,0},{8,12},{12,8},{16,20},{20,16},{24,28},{28,24},{1,5},{5... | collective-permute-start | bytes 1179656 | tf_op jit(solution)/shard_map/ppermute | solution.py:509
  52.3 24.4 %copy-start.7 = (bf16[256,1024]{1,0:T(8,128)(2,1)S(1)}, bf16[256,1024]{1,0:T(8,128)(2,1)}, u32[]{:S(2)}) copy-start(bf16[256,1024]{1,0:T(8,128)(2,1)} %refs_4_.5) | copy-start | bytes 1572868
  52.3 24.4 %copy-start.9 = (f32[4,2048]{1,0:T(4,128)S(1)}, f32[4,2048]{1,0:T(4,128)}, u32[]{:S(2)}) copy-start(f32[4,2048]{1,0:T(4,128)} %refs_0_.1) | copy-start | bytes 98308
  52.3 7.8 %collective-permute-start.6 = (f32[3,128,128]{2,1,0:T(8,128)S(1)}, f32[3,128,128]{2,1,0:T(8,128)S(1)}, u32[]{:S(2)}, u32[]{:S(2)}) collective-permute-start(f32[3,128,128]{2,1,0:T(8,128)S(1)} %get-tuple-element.62), channel_id=1, source_target_pairs={{0,8},{4,12},{8,0},{12,4},{16,24},{20,28},{24,16},{28,20},{1,9},{5... | collective-permute-start | bytes 589832 | tf_op jit(solution)/shard_map/ppermute | solution.py:509
  53.0 10.9 %collective-permute-start.7 = (f32[3,128,128]{2,1,0:T(8,128)S(1)}, f32[3,128,128]{2,1,0:T(8,128)S(1)}, u32[]{:S(2)}, u32[]{:S(2)}) collective-permute-start(f32[3,128,128]{2,1,0:T(8,128)S(1)} %get-tuple-element.63), channel_id=1, source_target_pairs={{0,16},{4,20},{8,24},{12,28},{16,0},{20,4},{24,8},{28,12},{1,17},{... | collective-permute-start | bytes 589832 | tf_op jit(solution)/shard_map/ppermute | solution.py:509
  53.5 10.4 %collective-permute-start.8 = (f32[3,128,128]{2,1,0:T(8,128)S(1)}, f32[3,128,128]{2,1,0:T(8,128)S(1)}, u32[]{:S(2)}, u32[]{:S(2)}) collective-permute-start(f32[3,128,128]{2,1,0:T(8,128)S(1)} %get-tuple-element.64), channel_id=1, source_target_pairs={{0,24},{4,28},{8,16},{12,20},{16,8},{20,12},{24,0},{28,4},{1,25},{... | collective-permute-start | bytes 589832 | tf_op jit(solution)/shard_map/ppermute | solution.py:509
  65.1 6.3 %collective-permute-start.9 = (f32[2,128,128]{2,1,0:T(8,128)S(1)}, f32[2,128,128]{2,1,0:T(8,128)S(1)}, u32[]{:S(2)}, u32[]{:S(2)}) collective-permute-start(f32[2,128,128]{2,1,0:T(8,128)S(1)} %get-tuple-element.66), channel_id=1, source_target_pairs={{0,8},{4,12},{8,0},{12,4},{16,24},{20,28},{24,16},{28,20},{1,9},{5... | collective-permute-start | bytes 393224 | tf_op jit(solution)/shard_map/ppermute | solution.py:509
  66.6 7.2 %collective-permute-start.10 = (f32[2,128,128]{2,1,0:T(8,128)S(1)}, f32[2,128,128]{2,1,0:T(8,128)S(1)}, u32[]{:S(2)}, u32[]{:S(2)}) collective-permute-start(f32[2,128,128]{2,1,0:T(8,128)S(1)} %get-tuple-element.67), channel_id=1, source_target_pairs={{0,16},{4,20},{8,24},{12,28},{16,0},{20,4},{24,8},{28,12},{1,17},{... | collective-permute-start | bytes 393224 | tf_op jit(solution)/shard_map/ppermute | solution.py:509
  66.9 6.9 %collective-permute-start.11 = (f32[2,128,128]{2,1,0:T(8,128)S(1)}, f32[2,128,128]{2,1,0:T(8,128)S(1)}, u32[]{:S(2)}, u32[]{:S(2)}) collective-permute-start(f32[2,128,128]{2,1,0:T(8,128)S(1)} %get-tuple-element.68), channel_id=1, source_target_pairs={{0,24},{4,28},{8,16},{12,20},{16,8},{20,12},{24,0},{28,4},{1,25},{... | collective-permute-start | bytes 393224 | tf_op jit(solution)/shard_map/ppermute | solution.py:509
  74.7 2.0 %collective-permute-start.12 = (f32[4,2,128,128]{3,2,1,0:T(8,128)S(1)}, f32[4,2,128,128]{3,2,1,0:T(8,128)S(1)}, u32[]{:S(2)}, u32[]{:S(2)}) collective-permute-start(f32[4,2,128,128]{3,2,1,0:T(8,128)S(1)} %get-tuple-element.69), channel_id=1, source_target_pairs={{0,4},{4,0},{8,12},{12,8},{16,20},{20,16},{24,28},{28,24},{1,5},{5... | collective-permute-start | bytes 1572872 | tf_op jit(solution)/shard_map/ppermute | solution.py:509
  88.2 11.1 %collective-permute-start.16 = (f32[16,2048]{1,0:T(8,128)S(1)}, f32[16,2048]{1,0:T(8,128)S(1)}, u32[]{:S(2)}, u32[]{:S(2)}) collective-permute-start(f32[16,2048]{1,0:T(8,128)S(1)} %get-tuple-element.94), channel_id=1, source_target_pairs={{4,0},{8,4},{12,8},{16,12},{20,16},{24,20},{28,24},{5,1},{9,5},{13... | collective-permute-start | bytes 393224 | tf_op jit(solution)/shard_map/ppermute | solution.py:505
  91.0 7.4 %collective-permute-start.20 = (f32[4,2048]{1,0:T(4,128)S(1)}, f32[4,2048]{1,0:T(4,128)S(1)}, u32[]{:S(2)}, u32[]{:S(2)}) collective-permute-start(f32[4,2048]{1,0:T(4,128)S(1)} %get-tuple-element.95), channel_id=1, source_target_pairs={{0,4},{4,0},{8,12},{12,8},{16,20},{20,16},{24,28},{28,24},{1,5},{5... | collective-permute-start | bytes 98312 | tf_op jit(solution)/shard_map/ppermute | solution.py:509
  91.1 33.8 %collective-permute-start.13 = (bf16[64,2048]{1,0:T(8,128)(2,1)S(1)}, bf16[64,2048]{1,0:T(8,128)(2,1)S(1)}, u32[]{:S(2)}, u32[]{:S(2)}) collective-permute-start(bf16[64,2048]{1,0:T(8,128)(2,1)S(1)} %get-tuple-element.88), channel_id=1, source_target_pairs={{0,1},{1,0},{2,3},{3,2},{4,5},{5,4},{6,7},{7,6},{8,9},{9,8},{10,11... | collective-permute-start | bytes 786440 | tf_op jit(solution)/shard_map/ppermute | solution.py:509
  95.9 29.0 %collective-permute-start.14 = (bf16[64,2048]{1,0:T(8,128)(2,1)S(1)}, bf16[64,2048]{1,0:T(8,128)(2,1)S(1)}, u32[]{:S(2)}, u32[]{:S(2)}) collective-permute-start(bf16[64,2048]{1,0:T(8,128)(2,1)S(1)} %get-tuple-element.89), channel_id=1, source_target_pairs={{0,2},{1,3},{2,0},{3,1},{4,6},{5,7},{6,4},{7,5},{8,10},{9,11},{10,... | collective-permute-start | bytes 786440 | tf_op jit(solution)/shard_map/ppermute | solution.py:509
  96.0 29.0 %collective-permute-start.15 = (bf16[64,2048]{1,0:T(8,128)(2,1)S(1)}, bf16[64,2048]{1,0:T(8,128)(2,1)S(1)}, u32[]{:S(2)}, u32[]{:S(2)}) collective-permute-start(bf16[64,2048]{1,0:T(8,128)(2,1)S(1)} %get-tuple-element.90), channel_id=1, source_target_pairs={{0,3},{1,2},{2,1},{3,0},{4,7},{5,6},{6,5},{7,4},{8,11},{9,10},{10,... | collective-permute-start | bytes 786440 | tf_op jit(solution)/shard_map/ppermute | solution.py:509
  98.4 4.0 %collective-permute-start.21 = (f32[4,2048]{1,0:T(4,128)S(1)}, f32[4,2048]{1,0:T(4,128)S(1)}, u32[]{:S(2)}, u32[]{:S(2)}) collective-permute-start(f32[4,2048]{1,0:T(4,128)S(1)} %add.13), channel_id=1, source_target_pairs={{0,8},{4,12},{8,0},{12,4},{16,24},{20,28},{24,16},{28,20},{1,9},{5... | collective-permute-start | bytes 98312 | tf_op jit(solution)/shard_map/ppermute | solution.py:509
  99.3 9.3 %collective-permute-start.19 = (bf16[16,2048]{1,0:T(8,128)(2,1)S(1)}, bf16[16,2048]{1,0:T(8,128)(2,1)S(1)}, u32[]{:S(2)}, u32[]{:S(2)}) collective-permute-start(bf16[16,2048]{1,0:T(8,128)(2,1)S(1)} %add_convert_fusion.refs_7_), channel_id=1, source_target_pairs={{2,3},{6,7},{10,11},{14,15},{18,19},{22,23},{26,27},{30,31}} | collective-permute-start | bytes 196616 | tf_op jit(solution)/shard_map/ppermute | solution.py:666
  102.4 4.0 %collective-permute-start.22 = (f32[4,2048]{1,0:T(4,128)S(1)}, f32[4,2048]{1,0:T(4,128)S(1)}, u32[]{:S(2)}, u32[]{:S(2)}) collective-permute-start(f32[4,2048]{1,0:T(4,128)S(1)} %add.14), channel_id=1, source_target_pairs={{0,16},{4,20},{8,24},{12,28},{16,0},{20,4},{24,8},{28,12},{1,17},{... | collective-permute-start | bytes 98312 | tf_op jit(solution)/shard_map/ppermute | solution.py:509
  106.4 18.6 %collective-permute-start.18 = (bf16[16,2048]{1,0:T(8,128)(2,1)S(1)}, bf16[16,2048]{1,0:T(8,128)(2,1)S(1)}, u32[]{:S(2)}, u32[]{:S(2)}) collective-permute-start(bf16[16,2048]{1,0:T(8,128)(2,1)S(1)} %add_convert_fusion.refs_7_), channel_id=1, source_target_pairs={{1,3},{5,7},{9,11},{13,15},{17,19},{21,23},{25,27},{29,31}} | collective-permute-start | bytes 196616 | tf_op jit(solution)/shard_map/ppermute | solution.py:666
  108.6 16.3 %collective-permute-start.17 = (bf16[16,2048]{1,0:T(8,128)(2,1)S(1)}, bf16[16,2048]{1,0:T(8,128)(2,1)S(1)}, u32[]{:S(2)}, u32[]{:S(2)}) collective-permute-start(bf16[16,2048]{1,0:T(8,128)(2,1)S(1)} %add_convert_fusion.refs_7_), channel_id=1, source_target_pairs={{0,3},{4,7},{8,11},{12,15},{16,19},{20,23},{24,27},{28,31}} | collective-permute-start | bytes 196616 | tf_op jit(solution)/shard_map/ppermute | solution.py:666

commit v3 on v2

--- a/solution.py
+++ b/solution.py
@@ -127,7 +127,13 @@
     return parts[:count] + parts[count : 2 * count] + parts[2 * count :]
 
 
-def gates_kernel(logit_ref, decay_ref, causal_ref, gates_ref, beta_ref):
+def gates_kernel(
+    place_ref, logit_ref, decay_ref, mixed_ref, w_ref, do_ref,
+    causal_ref, gates_ref, beta_ref, own_ref, w_out, do_out,
+):
+    own_ref[...] = mixed_ref[:, lanes(place_ref[0] * own_ref.shape[1], own_ref.shape[1])]
+    w_out[...] = w_ref[...]
+    do_out[...] = do_ref[...]
     heads, tokens = decay_ref.shape
     row, col = iotas(tokens, tokens)
     cum = prefix_sums(decay_ref[...])
@@ -160,14 +166,14 @@
     return pl.ds(start if isinstance(start, int) else pl.multiple_of(start, size), size)
 
 
-def local_kernel(slots, place_ref, mixed_ref, *refs):
+def local_kernel(slots, place_ref, *refs):
     each = len(slots)
     outs, exts = (refs[-6 * each : -each], refs[-each:])
     groups = [group_at(place_ref, slot) for slot in slots]
     lowers = []
     for at, group in enumerate(groups):
         lowers += group_system(
-            group, place_ref, mixed_ref, refs[: -6 * each], *outs[at : 3 * each : each], exts[at]
+            group, place_ref, refs[: -6 * each], *outs[at : 3 * each : each], exts[at]
         )
     inverses = unit_lower_inverses(lowers)
     for at, group in enumerate(groups):
@@ -176,21 +182,17 @@
         )
 
 
-def group_system(group, place_ref, mixed_ref, refs, x_out, act_ref, slope_ref, ext):
+def group_system(group, place_ref, refs, x_out, act_ref, slope_ref, ext):
     *piece_refs, halo_ref, w_ref, causal_ref, gates_in, do_ref = refs
     mine = place_ref[0]
     here = lanes(group * GROUP, GROUP)
-    count = mixed_ref.shape[0]
-    pieces = len(piece_refs) + 1
+    count = piece_refs[0].shape[0]
+    pieces = len(piece_refs)
     tokens = pieces * count
-    feats = mixed_ref.shape[1] // pieces
     ext[:EDGE] = halo_ref[:, here].astype(f32)
     x_out[:EDGE] = halo_ref[:, here]
     for s in range(pieces):
-        if s == 0:
-            piece = mixed_ref[:, pl.ds(pl.multiple_of(mine * feats + group * GROUP, GROUP), GROUP)]
-        else:
-            piece = piece_refs[s - 1][:, here]
+        piece = piece_refs[s][:, here]
         begin = pl.multiple_of(EDGE + (mine ^ s) * count, EDGE)
         ext[pl.ds(begin, count)] = piece.astype(f32)
         x_out[pl.ds(begin, count)] = piece
@@ -333,19 +335,20 @@
     each = len(slots)
     w_ref, beta_ref, causal_ref, gates_in, do_ref, *refs = refs
     ends_refs, refs = (refs[:sides], refs[sides:])
-    kept, (*out_refs, extra_ref, gates_ref, dext, ext) = (refs[: 4 * each], refs[4 * each :])
+    kept, (*out_refs, dext, ext) = (refs[: 4 * each], refs[4 * each :])
+    out_refs, last_refs = (out_refs[:-5], out_refs[-5:])
     for at, slot in enumerate(slots):
         side, first = divmod(at * RATIO, each * RATIO // sides)
         group_grads(
             group_at(place_ref, slot), at, place_ref[0], *kept[4 * at : 4 * at + 4], w_ref, beta_ref,
             causal_ref, gates_in, do_ref, ends_refs[side].at[pl.ds(first, RATIO)], out_refs,
-            extra_ref, gates_ref, dext, ext,
+            *last_refs, dext, ext,
         )
 
 
 def group_grads(
     group, at, mine, x_ref, act_ref, slope_ref, saved_ref, w_ref, beta_ref, causal_ref, gates_in,
-    do_ref, ends_ref, out_refs, extra_ref, gates_ref, dext, ext,
+    do_ref, ends_ref, out_refs, edge_ref, spill_ref, dw_ref, decay_ref, logit_ref, dext, ext,
 ):
     tokens = act_ref.shape[0]
     here = lanes(group * GROUP, GROUP)
@@ -403,11 +406,11 @@
         at_end = jnp.sum(left, axis=0, keepdims=True) + gamma[tokens - 1 :] * jnp.sum(
             state * adjoint, axis=0, keepdims=True
         )
-        gates_ref[at, h : h + 1] = (
+        decay_ref[pl.ds(head, 1)] = (
             summed[0:1] + summed[1:2] + summed[2:3] + jnp.sum(at_end, axis=1, keepdims=True)
         )
         closed = 1.0 - beta_ref[pl.ds(head, 1)]
-        gates_ref[at, RATIO + h : RATIO + h + 1] = closed * row_sums(dv * v - terms - key_in)
+        logit_ref[pl.ds(head, 1)] = closed * row_sums(dv * v - terms - key_in)
     dss, dgs = (split(dscores), split(dgram + dgram.T))
     dq += mm(dss, ks)
     dk += mm(split(dscores.T), qs) + mm(dgs, ks)
@@ -419,7 +422,7 @@
     ext[...] = x_ref[...].astype(f32)
     start = EDGE - (KW - 1)
     for tap in range(KW):
-        extra_ref[2 * EDGE + tap : 2 * EDGE + tap + 1, there] = jnp.sum(
+        dw_ref[tap : tap + 1, here] = jnp.sum(
             dconv * ext[start + tap : start + tap + tokens], axis=0, keepdims=True
         )
     zero = jnp.zeros((EDGE, GROUP), f32)
@@ -438,22 +441,8 @@
     for s, out_ref in enumerate(out_refs):
         begin = pl.multiple_of((mine ^ s) * count, EDGE)
         out_ref[:, there] = ext[pl.ds(begin, count)].astype(bf16)
-    extra_ref[:EDGE, there] = own[tokens - EDGE :]
-    extra_ref[EDGE : 2 * EDGE, there] = spill
-
-
-def finish_kernel(slots, place_ref, extra_ref, gates_ref, *outs):
-    edge_ref, spill_ref, dw_ref, decay_ref, beta_ref = outs
-    for at, slot in enumerate(slots):
-        group = group_at(place_ref, slot)
-        here = lanes(group * GROUP, GROUP)
-        there = slice(at * GROUP, (at + 1) * GROUP)
-        edge_ref[:, here] = extra_ref[:EDGE, there]
-        spill_ref[:, here] = extra_ref[EDGE : 2 * EDGE, there]
-        dw_ref[:, here] = extra_ref[2 * EDGE :, there]
-        for h in range(RATIO):
-            decay_ref[pl.ds(group * RATIO + h, 1)] = gates_ref[at, h : h + 1]
-            beta_ref[pl.ds(group * RATIO + h, 1)] = gates_ref[at, RATIO + h : RATIO + h + 1]
+    edge_ref[:, here] = own[tokens - EDGE :]
+    spill_ref[:, here] = spill
 
 
 def pack_kernel(place_ref, mixed_ref, *outs):
@@ -483,20 +472,17 @@
 
 
 def call(kernel, name, out_shape, place, args, scratch=(), flops=0):
-    in_specs = [pl.BlockSpec(memory_space=pltpu.VMEM)] * len(args)
-    if place is not None:
-        in_specs = [pl.BlockSpec(memory_space=pltpu.SMEM)] + in_specs
-        args = [place, *args]
+    vmem = pl.BlockSpec(memory_space=pltpu.VMEM)
     return pl.pallas_call(
         kernel,
-        in_specs=in_specs,
-        out_specs=jax.tree.map(lambda _: pl.BlockSpec(memory_space=pltpu.VMEM), out_shape),
+        in_specs=[pl.BlockSpec(memory_space=pltpu.SMEM)] + [vmem] * len(args),
+        out_specs=jax.tree.map(lambda _: vmem, out_shape),
         out_shape=out_shape,
         scratch_shapes=scratch,
         compiler_params=pltpu.CompilerParams(vmem_limit_bytes=VMEM_BYTES),
         cost_estimate=pl.CostEstimate(flops=flops, bytes_accessed=1 << 20, transcendentals=0),
         name=name,
-    )(*args)
+    )(place, *args)
 
 
 def from_behind(value, axis, by):
@@ -509,7 +495,7 @@
     return lax.ppermute(value, axis, [(i, i ^ by) for i in range(lax.axis_size(axis))])
 
 
-def local_pass(place, slots, mixed_in, received, halo, weight, gates, do):
+def local_pass(place, slots, received, halo, weight, gates, do):
     tokens = gates[0].shape[1]
     each = len(slots)
     outs = call(
@@ -520,7 +506,7 @@
         + [shape(RATIO, tokens, 2 * (DV + DK))] * each
         + [shape(RATIO, 3, DK, DV)] * each,
         place,
-        [mixed_in, *received, halo, weight, *gates, do],
+        [*received, halo, weight, *gates, do],
         [pltpu.VMEM((EDGE + tokens, GROUP), f32)] * each,
         flops=each * 6 * 10**9,
     )
@@ -535,7 +521,13 @@
         functools.partial(grad_kernel, slots, len(ends)),
         "grad_pass",
         [shape(tokens // pieces, each * GROUP, dtype=bf16)] * pieces
-        + [shape(2 * EDGE + KW, each * GROUP), shape(each, 2 * RATIO, tokens)],
+        + [
+            shape(EDGE, each * GROUP),
+            shape(EDGE, each * GROUP),
+            shape(KW, each * GROUP),
+            shape(each * RATIO, tokens),
+            shape(each * RATIO, tokens),
+        ],
         place,
         [weight, beta, *gates, do, *ends, *[a for part in kept for a in part]],
         [pltpu.VMEM((tokens + 2 * EDGE, GROUP), f32), pltpu.VMEM((tokens + EDGE, GROUP), f32)],
@@ -619,21 +611,29 @@
         [mixed_in],
     )
     arrived = [across(piece, "head", s + 1) for s, piece in enumerate(packed)]
-    mine = lax.axis_index("head")
-    edge_rows = mixed_in[mixed_in.shape[0] - EDGE :, feats * (pieces - 1) :]
-    for s, piece in enumerate(arrived):
-        edge_rows = jnp.where((mine ^ (s + 1)) == pieces - 1, piece[piece.shape[0] - EDGE :], edge_rows)
-    halo = from_behind(edge_rows, "ctx", 1)
-    *gates, beta = call(
+    causal, gates, beta, own_piece, near_weight, near_do = call(
         gates_kernel,
         "gates_pass",
-        [shape(heads, tokens, tokens), shape(groups, tokens, 8), shape(heads, tokens)],
-        None,
-        [write_strength_logit, decay_log],
-    )
-    kept, maps = local_pass(
-        place, slots, mixed_in, arrived, halo, conv_weight, gates, grad_out
-    )
+        [
+            shape(heads, tokens, tokens),
+            shape(groups, tokens, 8),
+            shape(heads, tokens),
+            shape(mixed_in.shape[0], feats, dtype=bf16),
+            shape(*conv_weight.shape),
+            shape(*grad_out.shape, dtype=bf16),
+        ],
+        place,
+        [write_strength_logit, decay_log, mixed_in, conv_weight, grad_out],
+    )
+    arrived[0], own_piece = lax.optimization_barrier((arrived[0], own_piece))
+    arrived = [own_piece, *arrived]
+    gates = (causal, gates)
+    mine = lax.axis_index("head")
+    edge_rows = own_piece[own_piece.shape[0] - EDGE :]
+    for s in range(1, pieces):
+        edge_rows = jnp.where((mine ^ s) == pieces - 1, arrived[s][-EDGE:], edge_rows)
+    halo = from_behind(edge_rows, "ctx", 1)
+    kept, maps = local_pass(place, slots, arrived, halo, near_weight, gates, near_do)
     if paired:
         others = [across(part, "ctx", 1) for part in maps[: groups // 2]]
         own_ends, other_ends = cross_chips(
@@ -644,23 +644,10 @@
         gathered = lax.all_gather(jnp.concatenate(maps), "ctx")
         gathered = scan_pass(gathered, initial_state, final_state_grad)
         ends = [lax.dynamic_index_in_dim(gathered, lax.axis_index("ctx"), 0, keepdims=False)]
-    out_pieces, extra, gate_grad = grad_pass(
+    out_pieces, edge, spill, dweight, grad_decay, grad_beta = grad_pass(
         place, slots, kept, ends, conv_weight, beta, gates, grad_out, pieces
     )
     received = [out_pieces[0]] + [across(out_pieces[s], "head", s) for s in range(1, pieces)]
-    edge, spill, dweight, grad_decay, grad_beta = call(
-        functools.partial(finish_kernel, slots),
-        "finish",
-        [
-            shape(EDGE, feats),
-            shape(EDGE, feats),
-            shape(KW, feats),
-            shape(heads, tokens),
-            shape(heads, tokens),
-        ],
-        place,
-        [extra, gate_grad],
-    )
     last = (edge + from_behind(spill, "ctx", -1)).astype(bf16)
     last_rows = [
         lax.ppermute(

time: 127 us -> 123 us (0.969)
  waiting for transfers between devices: 57.4 us -> 53.8 us
    ppermute x18, waiting for transfers between devices: 39.9 us -> 33.9 us  [across(): lax.ppermute(value, axis, [(i, i ^ by) for i in range(lax.axis_size(axis))])]
    ppermute x2, waiting for transfers between devices: 2.2 us -> 4.56 us  [from_behind(): return lax.ppermute(value, axis, pairs)]
    pallas_call x9 -> x8, Pallas kernels: 31.9 us -> 32 us  [call(): pl.pallas_call(kernel, in_specs=[pl.BlockSpec(memory_space=pltpu.SMEM)] +...]
where the time goes in v3:
time: 123 us; the launch traced here: 122 us
  waiting for transfers between devices  53.8 us (44%)
  Pallas kernels  32 us (26%)
  starting transfers between devices  29.2 us (24%)
  local copies, waits for them, and re-layouts  5.66 us (5%)
    ppermute x18, waiting for transfers between devices, across(): lax.ppermute(value, axis, [(i, i ^ by) for i in range(lax.axis_size(axis))])  33.9 us
    pallas_call x8, Pallas kernels, call(): pl.pallas_call(kernel, in_specs=[pl.BlockSpec(memory_space=pltpu.SMEM)] +...  32 us
    ppermute x18, starting transfers between devices, across(): lax.ppermute(value, axis, [(i, i ^ by) for i in range(lax.axis_size(axis))])  20.5 us
    ppermute x3, waiting for transfers between devices, on_device(): lax.ppermute(last, ('ctx', 'head'), [(c * pieces + h, (c + 1) * pieces -...  15.4 us
    unnamed x20, local copies, waits for them, and re-layouts  5.66 us
    ppermute x2, starting transfers between devices, from_behind(): return lax.ppermute(value, axis, pairs)  4.79 us
    ppermute x2, waiting for transfers between devices, from_behind(): return lax.ppermute(value, axis, pairs)  4.56 us
    ppermute x3, starting transfers between devices, on_device(): lax.ppermute(last, ('ctx', 'head'), [(c * pieces + h, (c + 1) * pieces -...  3.85 us
  transfers between devices with their start and end apart: 23, of which 14 were waited for; matrix products, arithmetic and copies ran while one was open for 1% of the time, Pallas kernels for 1%

profile of v3, /device:TPU:28, one launch (start us, length us, event | category | flops | bytes accessed | tf_op | source)
XLA Modules:
  0.0 122.2 jit_solution(2462194831552951738)
XLA Ops:
  0.7 1.2 %copy-done = bf16[64,8192]{1,0:T(8,128)(2,1)S(1)} copy-done((bf16[64,8192]{1,0:T(8,128)(2,1)S(1)}, bf16[64,8192]{1,0:T(8,128)(2,1)}, u32[]{:S(2)}) %copy-start) | copy-done | bytes 1048600
  1.9 0.6 pack.1
  2.5 0.5 collective-permute-start
  3.1 0.3 collective-permute-start.1
  3.4 3.6 %collective-permute-start.2 = (bf16[64,2048]{1,0:T(8,128)(2,1)S(1)}, bf16[64,2048]{1,0:T(8,128)(2,1)S(1)}, u32[]{:S(2)}, u32[]{:S(2)}) collective-permute-start(bf16[64,2048]{1,0:T(8,128)(2,1)S(1)} %get-tuple-element.62), channel_id=1, source_target_pairs={{0,3},{1,2},{2,1},{3,0},{4,7},{5,6},{6,5},{7,4},{8,11},{9,10},{10,... | collective-permute-start | bytes 786440 | tf_op jit(solution)/shard_map/ppermute | solution.py:495
  7.0 1.2 %copy-done.1 = bf16[64,8192]{1,0:T(8,128)(2,1)S(1)} copy-done((bf16[64,8192]{1,0:T(8,128)(2,1)S(1)}, bf16[64,8192]{1,0:T(8,128)(2,1)}, u32[]{:S(2)}) %copy-start.1) | copy-done | bytes 1048600
  8.2 1.0 copy-done.2
  9.3 0.8 copy-done.6
  10.0 0.7 copy-done.8
  10.7 0.7 copy-done.9
  11.4 1.6 %gates_pass.1 = (f32[8,256,256]{2,1,0:T(8,128)S(1)}, f32[4,256,8]{2,1,0:T(8,128)S(1)}, f32[8,256]{1,0:T(8,128)S(1)}, bf16[64,2048]{1,0:T(8,128)(2,1)S(1)}, f32[4...) custom-call(s32[2]{0:T(128)S(1)} %pad_add_fusion.place_ref, f32[8,256]{1,0:T(8,128)S(1)} %copy-done.8, ...), custom_call_target="tpu_custom_call" | custom-call | bytes 1048576 | tf_op jit(solution)/shard_map/gates_pass/pallas_call | solution.py:476
  13.0 2.0 %collective-permute-done.refs_1_ = bf16[64,2048]{1,0:T(8,128)(2,1)S(1)} collective-permute-done((bf16[64,2048]{1,0:T(8,128)(2,1)S(1)}, bf16[64,2048]{1,0:T(8,128)(2,1)S(1)}, u32[]{:S(2)}, u32[]{:S(2)}) %collective-permute-start) | collective-permute-done | bytes 262176 | tf_op jit(solution)/shard_map/ppermute | solution.py:495
  14.9 9.5 %collective-permute-done.1.refs_2_ = bf16[64,2048]{1,0:T(8,128)(2,1)S(1)} collective-permute-done((bf16[64,2048]{1,0:T(8,128)(2,1)S(1)}, bf16[64,2048]{1,0:T(8,128)(2,1)S(1)}, u32[]{:S(2)}, u32[]{:S(2)}) %collective-permute-start.1) | collective-permute-done | bytes 262176 | tf_op jit(solution)/shard_map/ppermute | solution.py:495
  24.4 1.9 %collective-permute-start.3 = (bf16[16,2048]{1,0:T(8,128)(2,1)S(1)}, bf16[16,2048]{1,0:T(8,128)(2,1)S(1)}, u32[]{:S(2)}, u32[]{:S(2)}) collective-permute-start(bf16[16,2048]{1,0:T(8,128)(2,1)S(1)} %fusion), channel_id=1, source_target_pairs={{0,4},{4,8},{8,12},{12,16},{16,20},{20,24},{24,28},{1,5},{5,9},{9,... | collective-permute-start | bytes 196616 | tf_op jit(solution)/shard_map/ppermute | solution.py:491
  26.4 4.6 %collective-permute-done.3.refs_4_ = bf16[16,2048]{1,0:T(8,128)(2,1)S(1)} collective-permute-done((bf16[16,2048]{1,0:T(8,128)(2,1)S(1)}, bf16[16,2048]{1,0:T(8,128)(2,1)S(1)}, u32[]{:S(2)}, u32[]{:S(2)}) %collective-permute-start.3) | collective-permute-done | bytes 65568 | tf_op jit(solution)/shard_map/ppermute | solution.py:491
  30.9 14.2 %local_pass.1 = (bf16[272,512]{1,0:T(8,128)(2,1)S(1)}, bf16[272,512]{1,0:T(8,128)(2,1)S(1)}, bf16[272,512]{1,0:T(8,128)(2,1)S(1)}, bf16[272,512]{1,0:T(8,128)(2,...) custom-call(s32[2]{0:T(128)S(1)} %pad_add_fusion.place_ref, ...), custom_call_target="tpu_custom_call" | custom-call | flops 24000000000 | bytes 1048576 | tf_op jit(solution)/shard_map/local_pass/pallas_call | solution.py:476
  45.2 0.5 collective-permute-start.5
  45.7 1.2 collective-permute-done.4.refs_2_.refs_6_
  47.0 0.6 collective-permute-done.5.refs_3_.refs_7_
  47.5 1.0 join_cores.1
  48.6 0.7 collective-permute-start.6
  49.2 0.5 collective-permute-start.7
  49.7 2.4 %collective-permute-start.8 = (f32[3,128,128]{2,1,0:T(8,128)S(1)}, f32[3,128,128]{2,1,0:T(8,128)S(1)}, u32[]{:S(2)}, u32[]{:S(2)}) collective-permute-start(f32[3,128,128]{2,1,0:T(8,128)S(1)} %get-tuple-element.72), channel_id=1, source_target_pairs={{0,24},{4,28},{8,16},{12,20},{16,8},{20,12},{24,0},{28,4},{1,25},{... | collective-permute-start | bytes 589832 | tf_op jit(solution)/shard_map/ppermute | solution.py:495
  52.1 4.3 %collective-permute-done.6.refs_1_ = f32[3,128,128]{2,1,0:T(8,128)S(1)} collective-permute-done((f32[3,128,128]{2,1,0:T(8,128)S(1)}, f32[3,128,128]{2,1,0:T(8,128)S(1)}, u32[]{:S(2)}, u32[]{:S(2)}) %collective-permute-start.6) | collective-permute-done | bytes 196640 | tf_op jit(solution)/shard_map/ppermute | solution.py:495
  56.4 3.7 %collective-permute-done.7.refs_2_ = f32[3,128,128]{2,1,0:T(8,128)S(1)} collective-permute-done((f32[3,128,128]{2,1,0:T(8,128)S(1)}, f32[3,128,128]{2,1,0:T(8,128)S(1)}, u32[]{:S(2)}, u32[]{:S(2)}) %collective-permute-start.7) | collective-permute-done | bytes 196640 | tf_op jit(solution)/shard_map/ppermute | solution.py:495
  60.1 1.2 over_chips.1
  61.3 1.5 %collective-permute-start.9 = (f32[2,128,128]{2,1,0:T(8,128)S(1)}, f32[2,128,128]{2,1,0:T(8,128)S(1)}, u32[]{:S(2)}, u32[]{:S(2)}) collective-permute-start(f32[2,128,128]{2,1,0:T(8,128)S(1)} %get-tuple-element.74), channel_id=1, source_target_pairs={{0,8},{4,12},{8,0},{12,4},{16,24},{20,28},{24,16},{28,20},{1,9},{5... | collective-permute-start | bytes 393224 | tf_op jit(solution)/shard_map/ppermute | solution.py:495
  62.8 0.3 collective-permute-start.10
  63.1 1.8 %collective-permute-start.11 = (f32[2,128,128]{2,1,0:T(8,128)S(1)}, f32[2,128,128]{2,1,0:T(8,128)S(1)}, u32[]{:S(2)}, u32[]{:S(2)}) collective-permute-start(f32[2,128,128]{2,1,0:T(8,128)S(1)} %get-tuple-element.76), channel_id=1, source_target_pairs={{0,24},{4,28},{8,16},{12,20},{16,8},{20,12},{24,0},{28,4},{1,25},{... | collective-permute-start | bytes 393224 | tf_op jit(solution)/shard_map/ppermute | solution.py:495
  64.9 2.4 %collective-permute-done.9.refs_1_ = f32[2,128,128]{2,1,0:T(8,128)S(1)} collective-permute-done((f32[2,128,128]{2,1,0:T(8,128)S(1)}, f32[2,128,128]{2,1,0:T(8,128)S(1)}, u32[]{:S(2)}, u32[]{:S(2)}) %collective-permute-start.9) | collective-permute-done | bytes 131104 | tf_op jit(solution)/shard_map/ppermute | solution.py:495
  67.3 2.7 %collective-permute-done.10.refs_2_ = f32[2,128,128]{2,1,0:T(8,128)S(1)} collective-permute-done((f32[2,128,128]{2,1,0:T(8,128)S(1)}, f32[2,128,128]{2,1,0:T(8,128)S(1)}, u32[]{:S(2)}, u32[]{:S(2)}) %collective-permute-start.10) | collective-permute-done | bytes 131104 | tf_op jit(solution)/shard_map/ppermute | solution.py:495
  70.0 0.9 within_chip.1
  71.0 1.9 %collective-permute-done.12.refs_5_ = f32[4,2,128,128]{3,2,1,0:T(8,128)S(1)} collective-permute-done((f32[4,2,128,128]{3,2,1,0:T(8,128)S(1)}, f32[4,2,128,128]{3,2,1,0:T(8,128)S(1)}, u32[]{:S(2)}, u32[]{:S(2)}) %collective-permute-start.12) | collective-permute-done | bytes 524320 | tf_op jit(solution)/shard_map/ppermute | solution.py:495
  72.9 10.9 %grad_pass.1 = (bf16[64,2048]{1,0:T(8,128)(2,1)S(1)}, bf16[64,2048]{1,0:T(8,128)(2,1)S(1)}, bf16[64,2048]{1,0:T(8,128)(2,1)S(1)}, bf16[64,2048]{1,0:T(8,128)(2,1...) custom-call(s32[2]{0:T(128)S(1)} %pad_add_fusion.place_ref, ...), custom_call_target="tpu_custom_call" | custom-call | flops 16000000000 | bytes 1048576 | tf_op jit(solution)/shard_map/grad_pass/pallas_call | solution.py:476
  83.8 2.9 %collective-permute-start.16 = (f32[16,2048]{1,0:T(8,128)S(1)}, f32[16,2048]{1,0:T(8,128)S(1)}, u32[]{:S(2)}, u32[]{:S(2)}) collective-permute-start(f32[16,2048]{1,0:T(8,128)S(1)} %get-tuple-element.100), channel_id=1, source_target_pairs={{4,0},{8,4},{12,8},{16,12},{20,16},{24,20},{28,24},{5,1},{9,5},{13... | collective-permute-start | bytes 393224 | tf_op jit(solution)/shard_map/ppermute | solution.py:491
  86.7 4.8 %collective-permute-start.13 = (bf16[64,2048]{1,0:T(8,128)(2,1)S(1)}, bf16[64,2048]{1,0:T(8,128)(2,1)S(1)}, u32[]{:S(2)}, u32[]{:S(2)}) collective-permute-start(bf16[64,2048]{1,0:T(8,128)(2,1)S(1)} %get-tuple-element.96), channel_id=1, source_target_pairs={{0,1},{1,0},{2,3},{3,2},{4,5},{5,4},{6,7},{7,6},{8,9},{9,8},{10,11... | collective-permute-start | bytes 786440 | tf_op jit(solution)/shard_map/ppermute | solution.py:495
  91.6 2.4 %collective-permute-start.15 = (bf16[64,2048]{1,0:T(8,128)(2,1)S(1)}, bf16[64,2048]{1,0:T(8,128)(2,1)S(1)}, u32[]{:S(2)}, u32[]{:S(2)}) collective-permute-start(bf16[64,2048]{1,0:T(8,128)(2,1)S(1)} %get-tuple-element.98), channel_id=1, source_target_pairs={{0,3},{1,2},{2,1},{3,0},{4,7},{5,6},{6,5},{7,4},{8,11},{9,10},{10,... | collective-permute-start | bytes 786440 | tf_op jit(solution)/shard_map/ppermute | solution.py:495
  94.0 0.9 collective-permute-start.21
  94.9 1.3 %collective-permute-start.19 = (bf16[16,2048]{1,0:T(8,128)(2,1)S(1)}, bf16[16,2048]{1,0:T(8,128)(2,1)S(1)}, u32[]{:S(2)}, u32[]{:S(2)}) collective-permute-start(bf16[16,2048]{1,0:T(8,128)(2,1)S(1)} %add_convert_fusion.refs_7_), channel_id=1, source_target_pairs={{2,3},{6,7},{10,11},{14,15},{18,19},{22,23},{26,27},{30,31}} | collective-permute-start | bytes 196616 | tf_op jit(solution)/shard_map/ppermute | solution.py:653
  96.2 1.8 %collective-permute-done.21 = f32[4,2048]{1,0:T(4,128)S(1)} collective-permute-done((f32[4,2048]{1,0:T(4,128)S(1)}, f32[4,2048]{1,0:T(4,128)S(1)}, u32[]{:S(2)}, u32[]{:S(2)}) %collective-permute-start.21) | collective-permute-done | bytes 32800 | tf_op jit(solution)/shard_map/ppermute | solution.py:495
  98.0 0.1 collective-permute-start.22
  98.1 3.8 %collective-permute-done.22 = f32[4,2048]{1,0:T(4,128)S(1)} collective-permute-done((f32[4,2048]{1,0:T(4,128)S(1)}, f32[4,2048]{1,0:T(4,128)S(1)}, u32[]{:S(2)}, u32[]{:S(2)}) %collective-permute-start.22) | collective-permute-done | bytes 32800 | tf_op jit(solution)/shard_map/ppermute | solution.py:495
  102.0 1.3 %collective-permute-start.18 = (bf16[16,2048]{1,0:T(8,128)(2,1)S(1)}, bf16[16,2048]{1,0:T(8,128)(2,1)S(1)}, u32[]{:S(2)}, u32[]{:S(2)}) collective-permute-start(bf16[16,2048]{1,0:T(8,128)(2,1)S(1)} %add_convert_fusion.refs_7_), channel_id=1, source_target_pairs={{1,3},{5,7},{9,11},{13,15},{17,19},{21,23},{25,27},{29,31}} | collective-permute-start | bytes 196616 | tf_op jit(solution)/shard_map/ppermute | solution.py:653
  103.3 1.0 collective-permute-done.19.refs_6_
  104.2 1.3 %collective-permute-start.17 = (bf16[16,2048]{1,0:T(8,128)(2,1)S(1)}, bf16[16,2048]{1,0:T(8,128)(2,1)S(1)}, u32[]{:S(2)}, u32[]{:S(2)}) collective-permute-start(bf16[16,2048]{1,0:T(8,128)(2,1)S(1)} %add_convert_fusion.refs_7_), channel_id=1, source_target_pairs={{0,3},{4,7},{8,11},{12,15},{16,19},{20,23},{24,27},{28,31}} | collective-permute-start | bytes 196616 | tf_op jit(solution)/shard_map/ppermute | solution.py:653
  105.5 0.6 add.15
  106.1 14.4 %collective-permute-done.18.refs_5_ = bf16[16,2048]{1,0:T(8,128)(2,1)S(1)} collective-permute-done((bf16[16,2048]{1,0:T(8,128)(2,1)S(1)}, bf16[16,2048]{1,0:T(8,128)(2,1)S(1)}, u32[]{:S(2)}, u32[]{:S(2)}) %collective-permute-start.18) | collective-permute-done | bytes 65568 | tf_op jit(solution)/shard_map/ppermute | solution.py:653
  120.6 1.6 %assemble.1 = bf16[64,8192]{1,0:T(8,128)(2,1)} custom-call(s32[2]{0:T(128)S(1)} %pad_add_fusion.place_ref, bf16[64,2048]{1,0:T(8,128)(2,1)S(1)} %get-tuple-element.95.refs_0_, bf16[64,2048]{1,0:T(8,128)(2,1)S(1)} %collective-permute-done.13.refs_1_, bf16[64,2048]{1,0:T(8,128)(2,1)S(1)} %collective-permute-done.14.refs_2_, ...), custom_call_target="tpu_custom_call" | custom-call | bytes 1048576 | tf_op jit(solution)/shard_map/assemble/pallas_call | solution.py:476
  (32 shorter events, 0.4 us)
Async XLA Ops:
  0.7 1.2 %copy-start = (bf16[64,8192]{1,0:T(8,128)(2,1)S(1)}, bf16[64,8192]{1,0:T(8,128)(2,1)}, u32[]{:S(2)}) copy-start(bf16[64,8192]{1,0:T(8,128)(2,1)} %mixed_ref.3) | copy-start | bytes 3145732
  2.5 12.4 %collective-permute-start = (bf16[64,2048]{1,0:T(8,128)(2,1)S(1)}, bf16[64,2048]{1,0:T(8,128)(2,1)S(1)}, u32[]{:S(2)}, u32[]{:S(2)}) collective-permute-start(bf16[64,2048]{1,0:T(8,128)(2,1)S(1)} %get-tuple-element.57), channel_id=1, source_target_pairs={{0,1},{1,0},{2,3},{3,2},{4,5},{5,4},{6,7},{7,6},{8,9},{9,8},{10,11... | collective-permute-start | bytes 786440 | tf_op jit(solution)/shard_map/ppermute | solution.py:495
  3.1 21.4 %collective-permute-start.1 = (bf16[64,2048]{1,0:T(8,128)(2,1)S(1)}, bf16[64,2048]{1,0:T(8,128)(2,1)S(1)}, u32[]{:S(2)}, u32[]{:S(2)}) collective-permute-start(bf16[64,2048]{1,0:T(8,128)(2,1)S(1)} %get-tuple-element.61), channel_id=1, source_target_pairs={{0,2},{1,3},{2,0},{3,1},{4,6},{5,7},{6,4},{7,5},{8,10},{9,11},{10,... | collective-permute-start | bytes 786440 | tf_op jit(solution)/shard_map/ppermute | solution.py:495
  3.4 21.0 %collective-permute-start.2 = (bf16[64,2048]{1,0:T(8,128)(2,1)S(1)}, bf16[64,2048]{1,0:T(8,128)(2,1)S(1)}, u32[]{:S(2)}, u32[]{:S(2)}) collective-permute-start(bf16[64,2048]{1,0:T(8,128)(2,1)S(1)} %get-tuple-element.62), channel_id=1, source_target_pairs={{0,3},{1,2},{2,1},{3,0},{4,7},{5,6},{6,5},{7,4},{8,11},{9,10},{10,... | collective-permute-start | bytes 786440 | tf_op jit(solution)/shard_map/ppermute | solution.py:495
  7.0 1.2 %copy-start.1 = (bf16[64,8192]{1,0:T(8,128)(2,1)S(1)}, bf16[64,8192]{1,0:T(8,128)(2,1)}, u32[]{:S(2)}) copy-start(bf16[64,8192]{1,0:T(8,128)(2,1)} %mixed_ref.3) | copy-start | bytes 3145732
  8.2 1.0 copy-start.2
  9.3 0.8 copy-start.6
  10.0 0.7 copy-start.8
  10.7 0.7 copy-start.9
  24.4 6.5 %collective-permute-start.3 = (bf16[16,2048]{1,0:T(8,128)(2,1)S(1)}, bf16[16,2048]{1,0:T(8,128)(2,1)S(1)}, u32[]{:S(2)}, u32[]{:S(2)}) collective-permute-start(bf16[16,2048]{1,0:T(8,128)(2,1)S(1)} %fusion), channel_id=1, source_target_pairs={{0,4},{4,8},{8,12},{12,16},{16,20},{20,24},{24,28},{1,5},{5,9},{9,... | collective-permute-start | bytes 196616 | tf_op jit(solution)/shard_map/ppermute | solution.py:491
  30.9 29.2 %copy-start.4 = (f32[8,128,128]{2,1,0:T(8,128)S(1)}, f32[8,128,128]{2,1,0:T(8,128)}, u32[]{:S(2)}) copy-start(f32[8,128,128]{2,1,0:T(8,128)} %refs_4_.2) | copy-start | bytes 1572868
  30.9 29.2 %copy-start.5 = (f32[8,128,128]{2,1,0:T(8,128)S(1)}, f32[8,128,128]{2,1,0:T(8,128)}, u32[]{:S(2)}) copy-start(f32[8,128,128]{2,1,0:T(8,128)} %refs_5_.1) | copy-start | bytes 1572868
  45.2 1.8 %collective-permute-start.4 = (f32[2,3,128,128]{3,2,1,0:T(8,128)S(1)}, f32[2,3,128,128]{3,2,1,0:T(8,128)S(1)}, u32[]{:S(2)}, u32[]{:S(2)}) collective-permute-start(f32[2,3,128,128]{3,2,1,0:T(8,128)S(1)} %get-tuple-element.67), channel_id=1, source_target_pairs={{0,4},{4,0},{8,12},{12,8},{16,20},{20,16},{24,28},{28,24},{1,5},{5... | collective-permute-start | bytes 1179656 | tf_op jit(solution)/shard_map/ppermute | solution.py:495
  45.2 2.3 %collective-permute-start.5 = (f32[2,3,128,128]{3,2,1,0:T(8,128)S(1)}, f32[2,3,128,128]{3,2,1,0:T(8,128)S(1)}, u32[]{:S(2)}, u32[]{:S(2)}) collective-permute-start(f32[2,3,128,128]{3,2,1,0:T(8,128)S(1)} %get-tuple-element.68), channel_id=1, source_target_pairs={{0,4},{4,0},{8,12},{12,8},{16,20},{20,16},{24,28},{28,24},{1,5},{5... | collective-permute-start | bytes 1179656 | tf_op jit(solution)/shard_map/ppermute | solution.py:495
  48.5 24.4 %copy-start.3 = (bf16[256,1024]{1,0:T(8,128)(2,1)S(1)}, bf16[256,1024]{1,0:T(8,128)(2,1)}, u32[]{:S(2)}) copy-start(bf16[256,1024]{1,0:T(8,128)(2,1)} %refs_4_.3) | copy-start | bytes 1572868
  48.5 24.4 %copy-start.7 = (f32[4,2048]{1,0:T(4,128)S(1)}, f32[4,2048]{1,0:T(4,128)}, u32[]{:S(2)}) copy-start(f32[4,2048]{1,0:T(4,128)} %refs_0_.1) | copy-start | bytes 98308
  48.6 7.8 %collective-permute-start.6 = (f32[3,128,128]{2,1,0:T(8,128)S(1)}, f32[3,128,128]{2,1,0:T(8,128)S(1)}, u32[]{:S(2)}, u32[]{:S(2)}) collective-permute-start(f32[3,128,128]{2,1,0:T(8,128)S(1)} %get-tuple-element.70), channel_id=1, source_target_pairs={{0,8},{4,12},{8,0},{12,4},{16,24},{20,28},{24,16},{28,20},{1,9},{5... | collective-permute-start | bytes 589832 | tf_op jit(solution)/shard_map/ppermute | solution.py:495
  49.2 10.9 %collective-permute-start.7 = (f32[3,128,128]{2,1,0:T(8,128)S(1)}, f32[3,128,128]{2,1,0:T(8,128)S(1)}, u32[]{:S(2)}, u32[]{:S(2)}) collective-permute-start(f32[3,128,128]{2,1,0:T(8,128)S(1)} %get-tuple-element.71), channel_id=1, source_target_pairs={{0,16},{4,20},{8,24},{12,28},{16,0},{20,4},{24,8},{28,12},{1,17},{... | collective-permute-start | bytes 589832 | tf_op jit(solution)/shard_map/ppermute | solution.py:495
  49.7 10.4 %collective-permute-start.8 = (f32[3,128,128]{2,1,0:T(8,128)S(1)}, f32[3,128,128]{2,1,0:T(8,128)S(1)}, u32[]{:S(2)}, u32[]{:S(2)}) collective-permute-start(f32[3,128,128]{2,1,0:T(8,128)S(1)} %get-tuple-element.72), channel_id=1, source_target_pairs={{0,24},{4,28},{8,16},{12,20},{16,8},{20,12},{24,0},{28,4},{1,25},{... | collective-permute-start | bytes 589832 | tf_op jit(solution)/shard_map/ppermute | solution.py:495
  61.3 5.9 %collective-permute-start.9 = (f32[2,128,128]{2,1,0:T(8,128)S(1)}, f32[2,128,128]{2,1,0:T(8,128)S(1)}, u32[]{:S(2)}, u32[]{:S(2)}) collective-permute-start(f32[2,128,128]{2,1,0:T(8,128)S(1)} %get-tuple-element.74), channel_id=1, source_target_pairs={{0,8},{4,12},{8,0},{12,4},{16,24},{20,28},{24,16},{28,20},{1,9},{5... | collective-permute-start | bytes 393224 | tf_op jit(solution)/shard_map/ppermute | solution.py:495
  62.8 7.2 %collective-permute-start.10 = (f32[2,128,128]{2,1,0:T(8,128)S(1)}, f32[2,128,128]{2,1,0:T(8,128)S(1)}, u32[]{:S(2)}, u32[]{:S(2)}) collective-permute-start(f32[2,128,128]{2,1,0:T(8,128)S(1)} %get-tuple-element.75), channel_id=1, source_target_pairs={{0,16},{4,20},{8,24},{12,28},{16,0},{20,4},{24,8},{28,12},{1,17},{... | collective-permute-start | bytes 393224 | tf_op jit(solution)/shard_map/ppermute | solution.py:495
  63.1 6.9 %collective-permute-start.11 = (f32[2,128,128]{2,1,0:T(8,128)S(1)}, f32[2,128,128]{2,1,0:T(8,128)S(1)}, u32[]{:S(2)}, u32[]{:S(2)}) collective-permute-start(f32[2,128,128]{2,1,0:T(8,128)S(1)} %get-tuple-element.76), channel_id=1, source_target_pairs={{0,24},{4,28},{8,16},{12,20},{16,8},{20,12},{24,0},{28,4},{1,25},{... | collective-permute-start | bytes 393224 | tf_op jit(solution)/shard_map/ppermute | solution.py:495
  70.9 2.0 %collective-permute-start.12 = (f32[4,2,128,128]{3,2,1,0:T(8,128)S(1)}, f32[4,2,128,128]{3,2,1,0:T(8,128)S(1)}, u32[]{:S(2)}, u32[]{:S(2)}) collective-permute-start(f32[4,2,128,128]{3,2,1,0:T(8,128)S(1)} %get-tuple-element.77), channel_id=1, source_target_pairs={{0,4},{4,0},{8,12},{12,8},{16,20},{20,16},{24,28},{28,24},{1,5},{5... | collective-permute-start | bytes 1572872 | tf_op jit(solution)/shard_map/ppermute | solution.py:495
  83.8 11.1 %collective-permute-start.16 = (f32[16,2048]{1,0:T(8,128)S(1)}, f32[16,2048]{1,0:T(8,128)S(1)}, u32[]{:S(2)}, u32[]{:S(2)}) collective-permute-start(f32[16,2048]{1,0:T(8,128)S(1)} %get-tuple-element.100), channel_id=1, source_target_pairs={{4,0},{8,4},{12,8},{16,12},{20,16},{24,20},{28,24},{5,1},{9,5},{13... | collective-permute-start | bytes 393224 | tf_op jit(solution)/shard_map/ppermute | solution.py:491
  86.6 7.4 %collective-permute-start.20 = (f32[4,2048]{1,0:T(4,128)S(1)}, f32[4,2048]{1,0:T(4,128)S(1)}, u32[]{:S(2)}, u32[]{:S(2)}) collective-permute-start(f32[4,2048]{1,0:T(4,128)S(1)} %get-tuple-element.101), channel_id=1, source_target_pairs={{0,4},{4,0},{8,12},{12,8},{16,20},{20,16},{24,28},{28,24},{1,5},{5... | collective-permute-start | bytes 98312 | tf_op jit(solution)/shard_map/ppermute | solution.py:495
  86.7 33.8 %collective-permute-start.13 = (bf16[64,2048]{1,0:T(8,128)(2,1)S(1)}, bf16[64,2048]{1,0:T(8,128)(2,1)S(1)}, u32[]{:S(2)}, u32[]{:S(2)}) collective-permute-start(bf16[64,2048]{1,0:T(8,128)(2,1)S(1)} %get-tuple-element.96), channel_id=1, source_target_pairs={{0,1},{1,0},{2,3},{3,2},{4,5},{5,4},{6,7},{7,6},{8,9},{9,8},{10,11... | collective-permute-start | bytes 786440 | tf_op jit(solution)/shard_map/ppermute | solution.py:495
  91.6 29.0 %collective-permute-start.14 = (bf16[64,2048]{1,0:T(8,128)(2,1)S(1)}, bf16[64,2048]{1,0:T(8,128)(2,1)S(1)}, u32[]{:S(2)}, u32[]{:S(2)}) collective-permute-start(bf16[64,2048]{1,0:T(8,128)(2,1)S(1)} %get-tuple-element.97), channel_id=1, source_target_pairs={{0,2},{1,3},{2,0},{3,1},{4,6},{5,7},{6,4},{7,5},{8,10},{9,11},{10,... | collective-permute-start | bytes 786440 | tf_op jit(solution)/shard_map/ppermute | solution.py:495
  91.6 29.0 %collective-permute-start.15 = (bf16[64,2048]{1,0:T(8,128)(2,1)S(1)}, bf16[64,2048]{1,0:T(8,128)(2,1)S(1)}, u32[]{:S(2)}, u32[]{:S(2)}) collective-permute-start(bf16[64,2048]{1,0:T(8,128)(2,1)S(1)} %get-tuple-element.98), channel_id=1, source_target_pairs={{0,3},{1,2},{2,1},{3,0},{4,7},{5,6},{6,5},{7,4},{8,11},{9,10},{10,... | collective-permute-start | bytes 786440 | tf_op jit(solution)/shard_map/ppermute | solution.py:495
  94.0 4.0 %collective-permute-start.21 = (f32[4,2048]{1,0:T(4,128)S(1)}, f32[4,2048]{1,0:T(4,128)S(1)}, u32[]{:S(2)}, u32[]{:S(2)}) collective-permute-start(f32[4,2048]{1,0:T(4,128)S(1)} %add.13), channel_id=1, source_target_pairs={{0,8},{4,12},{8,0},{12,4},{16,24},{20,28},{24,16},{28,20},{1,9},{5... | collective-permute-start | bytes 98312 | tf_op jit(solution)/shard_map/ppermute | solution.py:495
  94.9 9.3 %collective-permute-start.19 = (bf16[16,2048]{1,0:T(8,128)(2,1)S(1)}, bf16[16,2048]{1,0:T(8,128)(2,1)S(1)}, u32[]{:S(2)}, u32[]{:S(2)}) collective-permute-start(bf16[16,2048]{1,0:T(8,128)(2,1)S(1)} %add_convert_fusion.refs_7_), channel_id=1, source_target_pairs={{2,3},{6,7},{10,11},{14,15},{18,19},{22,23},{26,27},{30,31}} | collective-permute-start | bytes 196616 | tf_op jit(solution)/shard_map/ppermute | solution.py:653
  98.0 4.0 %collective-permute-start.22 = (f32[4,2048]{1,0:T(4,128)S(1)}, f32[4,2048]{1,0:T(4,128)S(1)}, u32[]{:S(2)}, u32[]{:S(2)}) collective-permute-start(f32[4,2048]{1,0:T(4,128)S(1)} %add.14), channel_id=1, source_target_pairs={{0,16},{4,20},{8,24},{12,28},{16,0},{20,4},{24,8},{28,12},{1,17},{... | collective-permute-start | bytes 98312 | tf_op jit(solution)/shard_map/ppermute | solution.py:495
  102.0 18.6 %collective-permute-start.18 = (bf16[16,2048]{1,0:T(8,128)(2,1)S(1)}, bf16[16,2048]{1,0:T(8,128)(2,1)S(1)}, u32[]{:S(2)}, u32[]{:S(2)}) collective-permute-start(bf16[16,2048]{1,0:T(8,128)(2,1)S(1)} %add_convert_fusion.refs_7_), channel_id=1, source_target_pairs={{1,3},{5,7},{9,11},{13,15},{17,19},{21,23},{25,27},{29,31}} | collective-permute-start | bytes 196616 | tf_op jit(solution)/shard_map/ppermute | solution.py:653
  104.2 16.3 %collective-permute-start.17 = (bf16[16,2048]{1,0:T(8,128)(2,1)S(1)}, bf16[16,2048]{1,0:T(8,128)(2,1)S(1)}, u32[]{:S(2)}, u32[]{:S(2)}) collective-permute-start(bf16[16,2048]{1,0:T(8,128)(2,1)S(1)} %add_convert_fusion.refs_7_), channel_id=1, source_target_pairs={{0,3},{4,7},{8,11},{12,15},{16,19},{20,23},{24,27},{28,31}} | collective-permute-start | bytes 196616 | tf_op jit(solution)/shard_map/ppermute | solution.py:653

commit v4 on v3

--- a/solution.py
+++ b/solution.py
@@ -15,6 +15,7 @@
 GROUP = 2 * DK + RATIO * DV
 TILE = 128
 BASE = 2
+STEP = 2
 EDGE = 16
 VMEM_BYTES = 24 * 1024 * 1024
 
@@ -61,6 +62,18 @@
     return total if exact else total + dot(a[1], high, dims)
 
 
+def together(works):
+    works = list(works)
+    while works:
+        works = [work for work in works if next(work, works) is None]
+        yield
+
+
+def finish(work):
+    for _ in work:
+        pass
+
+
 def iotas(rows, cols):
     return (
         lax.broadcasted_iota(jnp.int32, (rows, cols), 0),
@@ -177,8 +190,11 @@
         )
     inverses = unit_lower_inverses(lowers)
     for at, group in enumerate(groups):
-        group_maps(
-            group, inverses[at * RATIO : (at + 1) * RATIO], refs[: -6 * each], *outs[each + at :: each]
+        finish(
+            group_maps(
+                group, inverses[at * RATIO : (at + 1) * RATIO], refs[: -6 * each],
+                *outs[each + at :: each],
+            )
         )
 
 
@@ -231,7 +247,9 @@
     scores = mm(split(q), split(k), NT)
     qt = split(q.T)
     kt = split(k.T)
-    for h in range(RATIO):
+    yield
+
+    def head_maps(h):
         head = group * RATIO + h
         beta, gamma, tail = wide_gates(gates_in, group, h)
         beta_gamma = beta * gamma
@@ -239,16 +257,22 @@
         do = do_ref[:, lanes(head * DV, DV)]
         solved = mm(split(inverses[h]), split(jnp.concatenate([beta * v, beta_gamma * k], axis=1)))
         du = mm(split((causal_ref[head] * scores).T), (do,))
+        yield
+        saved_ref[h, :, : DV + DK] = solved
         pulled = mm(split(inverses[h].T), split(jnp.concatenate([du, tail * k], axis=1)))
-        saved_ref[h, :, : DV + DK] = solved
+        yield
         saved_ref[h, :, DV + DK :] = pulled
         packed = [tail * solved[:, :DV], tail * solved[:, DV:], beta_gamma * pulled[:, :DV]]
         moved = mm(kt, split(jnp.concatenate(packed, axis=1)))
+        adjoint = mm(qt, split(gamma * do.astype(f32)))
+        yield
         drow, dcol = iotas(DK, DK)
         total = gamma[tokens - 1 :]
         maps_ref[h, 0] = jnp.where(drow == dcol, total, 0.0) - moved[:, DV : DV + DK]
         maps_ref[h, 1] = moved[:, :DV]
-        maps_ref[h, 2] = mm(qt, split(gamma * do.astype(f32))) - moved[:, DV + DK :]
+        maps_ref[h, 2] = adjoint - moved[:, DV + DK :]
+
+    yield from together(head_maps(h) for h in range(RATIO))
 
 
 def ordered(core, own, other):
@@ -337,13 +361,18 @@
     ends_refs, refs = (refs[:sides], refs[sides:])
     kept, (*out_refs, dext, ext) = (refs[: 4 * each], refs[4 * each :])
     out_refs, last_refs = (out_refs[:-5], out_refs[-5:])
+    works = []
     for at, slot in enumerate(slots):
         side, first = divmod(at * RATIO, each * RATIO // sides)
-        group_grads(
-            group_at(place_ref, slot), at, place_ref[0], *kept[4 * at : 4 * at + 4], w_ref, beta_ref,
-            causal_ref, gates_in, do_ref, ends_refs[side].at[pl.ds(first, RATIO)], out_refs,
-            *last_refs, dext, ext,
-        )
+        works.append(
+            group_grads(
+                group_at(place_ref, slot), at, place_ref[0], *kept[4 * at : 4 * at + 4], w_ref,
+                beta_ref, causal_ref, gates_in, do_ref, ends_refs[side].at[pl.ds(first, RATIO)],
+                out_refs, *last_refs, dext.at[at % STEP], ext.at[at % STEP],
+            )
+        )
+    for first in range(0, each, STEP):
+        finish(together(works[first : first + STEP]))
 
 
 def group_grads(
@@ -362,10 +391,10 @@
     row, col = iotas(tokens, tokens)
     below = col < row
     suffix = jnp.where(row >= col, 1.0, 0.0).astype(bf16)
-    dq, dk = (jnp.zeros((tokens, DK), f32), jnp.zeros((tokens, DK), f32))
-    dscores, dgram = (jnp.zeros((tokens, tokens), f32), jnp.zeros((tokens, tokens), f32))
-    dvs = []
-    for h in range(RATIO):
+    yield
+    results = [None] * RATIO
+
+    def head_grads(h):
         head = group * RATIO + h
         beta, gamma, tail = wide_gates(gates_in, group, h)
         v = act_ref[:, 2 * DK + h * DV : 2 * DK + (h + 1) * DV]
@@ -376,21 +405,19 @@
         z = saved_ref[h, :, DV + DK : 2 * DV + DK] + mm(
             split(saved_ref[h, :, 2 * DV + DK :]), ds
         )
+        yield
         dv = beta * z
         us, zs = (split(u), split(dv))
         dq_in = gamma * mm(do, ss, NT)
         dk_in = gamma * mm(zs, ss, NT)
         dk_out = tail * mm(us, ds, NT)
+        yield
         causal = causal_ref[head]
         score_part = mm(do, us, NT) * causal
         gram_part = jnp.where(below, mm(zs, us, NT) * causal, 0.0)
-        dscores += score_part
-        dgram -= gram_part
+        yield
         gram_term = gram_part * gram
         both = score_part * scores - gram_term
-        dvs.append(dv)
-        dq += dq_in
-        dk += dk_out - dk_in
         key_in = dk_in * k
         left = dk_out * k
         parts = both[:, :DK]
@@ -399,6 +426,8 @@
             parts += both[:, begin : begin + DK]
             terms += gram_term[:, begin : begin + DK]
         dcum = row_sums(parts + dq_in * q - key_in - left) - jnp.sum(both, axis=0, keepdims=True)
+        results[h] = (dq_in, dk_out - dk_in, dv, score_part, gram_part)
+        yield
         high, low = split(dcum)
         rest = (dcum - high.astype(f32) - low.astype(f32)).astype(bf16)
         stack = [high, low, rest, high, low, rest, high, low]
@@ -411,9 +440,15 @@
         )
         closed = 1.0 - beta_ref[pl.ds(head, 1)]
         logit_ref[pl.ds(head, 1)] = closed * row_sums(dv * v - terms - key_in)
+
+    yield from together(head_grads(h) for h in range(RATIO))
+    dq, dk, _, dscores, dgram = (sum(parts[1:], parts[0]) for parts in zip(*results))
+    dgram = -dgram
+    dvs = [result[2] for result in results]
     dss, dgs = (split(dscores), split(dgram + dgram.T))
     dq += mm(dss, ks)
     dk += mm(split(dscores.T), qs) + mm(dgs, ks)
+    yield
     dq *= DK**-0.5
     dconv = jnp.concatenate(
         [dq - qn * wide_row_sums(qn * dq), dk - k * wide_row_sums(k * dk)] + dvs, axis=1
@@ -426,6 +461,7 @@
             dconv * ext[start + tap : start + tap + tokens], axis=0, keepdims=True
         )
     zero = jnp.zeros((EDGE, GROUP), f32)
+    yield
     dext[:EDGE] = zero
     dext[EDGE : EDGE + tokens] = dconv
     dext[EDGE + tokens :] = zero
@@ -530,7 +566,10 @@
         ],
         place,
         [weight, beta, *gates, do, *ends, *[a for part in kept for a in part]],
-        [pltpu.VMEM((tokens + 2 * EDGE, GROUP), f32), pltpu.VMEM((tokens + EDGE, GROUP), f32)],
+        [
+            pltpu.VMEM((STEP, tokens + 2 * EDGE, GROUP), f32),
+            pltpu.VMEM((STEP, tokens + EDGE, GROUP), f32),
+        ],
         flops=each * 4 * 10**9,
     )
     return (outs[:pieces], *outs[pieces:])

time: 123 us -> 119 us (0.967)
  Pallas kernels: 32 us -> 28.5 us
    pallas_call x8, Pallas kernels: 32 us -> 28.5 us  [call(): pl.pallas_call(kernel, in_specs=[pl.BlockSpec(memory_space=pltpu.SMEM)] +...]
where the time goes in v4:
time: 119 us
  waiting for transfers between devices  53.8 us (45%)
  starting transfers between devices  29.2 us (25%)
  Pallas kernels  28.5 us (24%)
  local copies, waits for them, and re-layouts  5.66 us (5%)
    ppermute x18, waiting for transfers between devices, across(): lax.ppermute(value, axis, [(i, i ^ by) for i in range(lax.axis_size(axis))])  33.9 us
    pallas_call x8, Pallas kernels, call(): pl.pallas_call(kernel, in_specs=[pl.BlockSpec(memory_space=pltpu.SMEM)] +...  28.5 us
    ppermute x18, starting transfers between devices, across(): lax.ppermute(value, axis, [(i, i ^ by) for i in range(lax.axis_size(axis))])  20.5 us
    ppermute x3, waiting for transfers between devices, on_device(): lax.ppermute(last, ('ctx', 'head'), [(c * pieces + h, (c + 1) * pieces -...  15.4 us
    unnamed x20, local copies, waits for them, and re-layouts  5.66 us
    ppermute x2, starting transfers between devices, from_behind(): return lax.ppermute(value, axis, pairs)  4.81 us
    ppermute x2, waiting for transfers between devices, from_behind(): return lax.ppermute(value, axis, pairs)  4.56 us
    ppermute x3, starting transfers between devices, on_device(): lax.ppermute(last, ('ctx', 'head'), [(c * pieces + h, (c + 1) * pieces -...  3.85 us
  transfers between devices with their start and end apart: 23, of which 14 were waited for; matrix products, arithmetic and copies ran while one was open for 1% of the time, Pallas kernels for 1%

profile of v4, /device:TPU:28, one launch (start us, length us, event | category | flops | bytes accessed | tf_op | source)
XLA Modules:
  0.0 118.7 jit_solution(14763646563319022882)
XLA Ops:
  0.7 1.2 %copy-done = bf16[64,8192]{1,0:T(8,128)(2,1)S(1)} copy-done((bf16[64,8192]{1,0:T(8,128)(2,1)S(1)}, bf16[64,8192]{1,0:T(8,128)(2,1)}, u32[]{:S(2)}) %copy-start) | copy-done | bytes 1048600
  1.9 0.6 pack.1
  2.5 0.5 collective-permute-start
  3.1 0.3 collective-permute-start.1
  3.4 3.6 %collective-permute-start.2 = (bf16[64,2048]{1,0:T(8,128)(2,1)S(1)}, bf16[64,2048]{1,0:T(8,128)(2,1)S(1)}, u32[]{:S(2)}, u32[]{:S(2)}) collective-permute-start(bf16[64,2048]{1,0:T(8,128)(2,1)S(1)} %get-tuple-element.62), channel_id=1, source_target_pairs={{0,3},{1,2},{2,1},{3,0},{4,7},{5,6},{6,5},{7,4},{8,11},{9,10},{10,... | collective-permute-start | bytes 786440 | tf_op jit(solution)/shard_map/ppermute | solution.py:531
  7.0 1.2 %copy-done.1 = bf16[64,8192]{1,0:T(8,128)(2,1)S(1)} copy-done((bf16[64,8192]{1,0:T(8,128)(2,1)S(1)}, bf16[64,8192]{1,0:T(8,128)(2,1)}, u32[]{:S(2)}) %copy-start.1) | copy-done | bytes 1048600
  8.2 1.0 copy-done.2
  9.3 0.8 copy-done.6
  10.0 0.7 copy-done.8
  10.7 0.7 copy-done.9
  11.4 1.6 %gates_pass.1 = (f32[8,256,256]{2,1,0:T(8,128)S(1)}, f32[4,256,8]{2,1,0:T(8,128)S(1)}, f32[8,256]{1,0:T(8,128)S(1)}, bf16[64,2048]{1,0:T(8,128)(2,1)S(1)}, f32[4...) custom-call(s32[2]{0:T(128)S(1)} %pad_add_fusion.place_ref, f32[8,256]{1,0:T(8,128)S(1)} %copy-done.8, ...), custom_call_target="tpu_custom_call" | custom-call | bytes 1048576 | tf_op jit(solution)/shard_map/gates_pass/pallas_call | solution.py:512
  13.0 2.0 %collective-permute-done.refs_1_ = bf16[64,2048]{1,0:T(8,128)(2,1)S(1)} collective-permute-done((bf16[64,2048]{1,0:T(8,128)(2,1)S(1)}, bf16[64,2048]{1,0:T(8,128)(2,1)S(1)}, u32[]{:S(2)}, u32[]{:S(2)}) %collective-permute-start) | collective-permute-done | bytes 262176 | tf_op jit(solution)/shard_map/ppermute | solution.py:531
  14.9 9.5 %collective-permute-done.1.refs_2_ = bf16[64,2048]{1,0:T(8,128)(2,1)S(1)} collective-permute-done((bf16[64,2048]{1,0:T(8,128)(2,1)S(1)}, bf16[64,2048]{1,0:T(8,128)(2,1)S(1)}, u32[]{:S(2)}, u32[]{:S(2)}) %collective-permute-start.1) | collective-permute-done | bytes 262176 | tf_op jit(solution)/shard_map/ppermute | solution.py:531
  24.4 1.9 %collective-permute-start.3 = (bf16[16,2048]{1,0:T(8,128)(2,1)S(1)}, bf16[16,2048]{1,0:T(8,128)(2,1)S(1)}, u32[]{:S(2)}, u32[]{:S(2)}) collective-permute-start(bf16[16,2048]{1,0:T(8,128)(2,1)S(1)} %fusion), channel_id=1, source_target_pairs={{0,4},{4,8},{8,12},{12,16},{16,20},{20,24},{24,28},{1,5},{5,9},{9,... | collective-permute-start | bytes 196616 | tf_op jit(solution)/shard_map/ppermute | solution.py:527
  26.4 4.6 %collective-permute-done.3.refs_4_ = bf16[16,2048]{1,0:T(8,128)(2,1)S(1)} collective-permute-done((bf16[16,2048]{1,0:T(8,128)(2,1)S(1)}, bf16[16,2048]{1,0:T(8,128)(2,1)S(1)}, u32[]{:S(2)}, u32[]{:S(2)}) %collective-permute-start.3) | collective-permute-done | bytes 65568 | tf_op jit(solution)/shard_map/ppermute | solution.py:527
  30.9 12.4 %local_pass.1 = (bf16[272,512]{1,0:T(8,128)(2,1)S(1)}, bf16[272,512]{1,0:T(8,128)(2,1)S(1)}, bf16[272,512]{1,0:T(8,128)(2,1)S(1)}, bf16[272,512]{1,0:T(8,128)(2,...) custom-call(s32[2]{0:T(128)S(1)} %pad_add_fusion.place_ref, ...), custom_call_target="tpu_custom_call" | custom-call | flops 24000000000 | bytes 1048576 | tf_op jit(solution)/shard_map/local_pass/pallas_call | solution.py:512
  43.4 0.5 collective-permute-start.5
  43.9 1.2 %collective-permute-done.4.refs_2_.refs_6_ = f32[2,3,128,128]{3,2,1,0:T(8,128)S(1)} collective-permute-done((f32[2,3,128,128]{3,2,1,0:T(8,128)S(1)}, f32[2,3,128,128]{3,2,1,0:T(8,128)S(1)}, u32[]{:S(2)}, u32[]{:S(2)}) %collective-permute-start.4) | collective-permute-done | bytes 393248 | tf_op jit(solution)/shard_map/ppermute | solution.py:531
  45.1 0.6 collective-permute-done.5.refs_3_.refs_7_
  45.7 1.2 join_cores.1
  46.9 0.7 collective-permute-start.6
  47.5 0.5 collective-permute-start.7
  48.0 2.4 %collective-permute-start.8 = (f32[3,128,128]{2,1,0:T(8,128)S(1)}, f32[3,128,128]{2,1,0:T(8,128)S(1)}, u32[]{:S(2)}, u32[]{:S(2)}) collective-permute-start(f32[3,128,128]{2,1,0:T(8,128)S(1)} %get-tuple-element.72), channel_id=1, source_target_pairs={{0,24},{4,28},{8,16},{12,20},{16,8},{20,12},{24,0},{28,4},{1,25},{... | collective-permute-start | bytes 589832 | tf_op jit(solution)/shard_map/ppermute | solution.py:531
  50.4 4.3 %collective-permute-done.6.refs_1_ = f32[3,128,128]{2,1,0:T(8,128)S(1)} collective-permute-done((f32[3,128,128]{2,1,0:T(8,128)S(1)}, f32[3,128,128]{2,1,0:T(8,128)S(1)}, u32[]{:S(2)}, u32[]{:S(2)}) %collective-permute-start.6) | collective-permute-done | bytes 196640 | tf_op jit(solution)/shard_map/ppermute | solution.py:531
  54.7 3.7 %collective-permute-done.7.refs_2_ = f32[3,128,128]{2,1,0:T(8,128)S(1)} collective-permute-done((f32[3,128,128]{2,1,0:T(8,128)S(1)}, f32[3,128,128]{2,1,0:T(8,128)S(1)}, u32[]{:S(2)}, u32[]{:S(2)}) %collective-permute-start.7) | collective-permute-done | bytes 196640 | tf_op jit(solution)/shard_map/ppermute | solution.py:531
  58.4 1.2 %over_chips.1 = (f32[2,128,128]{2,1,0:T(8,128)S(1)}, f32[2,128,128]{2,1,0:T(8,128)S(1)}, f32[2,128,128]{2,1,0:T(8,128)S(1)}, f32[2,128,128]{2,1,0:T(8,128)S(1)}) custom-call(s32[2]{0:T(128)S(1)} %pad_add_fusion.place_ref, f32[3,128,128]{2,1,0:T(8,128)S(1)} %get-tuple-element.69.refs_0_, f32[3,128,128]{2,1,0:T(8,128)S(1)} %collective-permute-done.6.refs_1_, ...), custom_call_target="tpu_custom_call" | custom-call | bytes 1048576 | tf_op jit(solution)/shard_map/over_chips/pallas_call | solution.py:512
  59.6 1.5 %collective-permute-start.9 = (f32[2,128,128]{2,1,0:T(8,128)S(1)}, f32[2,128,128]{2,1,0:T(8,128)S(1)}, u32[]{:S(2)}, u32[]{:S(2)}) collective-permute-start(f32[2,128,128]{2,1,0:T(8,128)S(1)} %get-tuple-element.74), channel_id=1, source_target_pairs={{0,8},{4,12},{8,0},{12,4},{16,24},{20,28},{24,16},{28,20},{1,9},{5... | collective-permute-start | bytes 393224 | tf_op jit(solution)/shard_map/ppermute | solution.py:531
  61.1 0.3 collective-permute-start.10
  61.4 1.8 %collective-permute-start.11 = (f32[2,128,128]{2,1,0:T(8,128)S(1)}, f32[2,128,128]{2,1,0:T(8,128)S(1)}, u32[]{:S(2)}, u32[]{:S(2)}) collective-permute-start(f32[2,128,128]{2,1,0:T(8,128)S(1)} %get-tuple-element.76), channel_id=1, source_target_pairs={{0,24},{4,28},{8,16},{12,20},{16,8},{20,12},{24,0},{28,4},{1,25},{... | collective-permute-start | bytes 393224 | tf_op jit(solution)/shard_map/ppermute | solution.py:531
  63.2 2.4 %collective-permute-done.9.refs_1_ = f32[2,128,128]{2,1,0:T(8,128)S(1)} collective-permute-done((f32[2,128,128]{2,1,0:T(8,128)S(1)}, f32[2,128,128]{2,1,0:T(8,128)S(1)}, u32[]{:S(2)}, u32[]{:S(2)}) %collective-permute-start.9) | collective-permute-done | bytes 131104 | tf_op jit(solution)/shard_map/ppermute | solution.py:531
  65.6 2.7 %collective-permute-done.10.refs_2_ = f32[2,128,128]{2,1,0:T(8,128)S(1)} collective-permute-done((f32[2,128,128]{2,1,0:T(8,128)S(1)}, f32[2,128,128]{2,1,0:T(8,128)S(1)}, u32[]{:S(2)}, u32[]{:S(2)}) %collective-permute-start.10) | collective-permute-done | bytes 131104 | tf_op jit(solution)/shard_map/ppermute | solution.py:531
  68.3 0.9 within_chip.1
  69.3 1.9 %collective-permute-done.12.refs_5_ = f32[4,2,128,128]{3,2,1,0:T(8,128)S(1)} collective-permute-done((f32[4,2,128,128]{3,2,1,0:T(8,128)S(1)}, f32[4,2,128,128]{3,2,1,0:T(8,128)S(1)}, u32[]{:S(2)}, u32[]{:S(2)}) %collective-permute-start.12) | collective-permute-done | bytes 524320 | tf_op jit(solution)/shard_map/ppermute | solution.py:531
  71.2 9.0 %grad_pass.1 = (bf16[64,2048]{1,0:T(8,128)(2,1)S(1)}, bf16[64,2048]{1,0:T(8,128)(2,1)S(1)}, bf16[64,2048]{1,0:T(8,128)(2,1)S(1)}, bf16[64,2048]{1,0:T(8,128)(2,1...) custom-call(s32[2]{0:T(128)S(1)} %pad_add_fusion.place_ref, ...), custom_call_target="tpu_custom_call" | custom-call | flops 16000000000 | bytes 1048576 | tf_op jit(solution)/shard_map/grad_pass/pallas_call | solution.py:512
  80.3 2.9 %collective-permute-start.16 = (f32[16,2048]{1,0:T(8,128)S(1)}, f32[16,2048]{1,0:T(8,128)S(1)}, u32[]{:S(2)}, u32[]{:S(2)}) collective-permute-start(f32[16,2048]{1,0:T(8,128)S(1)} %get-tuple-element.100), channel_id=1, source_target_pairs={{4,0},{8,4},{12,8},{16,12},{20,16},{24,20},{28,24},{5,1},{9,5},{13... | collective-permute-start | bytes 393224 | tf_op jit(solution)/shard_map/ppermute | solution.py:527
  83.2 4.8 %collective-permute-start.13 = (bf16[64,2048]{1,0:T(8,128)(2,1)S(1)}, bf16[64,2048]{1,0:T(8,128)(2,1)S(1)}, u32[]{:S(2)}, u32[]{:S(2)}) collective-permute-start(bf16[64,2048]{1,0:T(8,128)(2,1)S(1)} %get-tuple-element.96), channel_id=1, source_target_pairs={{0,1},{1,0},{2,3},{3,2},{4,5},{5,4},{6,7},{7,6},{8,9},{9,8},{10,11... | collective-permute-start | bytes 786440 | tf_op jit(solution)/shard_map/ppermute | solution.py:531
  88.1 2.4 %collective-permute-start.15 = (bf16[64,2048]{1,0:T(8,128)(2,1)S(1)}, bf16[64,2048]{1,0:T(8,128)(2,1)S(1)}, u32[]{:S(2)}, u32[]{:S(2)}) collective-permute-start(bf16[64,2048]{1,0:T(8,128)(2,1)S(1)} %get-tuple-element.98), channel_id=1, source_target_pairs={{0,3},{1,2},{2,1},{3,0},{4,7},{5,6},{6,5},{7,4},{8,11},{9,10},{10,... | collective-permute-start | bytes 786440 | tf_op jit(solution)/shard_map/ppermute | solution.py:531
  90.5 0.9 collective-permute-start.21
  91.4 1.3 %collective-permute-start.19 = (bf16[16,2048]{1,0:T(8,128)(2,1)S(1)}, bf16[16,2048]{1,0:T(8,128)(2,1)S(1)}, u32[]{:S(2)}, u32[]{:S(2)}) collective-permute-start(bf16[16,2048]{1,0:T(8,128)(2,1)S(1)} %add_convert_fusion.refs_7_), channel_id=1, source_target_pairs={{2,3},{6,7},{10,11},{14,15},{18,19},{22,23},{26,27},{30,31}} | collective-permute-start | bytes 196616 | tf_op jit(solution)/shard_map/ppermute | solution.py:692
  92.7 1.8 %collective-permute-done.21 = f32[4,2048]{1,0:T(4,128)S(1)} collective-permute-done((f32[4,2048]{1,0:T(4,128)S(1)}, f32[4,2048]{1,0:T(4,128)S(1)}, u32[]{:S(2)}, u32[]{:S(2)}) %collective-permute-start.21) | collective-permute-done | bytes 32800 | tf_op jit(solution)/shard_map/ppermute | solution.py:531
  94.5 0.1 collective-permute-start.22
  94.7 3.8 %collective-permute-done.22 = f32[4,2048]{1,0:T(4,128)S(1)} collective-permute-done((f32[4,2048]{1,0:T(4,128)S(1)}, f32[4,2048]{1,0:T(4,128)S(1)}, u32[]{:S(2)}, u32[]{:S(2)}) %collective-permute-start.22) | collective-permute-done | bytes 32800 | tf_op jit(solution)/shard_map/ppermute | solution.py:531
  98.5 1.3 %collective-permute-start.18 = (bf16[16,2048]{1,0:T(8,128)(2,1)S(1)}, bf16[16,2048]{1,0:T(8,128)(2,1)S(1)}, u32[]{:S(2)}, u32[]{:S(2)}) collective-permute-start(bf16[16,2048]{1,0:T(8,128)(2,1)S(1)} %add_convert_fusion.refs_7_), channel_id=1, source_target_pairs={{1,3},{5,7},{9,11},{13,15},{17,19},{21,23},{25,27},{29,31}} | collective-permute-start | bytes 196616 | tf_op jit(solution)/shard_map/ppermute | solution.py:692
  99.8 1.0 collective-permute-done.19.refs_6_
  100.7 1.3 %collective-permute-start.17 = (bf16[16,2048]{1,0:T(8,128)(2,1)S(1)}, bf16[16,2048]{1,0:T(8,128)(2,1)S(1)}, u32[]{:S(2)}, u32[]{:S(2)}) collective-permute-start(bf16[16,2048]{1,0:T(8,128)(2,1)S(1)} %add_convert_fusion.refs_7_), channel_id=1, source_target_pairs={{0,3},{4,7},{8,11},{12,15},{16,19},{20,23},{24,27},{28,31}} | collective-permute-start | bytes 196616 | tf_op jit(solution)/shard_map/ppermute | solution.py:692
  102.0 0.6 add.15
  102.7 14.4 %collective-permute-done.18.refs_5_ = bf16[16,2048]{1,0:T(8,128)(2,1)S(1)} collective-permute-done((bf16[16,2048]{1,0:T(8,128)(2,1)S(1)}, bf16[16,2048]{1,0:T(8,128)(2,1)S(1)}, u32[]{:S(2)}, u32[]{:S(2)}) %collective-permute-start.18) | collective-permute-done | bytes 65568 | tf_op jit(solution)/shard_map/ppermute | solution.py:692
  117.1 1.6 %assemble.1 = bf16[64,8192]{1,0:T(8,128)(2,1)} custom-call(s32[2]{0:T(128)S(1)} %pad_add_fusion.place_ref, bf16[64,2048]{1,0:T(8,128)(2,1)S(1)} %get-tuple-element.95.refs_0_, bf16[64,2048]{1,0:T(8,128)(2,1)S(1)} %collective-permute-done.13.refs_1_, bf16[64,2048]{1,0:T(8,128)(2,1)S(1)} %collective-permute-done.14.refs_2_, ...), custom_call_target="tpu_custom_call" | custom-call | bytes 1048576 | tf_op jit(solution)/shard_map/assemble/pallas_call | solution.py:512
  (32 shorter events, 0.4 us)
Async XLA Ops:
  0.7 1.2 %copy-start = (bf16[64,8192]{1,0:T(8,128)(2,1)S(1)}, bf16[64,8192]{1,0:T(8,128)(2,1)}, u32[]{:S(2)}) copy-start(bf16[64,8192]{1,0:T(8,128)(2,1)} %mixed_ref.3) | copy-start | bytes 3145732
  2.5 12.4 %collective-permute-start = (bf16[64,2048]{1,0:T(8,128)(2,1)S(1)}, bf16[64,2048]{1,0:T(8,128)(2,1)S(1)}, u32[]{:S(2)}, u32[]{:S(2)}) collective-permute-start(bf16[64,2048]{1,0:T(8,128)(2,1)S(1)} %get-tuple-element.57), channel_id=1, source_target_pairs={{0,1},{1,0},{2,3},{3,2},{4,5},{5,4},{6,7},{7,6},{8,9},{9,8},{10,11... | collective-permute-start | bytes 786440 | tf_op jit(solution)/shard_map/ppermute | solution.py:531
  3.1 21.4 %collective-permute-start.1 = (bf16[64,2048]{1,0:T(8,128)(2,1)S(1)}, bf16[64,2048]{1,0:T(8,128)(2,1)S(1)}, u32[]{:S(2)}, u32[]{:S(2)}) collective-permute-start(bf16[64,2048]{1,0:T(8,128)(2,1)S(1)} %get-tuple-element.61), channel_id=1, source_target_pairs={{0,2},{1,3},{2,0},{3,1},{4,6},{5,7},{6,4},{7,5},{8,10},{9,11},{10,... | collective-permute-start | bytes 786440 | tf_op jit(solution)/shard_map/ppermute | solution.py:531
  3.4 21.0 %collective-permute-start.2 = (bf16[64,2048]{1,0:T(8,128)(2,1)S(1)}, bf16[64,2048]{1,0:T(8,128)(2,1)S(1)}, u32[]{:S(2)}, u32[]{:S(2)}) collective-permute-start(bf16[64,2048]{1,0:T(8,128)(2,1)S(1)} %get-tuple-element.62), channel_id=1, source_target_pairs={{0,3},{1,2},{2,1},{3,0},{4,7},{5,6},{6,5},{7,4},{8,11},{9,10},{10,... | collective-permute-start | bytes 786440 | tf_op jit(solution)/shard_map/ppermute | solution.py:531
  7.0 1.2 %copy-start.1 = (bf16[64,8192]{1,0:T(8,128)(2,1)S(1)}, bf16[64,8192]{1,0:T(8,128)(2,1)}, u32[]{:S(2)}) copy-start(bf16[64,8192]{1,0:T(8,128)(2,1)} %mixed_ref.3) | copy-start | bytes 3145732
  8.2 1.0 copy-start.2
  9.3 0.8 copy-start.6
  10.0 0.7 copy-start.8
  10.7 0.7 copy-start.9
  24.4 6.5 %collective-permute-start.3 = (bf16[16,2048]{1,0:T(8,128)(2,1)S(1)}, bf16[16,2048]{1,0:T(8,128)(2,1)S(1)}, u32[]{:S(2)}, u32[]{:S(2)}) collective-permute-start(bf16[16,2048]{1,0:T(8,128)(2,1)S(1)} %fusion), channel_id=1, source_target_pairs={{0,4},{4,8},{8,12},{12,16},{16,20},{20,24},{24,28},{1,5},{5,9},{9,... | collective-permute-start | bytes 196616 | tf_op jit(solution)/shard_map/ppermute | solution.py:527
  30.9 27.5 %copy-start.4 = (f32[8,128,128]{2,1,0:T(8,128)S(1)}, f32[8,128,128]{2,1,0:T(8,128)}, u32[]{:S(2)}) copy-start(f32[8,128,128]{2,1,0:T(8,128)} %refs_4_.2) | copy-start | bytes 1572868
  30.9 27.5 %copy-start.5 = (f32[8,128,128]{2,1,0:T(8,128)S(1)}, f32[8,128,128]{2,1,0:T(8,128)}, u32[]{:S(2)}) copy-start(f32[8,128,128]{2,1,0:T(8,128)} %refs_5_.1) | copy-start | bytes 1572868
  43.3 1.8 %collective-permute-start.4 = (f32[2,3,128,128]{3,2,1,0:T(8,128)S(1)}, f32[2,3,128,128]{3,2,1,0:T(8,128)S(1)}, u32[]{:S(2)}, u32[]{:S(2)}) collective-permute-start(f32[2,3,128,128]{3,2,1,0:T(8,128)S(1)} %get-tuple-element.67), channel_id=1, source_target_pairs={{0,4},{4,0},{8,12},{12,8},{16,20},{20,16},{24,28},{28,24},{1,5},{5... | collective-permute-start | bytes 1179656 | tf_op jit(solution)/shard_map/ppermute | solution.py:531
  43.4 2.3 %collective-permute-start.5 = (f32[2,3,128,128]{3,2,1,0:T(8,128)S(1)}, f32[2,3,128,128]{3,2,1,0:T(8,128)S(1)}, u32[]{:S(2)}, u32[]{:S(2)}) collective-permute-start(f32[2,3,128,128]{3,2,1,0:T(8,128)S(1)} %get-tuple-element.68), channel_id=1, source_target_pairs={{0,4},{4,0},{8,12},{12,8},{16,20},{20,16},{24,28},{28,24},{1,5},{5... | collective-permute-start | bytes 1179656 | tf_op jit(solution)/shard_map/ppermute | solution.py:531
  46.8 24.4 %copy-start.3 = (bf16[256,1024]{1,0:T(8,128)(2,1)S(1)}, bf16[256,1024]{1,0:T(8,128)(2,1)}, u32[]{:S(2)}) copy-start(bf16[256,1024]{1,0:T(8,128)(2,1)} %refs_4_.3) | copy-start | bytes 1572868
  46.8 24.4 %copy-start.7 = (f32[4,2048]{1,0:T(4,128)S(1)}, f32[4,2048]{1,0:T(4,128)}, u32[]{:S(2)}) copy-start(f32[4,2048]{1,0:T(4,128)} %refs_0_.1) | copy-start | bytes 98308
  46.9 7.8 %collective-permute-start.6 = (f32[3,128,128]{2,1,0:T(8,128)S(1)}, f32[3,128,128]{2,1,0:T(8,128)S(1)}, u32[]{:S(2)}, u32[]{:S(2)}) collective-permute-start(f32[3,128,128]{2,1,0:T(8,128)S(1)} %get-tuple-element.70), channel_id=1, source_target_pairs={{0,8},{4,12},{8,0},{12,4},{16,24},{20,28},{24,16},{28,20},{1,9},{5... | collective-permute-start | bytes 589832 | tf_op jit(solution)/shard_map/ppermute | solution.py:531
  47.5 10.9 %collective-permute-start.7 = (f32[3,128,128]{2,1,0:T(8,128)S(1)}, f32[3,128,128]{2,1,0:T(8,128)S(1)}, u32[]{:S(2)}, u32[]{:S(2)}) collective-permute-start(f32[3,128,128]{2,1,0:T(8,128)S(1)} %get-tuple-element.71), channel_id=1, source_target_pairs={{0,16},{4,20},{8,24},{12,28},{16,0},{20,4},{24,8},{28,12},{1,17},{... | collective-permute-start | bytes 589832 | tf_op jit(solution)/shard_map/ppermute | solution.py:531
  48.0 10.4 %collective-permute-start.8 = (f32[3,128,128]{2,1,0:T(8,128)S(1)}, f32[3,128,128]{2,1,0:T(8,128)S(1)}, u32[]{:S(2)}, u32[]{:S(2)}) collective-permute-start(f32[3,128,128]{2,1,0:T(8,128)S(1)} %get-tuple-element.72), channel_id=1, source_target_pairs={{0,24},{4,28},{8,16},{12,20},{16,8},{20,12},{24,0},{28,4},{1,25},{... | collective-permute-start | bytes 589832 | tf_op jit(solution)/shard_map/ppermute | solution.py:531
  59.6 5.9 %collective-permute-start.9 = (f32[2,128,128]{2,1,0:T(8,128)S(1)}, f32[2,128,128]{2,1,0:T(8,128)S(1)}, u32[]{:S(2)}, u32[]{:S(2)}) collective-permute-start(f32[2,128,128]{2,1,0:T(8,128)S(1)} %get-tuple-element.74), channel_id=1, source_target_pairs={{0,8},{4,12},{8,0},{12,4},{16,24},{20,28},{24,16},{28,20},{1,9},{5... | collective-permute-start | bytes 393224 | tf_op jit(solution)/shard_map/ppermute | solution.py:531
  61.1 7.2 %collective-permute-start.10 = (f32[2,128,128]{2,1,0:T(8,128)S(1)}, f32[2,128,128]{2,1,0:T(8,128)S(1)}, u32[]{:S(2)}, u32[]{:S(2)}) collective-permute-start(f32[2,128,128]{2,1,0:T(8,128)S(1)} %get-tuple-element.75), channel_id=1, source_target_pairs={{0,16},{4,20},{8,24},{12,28},{16,0},{20,4},{24,8},{28,12},{1,17},{... | collective-permute-start | bytes 393224 | tf_op jit(solution)/shard_map/ppermute | solution.py:531
  61.4 6.9 %collective-permute-start.11 = (f32[2,128,128]{2,1,0:T(8,128)S(1)}, f32[2,128,128]{2,1,0:T(8,128)S(1)}, u32[]{:S(2)}, u32[]{:S(2)}) collective-permute-start(f32[2,128,128]{2,1,0:T(8,128)S(1)} %get-tuple-element.76), channel_id=1, source_target_pairs={{0,24},{4,28},{8,16},{12,20},{16,8},{20,12},{24,0},{28,4},{1,25},{... | collective-permute-start | bytes 393224 | tf_op jit(solution)/shard_map/ppermute | solution.py:531
  69.2 2.0 %collective-permute-start.12 = (f32[4,2,128,128]{3,2,1,0:T(8,128)S(1)}, f32[4,2,128,128]{3,2,1,0:T(8,128)S(1)}, u32[]{:S(2)}, u32[]{:S(2)}) collective-permute-start(f32[4,2,128,128]{3,2,1,0:T(8,128)S(1)} %get-tuple-element.77), channel_id=1, source_target_pairs={{0,4},{4,0},{8,12},{12,8},{16,20},{20,16},{24,28},{28,24},{1,5},{5... | collective-permute-start | bytes 1572872 | tf_op jit(solution)/shard_map/ppermute | solution.py:531
  80.3 11.1 %collective-permute-start.16 = (f32[16,2048]{1,0:T(8,128)S(1)}, f32[16,2048]{1,0:T(8,128)S(1)}, u32[]{:S(2)}, u32[]{:S(2)}) collective-permute-start(f32[16,2048]{1,0:T(8,128)S(1)} %get-tuple-element.100), channel_id=1, source_target_pairs={{4,0},{8,4},{12,8},{16,12},{20,16},{24,20},{28,24},{5,1},{9,5},{13... | collective-permute-start | bytes 393224 | tf_op jit(solution)/shard_map/ppermute | solution.py:527
  83.2 7.3 %collective-permute-start.20 = (f32[4,2048]{1,0:T(4,128)S(1)}, f32[4,2048]{1,0:T(4,128)S(1)}, u32[]{:S(2)}, u32[]{:S(2)}) collective-permute-start(f32[4,2048]{1,0:T(4,128)S(1)} %get-tuple-element.101), channel_id=1, source_target_pairs={{0,4},{4,0},{8,12},{12,8},{16,20},{20,16},{24,28},{28,24},{1,5},{5... | collective-permute-start | bytes 98312 | tf_op jit(solution)/shard_map/ppermute | solution.py:531
  83.2 33.8 %collective-permute-start.13 = (bf16[64,2048]{1,0:T(8,128)(2,1)S(1)}, bf16[64,2048]{1,0:T(8,128)(2,1)S(1)}, u32[]{:S(2)}, u32[]{:S(2)}) collective-permute-start(bf16[64,2048]{1,0:T(8,128)(2,1)S(1)} %get-tuple-element.96), channel_id=1, source_target_pairs={{0,1},{1,0},{2,3},{3,2},{4,5},{5,4},{6,7},{7,6},{8,9},{9,8},{10,11... | collective-permute-start | bytes 786440 | tf_op jit(solution)/shard_map/ppermute | solution.py:531
  88.1 29.0 %collective-permute-start.14 = (bf16[64,2048]{1,0:T(8,128)(2,1)S(1)}, bf16[64,2048]{1,0:T(8,128)(2,1)S(1)}, u32[]{:S(2)}, u32[]{:S(2)}) collective-permute-start(bf16[64,2048]{1,0:T(8,128)(2,1)S(1)} %get-tuple-element.97), channel_id=1, source_target_pairs={{0,2},{1,3},{2,0},{3,1},{4,6},{5,7},{6,4},{7,5},{8,10},{9,11},{10,... | collective-permute-start | bytes 786440 | tf_op jit(solution)/shard_map/ppermute | solution.py:531
  88.1 29.0 %collective-permute-start.15 = (bf16[64,2048]{1,0:T(8,128)(2,1)S(1)}, bf16[64,2048]{1,0:T(8,128)(2,1)S(1)}, u32[]{:S(2)}, u32[]{:S(2)}) collective-permute-start(bf16[64,2048]{1,0:T(8,128)(2,1)S(1)} %get-tuple-element.98), channel_id=1, source_target_pairs={{0,3},{1,2},{2,1},{3,0},{4,7},{5,6},{6,5},{7,4},{8,11},{9,10},{10,... | collective-permute-start | bytes 786440 | tf_op jit(solution)/shard_map/ppermute | solution.py:531
  90.5 4.0 %collective-permute-start.21 = (f32[4,2048]{1,0:T(4,128)S(1)}, f32[4,2048]{1,0:T(4,128)S(1)}, u32[]{:S(2)}, u32[]{:S(2)}) collective-permute-start(f32[4,2048]{1,0:T(4,128)S(1)} %add.13), channel_id=1, source_target_pairs={{0,8},{4,12},{8,0},{12,4},{16,24},{20,28},{24,16},{28,20},{1,9},{5... | collective-permute-start | bytes 98312 | tf_op jit(solution)/shard_map/ppermute | solution.py:531
  91.4 9.3 %collective-permute-start.19 = (bf16[16,2048]{1,0:T(8,128)(2,1)S(1)}, bf16[16,2048]{1,0:T(8,128)(2,1)S(1)}, u32[]{:S(2)}, u32[]{:S(2)}) collective-permute-start(bf16[16,2048]{1,0:T(8,128)(2,1)S(1)} %add_convert_fusion.refs_7_), channel_id=1, source_target_pairs={{2,3},{6,7},{10,11},{14,15},{18,19},{22,23},{26,27},{30,31}} | collective-permute-start | bytes 196616 | tf_op jit(solution)/shard_map/ppermute | solution.py:692
  94.5 4.0 %collective-permute-start.22 = (f32[4,2048]{1,0:T(4,128)S(1)}, f32[4,2048]{1,0:T(4,128)S(1)}, u32[]{:S(2)}, u32[]{:S(2)}) collective-permute-start(f32[4,2048]{1,0:T(4,128)S(1)} %add.14), channel_id=1, source_target_pairs={{0,16},{4,20},{8,24},{12,28},{16,0},{20,4},{24,8},{28,12},{1,17},{... | collective-permute-start | bytes 98312 | tf_op jit(solution)/shard_map/ppermute | solution.py:531
  98.5 18.6 %collective-permute-start.18 = (bf16[16,2048]{1,0:T(8,128)(2,1)S(1)}, bf16[16,2048]{1,0:T(8,128)(2,1)S(1)}, u32[]{:S(2)}, u32[]{:S(2)}) collective-permute-start(bf16[16,2048]{1,0:T(8,128)(2,1)S(1)} %add_convert_fusion.refs_7_), channel_id=1, source_target_pairs={{1,3},{5,7},{9,11},{13,15},{17,19},{21,23},{25,27},{29,31}} | collective-permute-start | bytes 196616 | tf_op jit(solution)/shard_map/ppermute | solution.py:692
  100.7 16.3 %collective-permute-start.17 = (bf16[16,2048]{1,0:T(8,128)(2,1)S(1)}, bf16[16,2048]{1,0:T(8,128)(2,1)S(1)}, u32[]{:S(2)}, u32[]{:S(2)}) collective-permute-start(bf16[16,2048]{1,0:T(8,128)(2,1)S(1)} %add_convert_fusion.refs_7_), channel_id=1, source_target_pairs={{0,3},{4,7},{8,11},{12,15},{16,19},{20,23},{24,27},{28,31}} | collective-permute-start | bytes 196616 | tf_op jit(solution)/shard_map/ppermute | solution.py:692

commit v5 on v4

--- a/solution.py
+++ b/solution.py
@@ -687,7 +687,8 @@
         place, slots, kept, ends, conv_weight, beta, gates, grad_out, pieces
     )
     received = [out_pieces[0]] + [across(out_pieces[s], "head", s) for s in range(1, pieces)]
-    last = (edge + from_behind(spill, "ctx", -1)).astype(bf16)
+    spilled, dweight = lax.optimization_barrier((from_behind(spill, "ctx", -1), dweight))
+    last = (edge + spilled).astype(bf16)
     last_rows = [
         lax.ppermute(
             last, ("ctx", "head"), [(c * pieces + h, (c + 1) * pieces - 1) for c in range(devices)]

time: 119 us -> 119 us (level)
    ppermute x18, waiting for transfers between devices: 33.9 us -> 31.4 us  [across(): lax.ppermute(value, axis, [(i, i ^ by) for i in range(lax.axis_size(axis))])]
    ppermute x3, waiting for transfers between devices: 15.4 us -> 17 us  [on_device(): lax.ppermute(last, ('ctx', 'head'), [(c * pieces + h, (c + 1) * pieces -...]
  transfers between devices with their start and end apart: 23 -> 23, of which waited for: 14 -> 13; matrix products, arithmetic and copies ran while one was open for 1% -> 1% of each run, Pallas kernels for 1% -> 1%
where the time goes in v5:
time: 119 us; the launch traced here: 118 us
  waiting for transfers between devices  52.9 us (44%)
  starting transfers between devices  29.1 us (24%)
  Pallas kernels  28.5 us (24%)
  local copies, waits for them, and re-layouts  5.66 us (5%)
    ppermute x18, waiting for transfers between devices, across(): lax.ppermute(value, axis, [(i, i ^ by) for i in range(lax.axis_size(axis))])  31.4 us
    pallas_call x8, Pallas kernels, call(): pl.pallas_call(kernel, in_specs=[pl.BlockSpec(memory_space=pltpu.SMEM)] +...  28.5 us
    ppermute x18, starting transfers between devices, across(): lax.ppermute(value, axis, [(i, i ^ by) for i in range(lax.axis_size(axis))])  20.4 us
    ppermute x3, waiting for transfers between devices, on_device(): lax.ppermute(last, ('ctx', 'head'), [(c * pieces + h, (c + 1) * pieces -...  17 us
    unnamed x20, local copies, waits for them, and re-layouts  5.66 us
    ppermute x2, starting transfers between devices, from_behind(): return lax.ppermute(value, axis, pairs)  4.81 us
    ppermute x2, waiting for transfers between devices, from_behind(): return lax.ppermute(value, axis, pairs)  4.56 us
    ppermute x3, starting transfers between devices, on_device(): lax.ppermute(last, ('ctx', 'head'), [(c * pieces + h, (c + 1) * pieces -...  3.86 us
  transfers between devices with their start and end apart: 23, of which 13 were waited for; matrix products, arithmetic and copies ran while one was open for 1% of the time, Pallas kernels for 1%

profile of v5, /device:TPU:28, one launch (start us, length us, event | category | flops | bytes accessed | tf_op | source)
XLA Modules:
  0.0 117.7 jit_solution(1898533571062417099)
XLA Ops:
  0.6 0.1 pad_add_fusion.place_ref
  0.7 1.2 %copy-done = bf16[64,8192]{1,0:T(8,128)(2,1)S(1)} copy-done((bf16[64,8192]{1,0:T(8,128)(2,1)S(1)}, bf16[64,8192]{1,0:T(8,128)(2,1)}, u32[]{:S(2)}) %copy-start) | copy-done | bytes 1048600
  1.9 0.6 pack.1
  2.5 0.5 collective-permute-start
  3.1 0.3 collective-permute-start.1
  3.4 3.6 %collective-permute-start.2 = (bf16[64,2048]{1,0:T(8,128)(2,1)S(1)}, bf16[64,2048]{1,0:T(8,128)(2,1)S(1)}, u32[]{:S(2)}, u32[]{:S(2)}) collective-permute-start(bf16[64,2048]{1,0:T(8,128)(2,1)S(1)} %get-tuple-element.64), channel_id=1, source_target_pairs={{0,3},{1,2},{2,1},{3,0},{4,7},{5,6},{6,5},{7,4},{8,11},{9,10},{10,... | collective-permute-start | bytes 786440 | tf_op jit(solution)/shard_map/ppermute | solution.py:531
  7.0 1.2 %copy-done.1 = bf16[64,8192]{1,0:T(8,128)(2,1)S(1)} copy-done((bf16[64,8192]{1,0:T(8,128)(2,1)S(1)}, bf16[64,8192]{1,0:T(8,128)(2,1)}, u32[]{:S(2)}) %copy-start.1) | copy-done | bytes 1048600
  8.2 1.0 copy-done.2
  9.3 0.8 copy-done.6
  10.0 0.7 copy-done.8
  10.7 0.7 copy-done.9
  11.4 1.6 %gates_pass.1 = (f32[8,256,256]{2,1,0:T(8,128)S(1)}, f32[4,256,8]{2,1,0:T(8,128)S(1)}, f32[8,256]{1,0:T(8,128)S(1)}, bf16[64,2048]{1,0:T(8,128)(2,1)S(1)}, f32[4...) custom-call(s32[2]{0:T(128)S(1)} %pad_add_fusion.place_ref, f32[8,256]{1,0:T(8,128)S(1)} %copy-done.8, ...), custom_call_target="tpu_custom_call" | custom-call | bytes 1048576 | tf_op jit(solution)/shard_map/gates_pass/pallas_call | solution.py:512
  13.0 2.0 %collective-permute-done.refs_1_ = bf16[64,2048]{1,0:T(8,128)(2,1)S(1)} collective-permute-done((bf16[64,2048]{1,0:T(8,128)(2,1)S(1)}, bf16[64,2048]{1,0:T(8,128)(2,1)S(1)}, u32[]{:S(2)}, u32[]{:S(2)}) %collective-permute-start) | collective-permute-done | bytes 262176 | tf_op jit(solution)/shard_map/ppermute | solution.py:531
  14.9 9.5 %collective-permute-done.1.refs_2_ = bf16[64,2048]{1,0:T(8,128)(2,1)S(1)} collective-permute-done((bf16[64,2048]{1,0:T(8,128)(2,1)S(1)}, bf16[64,2048]{1,0:T(8,128)(2,1)S(1)}, u32[]{:S(2)}, u32[]{:S(2)}) %collective-permute-start.1) | collective-permute-done | bytes 262176 | tf_op jit(solution)/shard_map/ppermute | solution.py:531
  24.4 1.9 %collective-permute-start.3 = (bf16[16,2048]{1,0:T(8,128)(2,1)S(1)}, bf16[16,2048]{1,0:T(8,128)(2,1)S(1)}, u32[]{:S(2)}, u32[]{:S(2)}) collective-permute-start(bf16[16,2048]{1,0:T(8,128)(2,1)S(1)} %fusion), channel_id=1, source_target_pairs={{0,4},{4,8},{8,12},{12,16},{16,20},{20,24},{24,28},{1,5},{5,9},{9,... | collective-permute-start | bytes 196616 | tf_op jit(solution)/shard_map/ppermute | solution.py:527
  26.4 4.6 %collective-permute-done.3.refs_4_ = bf16[16,2048]{1,0:T(8,128)(2,1)S(1)} collective-permute-done((bf16[16,2048]{1,0:T(8,128)(2,1)S(1)}, bf16[16,2048]{1,0:T(8,128)(2,1)S(1)}, u32[]{:S(2)}, u32[]{:S(2)}) %collective-permute-start.3) | collective-permute-done | bytes 65568 | tf_op jit(solution)/shard_map/ppermute | solution.py:527
  30.9 12.4 %local_pass.1 = (bf16[272,512]{1,0:T(8,128)(2,1)S(1)}, bf16[272,512]{1,0:T(8,128)(2,1)S(1)}, bf16[272,512]{1,0:T(8,128)(2,1)S(1)}, bf16[272,512]{1,0:T(8,128)(2,...) custom-call(s32[2]{0:T(128)S(1)} %pad_add_fusion.place_ref, ...), custom_call_target="tpu_custom_call" | custom-call | flops 24000000000 | bytes 1048576 | tf_op jit(solution)/shard_map/local_pass/pallas_call | solution.py:512
  43.3 0.1 collective-permute-start.4
  43.4 0.5 collective-permute-start.5
  43.9 1.2 %collective-permute-done.4.refs_2_.refs_6_ = f32[2,3,128,128]{3,2,1,0:T(8,128)S(1)} collective-permute-done((f32[2,3,128,128]{3,2,1,0:T(8,128)S(1)}, f32[2,3,128,128]{3,2,1,0:T(8,128)S(1)}, u32[]{:S(2)}, u32[]{:S(2)}) %collective-permute-start.4) | collective-permute-done | bytes 393248 | tf_op jit(solution)/shard_map/ppermute | solution.py:531
  45.1 0.6 collective-permute-done.5.refs_3_.refs_7_
  45.7 1.2 join_cores.1
  46.9 0.7 collective-permute-start.6
  47.5 0.5 collective-permute-start.7
  48.0 2.4 %collective-permute-start.8 = (f32[3,128,128]{2,1,0:T(8,128)S(1)}, f32[3,128,128]{2,1,0:T(8,128)S(1)}, u32[]{:S(2)}, u32[]{:S(2)}) collective-permute-start(f32[3,128,128]{2,1,0:T(8,128)S(1)} %get-tuple-element.74), channel_id=1, source_target_pairs={{0,24},{4,28},{8,16},{12,20},{16,8},{20,12},{24,0},{28,4},{1,25},{... | collective-permute-start | bytes 589832 | tf_op jit(solution)/shard_map/ppermute | solution.py:531
  50.4 4.3 %collective-permute-done.6.refs_1_ = f32[3,128,128]{2,1,0:T(8,128)S(1)} collective-permute-done((f32[3,128,128]{2,1,0:T(8,128)S(1)}, f32[3,128,128]{2,1,0:T(8,128)S(1)}, u32[]{:S(2)}, u32[]{:S(2)}) %collective-permute-start.6) | collective-permute-done | bytes 196640 | tf_op jit(solution)/shard_map/ppermute | solution.py:531
  54.7 3.7 %collective-permute-done.7.refs_2_ = f32[3,128,128]{2,1,0:T(8,128)S(1)} collective-permute-done((f32[3,128,128]{2,1,0:T(8,128)S(1)}, f32[3,128,128]{2,1,0:T(8,128)S(1)}, u32[]{:S(2)}, u32[]{:S(2)}) %collective-permute-start.7) | collective-permute-done | bytes 196640 | tf_op jit(solution)/shard_map/ppermute | solution.py:531
  58.4 1.2 %over_chips.1 = (f32[2,128,128]{2,1,0:T(8,128)S(1)}, f32[2,128,128]{2,1,0:T(8,128)S(1)}, f32[2,128,128]{2,1,0:T(8,128)S(1)}, f32[2,128,128]{2,1,0:T(8,128)S(1)}) custom-call(s32[2]{0:T(128)S(1)} %pad_add_fusion.place_ref, f32[3,128,128]{2,1,0:T(8,128)S(1)} %get-tuple-element.71.refs_0_, f32[3,128,128]{2,1,0:T(8,128)S(1)} %collective-permute-done.6.refs_1_, ...), custom_call_target="tpu_custom_call" | custom-call | bytes 1048576 | tf_op jit(solution)/shard_map/over_chips/pallas_call | solution.py:512
  59.6 1.5 %collective-permute-start.9 = (f32[2,128,128]{2,1,0:T(8,128)S(1)}, f32[2,128,128]{2,1,0:T(8,128)S(1)}, u32[]{:S(2)}, u32[]{:S(2)}) collective-permute-start(f32[2,128,128]{2,1,0:T(8,128)S(1)} %get-tuple-element.76), channel_id=1, source_target_pairs={{0,8},{4,12},{8,0},{12,4},{16,24},{20,28},{24,16},{28,20},{1,9},{5... | collective-permute-start | bytes 393224 | tf_op jit(solution)/shard_map/ppermute | solution.py:531
  61.1 0.3 collective-permute-start.10
  61.4 1.8 %collective-permute-start.11 = (f32[2,128,128]{2,1,0:T(8,128)S(1)}, f32[2,128,128]{2,1,0:T(8,128)S(1)}, u32[]{:S(2)}, u32[]{:S(2)}) collective-permute-start(f32[2,128,128]{2,1,0:T(8,128)S(1)} %get-tuple-element.78), channel_id=1, source_target_pairs={{0,24},{4,28},{8,16},{12,20},{16,8},{20,12},{24,0},{28,4},{1,25},{... | collective-permute-start | bytes 393224 | tf_op jit(solution)/shard_map/ppermute | solution.py:531
  63.2 2.4 %collective-permute-done.9.refs_1_ = f32[2,128,128]{2,1,0:T(8,128)S(1)} collective-permute-done((f32[2,128,128]{2,1,0:T(8,128)S(1)}, f32[2,128,128]{2,1,0:T(8,128)S(1)}, u32[]{:S(2)}, u32[]{:S(2)}) %collective-permute-start.9) | collective-permute-done | bytes 131104 | tf_op jit(solution)/shard_map/ppermute | solution.py:531
  65.6 2.7 %collective-permute-done.10.refs_2_ = f32[2,128,128]{2,1,0:T(8,128)S(1)} collective-permute-done((f32[2,128,128]{2,1,0:T(8,128)S(1)}, f32[2,128,128]{2,1,0:T(8,128)S(1)}, u32[]{:S(2)}, u32[]{:S(2)}) %collective-permute-start.10) | collective-permute-done | bytes 131104 | tf_op jit(solution)/shard_map/ppermute | solution.py:531
  68.3 0.9 within_chip.1
  69.3 1.9 %collective-permute-done.12.refs_5_ = f32[4,2,128,128]{3,2,1,0:T(8,128)S(1)} collective-permute-done((f32[4,2,128,128]{3,2,1,0:T(8,128)S(1)}, f32[4,2,128,128]{3,2,1,0:T(8,128)S(1)}, u32[]{:S(2)}, u32[]{:S(2)}) %collective-permute-start.12) | collective-permute-done | bytes 524320 | tf_op jit(solution)/shard_map/ppermute | solution.py:531
  71.2 9.0 %grad_pass.1 = (bf16[64,2048]{1,0:T(8,128)(2,1)S(1)}, bf16[64,2048]{1,0:T(8,128)(2,1)S(1)}, bf16[64,2048]{1,0:T(8,128)(2,1)S(1)}, bf16[64,2048]{1,0:T(8,128)(2,1...) custom-call(s32[2]{0:T(128)S(1)} %pad_add_fusion.place_ref, ...), custom_call_target="tpu_custom_call" | custom-call | flops 16000000000 | bytes 1048576 | tf_op jit(solution)/shard_map/grad_pass/pallas_call | solution.py:512
  80.3 2.9 %collective-permute-start.16 = (f32[16,2048]{1,0:T(8,128)S(1)}, f32[16,2048]{1,0:T(8,128)S(1)}, u32[]{:S(2)}, u32[]{:S(2)}) collective-permute-start(f32[16,2048]{1,0:T(8,128)S(1)} %get-tuple-element.102), channel_id=1, source_target_pairs={{4,0},{8,4},{12,8},{16,12},{20,16},{24,20},{28,24},{5,1},{9,5},{13... | collective-permute-start | bytes 393224 | tf_op jit(solution)/shard_map/ppermute | solution.py:527
  83.2 4.8 %collective-permute-start.13 = (bf16[64,2048]{1,0:T(8,128)(2,1)S(1)}, bf16[64,2048]{1,0:T(8,128)(2,1)S(1)}, u32[]{:S(2)}, u32[]{:S(2)}) collective-permute-start(bf16[64,2048]{1,0:T(8,128)(2,1)S(1)} %get-tuple-element.98), channel_id=1, source_target_pairs={{0,1},{1,0},{2,3},{3,2},{4,5},{5,4},{6,7},{7,6},{8,9},{9,8},{10,11... | collective-permute-start | bytes 786440 | tf_op jit(solution)/shard_map/ppermute | solution.py:531
  88.0 2.4 %collective-permute-start.15 = (bf16[64,2048]{1,0:T(8,128)(2,1)S(1)}, bf16[64,2048]{1,0:T(8,128)(2,1)S(1)}, u32[]{:S(2)}, u32[]{:S(2)}) collective-permute-start(bf16[64,2048]{1,0:T(8,128)(2,1)S(1)} %get-tuple-element.100), channel_id=1, source_target_pairs={{0,3},{1,2},{2,1},{3,0},{4,7},{5,6},{6,5},{7,4},{8,11},{9,10},{10,... | collective-permute-start | bytes 786440 | tf_op jit(solution)/shard_map/ppermute | solution.py:531
  90.5 1.3 %collective-permute-start.19 = (bf16[16,2048]{1,0:T(8,128)(2,1)S(1)}, bf16[16,2048]{1,0:T(8,128)(2,1)S(1)}, u32[]{:S(2)}, u32[]{:S(2)}) collective-permute-start(bf16[16,2048]{1,0:T(8,128)(2,1)S(1)} %add_convert_fusion.refs_7_), channel_id=1, source_target_pairs={{2,3},{6,7},{10,11},{14,15},{18,19},{22,23},{26,27},{30,31}} | collective-permute-start | bytes 196616 | tf_op jit(solution)/shard_map/ppermute | solution.py:693
  91.8 0.9 collective-permute-start.21
  92.7 3.1 %collective-permute-done.21 = f32[4,2048]{1,0:T(4,128)S(1)} collective-permute-done((f32[4,2048]{1,0:T(4,128)S(1)}, f32[4,2048]{1,0:T(4,128)S(1)}, u32[]{:S(2)}, u32[]{:S(2)}) %collective-permute-start.21) | collective-permute-done | bytes 32800 | tf_op jit(solution)/shard_map/ppermute | solution.py:531
  95.9 3.9 %collective-permute-done.19.refs_6_ = bf16[16,2048]{1,0:T(8,128)(2,1)S(1)} collective-permute-done((bf16[16,2048]{1,0:T(8,128)(2,1)S(1)}, bf16[16,2048]{1,0:T(8,128)(2,1)S(1)}, u32[]{:S(2)}, u32[]{:S(2)}) %collective-permute-start.19) | collective-permute-done | bytes 65568 | tf_op jit(solution)/shard_map/ppermute | solution.py:693
  99.8 1.3 %collective-permute-start.18 = (bf16[16,2048]{1,0:T(8,128)(2,1)S(1)}, bf16[16,2048]{1,0:T(8,128)(2,1)S(1)}, u32[]{:S(2)}, u32[]{:S(2)}) collective-permute-start(bf16[16,2048]{1,0:T(8,128)(2,1)S(1)} %add_convert_fusion.refs_7_), channel_id=1, source_target_pairs={{1,3},{5,7},{9,11},{13,15},{17,19},{21,23},{25,27},{29,31}} | collective-permute-start | bytes 196616 | tf_op jit(solution)/shard_map/ppermute | solution.py:693
  101.1 1.3 %collective-permute-start.17 = (bf16[16,2048]{1,0:T(8,128)(2,1)S(1)}, bf16[16,2048]{1,0:T(8,128)(2,1)S(1)}, u32[]{:S(2)}, u32[]{:S(2)}) collective-permute-start(bf16[16,2048]{1,0:T(8,128)(2,1)S(1)} %add_convert_fusion.refs_7_), channel_id=1, source_target_pairs={{0,3},{4,7},{8,11},{12,15},{16,19},{20,23},{24,27},{28,31}} | collective-permute-start | bytes 196616 | tf_op jit(solution)/shard_map/ppermute | solution.py:693
  102.4 0.6 add.15
  103.0 13.1 %collective-permute-done.18.refs_5_ = bf16[16,2048]{1,0:T(8,128)(2,1)S(1)} collective-permute-done((bf16[16,2048]{1,0:T(8,128)(2,1)S(1)}, bf16[16,2048]{1,0:T(8,128)(2,1)S(1)}, u32[]{:S(2)}, u32[]{:S(2)}) %collective-permute-start.18) | collective-permute-done | bytes 65568 | tf_op jit(solution)/shard_map/ppermute | solution.py:693
  116.1 1.6 %assemble.1 = bf16[64,8192]{1,0:T(8,128)(2,1)} custom-call(s32[2]{0:T(128)S(1)} %pad_add_fusion.place_ref, bf16[64,2048]{1,0:T(8,128)(2,1)S(1)} %get-tuple-element.97.refs_0_, bf16[64,2048]{1,0:T(8,128)(2,1)S(1)} %collective-permute-done.13.refs_1_, bf16[64,2048]{1,0:T(8,128)(2,1)S(1)} %collective-permute-done.14.refs_2_, ...), custom_call_target="tpu_custom_call" | custom-call | bytes 1048576 | tf_op jit(solution)/shard_map/assemble/pallas_call | solution.py:512
  (32 shorter events, 0.3 us)
Async XLA Ops:
  0.7 1.2 %copy-start = (bf16[64,8192]{1,0:T(8,128)(2,1)S(1)}, bf16[64,8192]{1,0:T(8,128)(2,1)}, u32[]{:S(2)}) copy-start(bf16[64,8192]{1,0:T(8,128)(2,1)} %mixed_ref.3) | copy-start | bytes 3145732
  2.5 12.4 %collective-permute-start = (bf16[64,2048]{1,0:T(8,128)(2,1)S(1)}, bf16[64,2048]{1,0:T(8,128)(2,1)S(1)}, u32[]{:S(2)}, u32[]{:S(2)}) collective-permute-start(bf16[64,2048]{1,0:T(8,128)(2,1)S(1)} %get-tuple-element.59), channel_id=1, source_target_pairs={{0,1},{1,0},{2,3},{3,2},{4,5},{5,4},{6,7},{7,6},{8,9},{9,8},{10,11... | collective-permute-start | bytes 786440 | tf_op jit(solution)/shard_map/ppermute | solution.py:531
  3.1 21.4 %collective-permute-start.1 = (bf16[64,2048]{1,0:T(8,128)(2,1)S(1)}, bf16[64,2048]{1,0:T(8,128)(2,1)S(1)}, u32[]{:S(2)}, u32[]{:S(2)}) collective-permute-start(bf16[64,2048]{1,0:T(8,128)(2,1)S(1)} %get-tuple-element.63), channel_id=1, source_target_pairs={{0,2},{1,3},{2,0},{3,1},{4,6},{5,7},{6,4},{7,5},{8,10},{9,11},{10,... | collective-permute-start | bytes 786440 | tf_op jit(solution)/shard_map/ppermute | solution.py:531
  3.4 21.0 %collective-permute-start.2 = (bf16[64,2048]{1,0:T(8,128)(2,1)S(1)}, bf16[64,2048]{1,0:T(8,128)(2,1)S(1)}, u32[]{:S(2)}, u32[]{:S(2)}) collective-permute-start(bf16[64,2048]{1,0:T(8,128)(2,1)S(1)} %get-tuple-element.64), channel_id=1, source_target_pairs={{0,3},{1,2},{2,1},{3,0},{4,7},{5,6},{6,5},{7,4},{8,11},{9,10},{10,... | collective-permute-start | bytes 786440 | tf_op jit(solution)/shard_map/ppermute | solution.py:531
  7.0 1.2 %copy-start.1 = (bf16[64,8192]{1,0:T(8,128)(2,1)S(1)}, bf16[64,8192]{1,0:T(8,128)(2,1)}, u32[]{:S(2)}) copy-start(bf16[64,8192]{1,0:T(8,128)(2,1)} %mixed_ref.3) | copy-start | bytes 3145732
  8.2 1.0 copy-start.2
  9.3 0.8 copy-start.6
  10.0 0.7 copy-start.8
  10.7 0.7 copy-start.9
  24.4 6.5 %collective-permute-start.3 = (bf16[16,2048]{1,0:T(8,128)(2,1)S(1)}, bf16[16,2048]{1,0:T(8,128)(2,1)S(1)}, u32[]{:S(2)}, u32[]{:S(2)}) collective-permute-start(bf16[16,2048]{1,0:T(8,128)(2,1)S(1)} %fusion), channel_id=1, source_target_pairs={{0,4},{4,8},{8,12},{12,16},{16,20},{20,24},{24,28},{1,5},{5,9},{9,... | collective-permute-start | bytes 196616 | tf_op jit(solution)/shard_map/ppermute | solution.py:527
  30.9 27.5 %copy-start.4 = (f32[8,128,128]{2,1,0:T(8,128)S(1)}, f32[8,128,128]{2,1,0:T(8,128)}, u32[]{:S(2)}) copy-start(f32[8,128,128]{2,1,0:T(8,128)} %refs_4_.2) | copy-start | bytes 1572868
  30.9 27.5 %copy-start.5 = (f32[8,128,128]{2,1,0:T(8,128)S(1)}, f32[8,128,128]{2,1,0:T(8,128)}, u32[]{:S(2)}) copy-start(f32[8,128,128]{2,1,0:T(8,128)} %refs_5_.1) | copy-start | bytes 1572868
  43.3 1.8 %collective-permute-start.4 = (f32[2,3,128,128]{3,2,1,0:T(8,128)S(1)}, f32[2,3,128,128]{3,2,1,0:T(8,128)S(1)}, u32[]{:S(2)}, u32[]{:S(2)}) collective-permute-start(f32[2,3,128,128]{3,2,1,0:T(8,128)S(1)} %get-tuple-element.69), channel_id=1, source_target_pairs={{0,4},{4,0},{8,12},{12,8},{16,20},{20,16},{24,28},{28,24},{1,5},{5... | collective-permute-start | bytes 1179656 | tf_op jit(solution)/shard_map/ppermute | solution.py:531
  43.4 2.3 %collective-permute-start.5 = (f32[2,3,128,128]{3,2,1,0:T(8,128)S(1)}, f32[2,3,128,128]{3,2,1,0:T(8,128)S(1)}, u32[]{:S(2)}, u32[]{:S(2)}) collective-permute-start(f32[2,3,128,128]{3,2,1,0:T(8,128)S(1)} %get-tuple-element.70), channel_id=1, source_target_pairs={{0,4},{4,0},{8,12},{12,8},{16,20},{20,16},{24,28},{28,24},{1,5},{5... | collective-permute-start | bytes 1179656 | tf_op jit(solution)/shard_map/ppermute | solution.py:531
  46.8 24.4 %copy-start.3 = (bf16[256,1024]{1,0:T(8,128)(2,1)S(1)}, bf16[256,1024]{1,0:T(8,128)(2,1)}, u32[]{:S(2)}) copy-start(bf16[256,1024]{1,0:T(8,128)(2,1)} %refs_4_.3) | copy-start | bytes 1572868
  46.8 24.4 %copy-start.7 = (f32[4,2048]{1,0:T(4,128)S(1)}, f32[4,2048]{1,0:T(4,128)}, u32[]{:S(2)}) copy-start(f32[4,2048]{1,0:T(4,128)} %refs_0_.1) | copy-start | bytes 98308
  46.9 7.8 %collective-permute-start.6 = (f32[3,128,128]{2,1,0:T(8,128)S(1)}, f32[3,128,128]{2,1,0:T(8,128)S(1)}, u32[]{:S(2)}, u32[]{:S(2)}) collective-permute-start(f32[3,128,128]{2,1,0:T(8,128)S(1)} %get-tuple-element.72), channel_id=1, source_target_pairs={{0,8},{4,12},{8,0},{12,4},{16,24},{20,28},{24,16},{28,20},{1,9},{5... | collective-permute-start | bytes 589832 | tf_op jit(solution)/shard_map/ppermute | solution.py:531
  47.5 10.9 %collective-permute-start.7 = (f32[3,128,128]{2,1,0:T(8,128)S(1)}, f32[3,128,128]{2,1,0:T(8,128)S(1)}, u32[]{:S(2)}, u32[]{:S(2)}) collective-permute-start(f32[3,128,128]{2,1,0:T(8,128)S(1)} %get-tuple-element.73), channel_id=1, source_target_pairs={{0,16},{4,20},{8,24},{12,28},{16,0},{20,4},{24,8},{28,12},{1,17},{... | collective-permute-start | bytes 589832 | tf_op jit(solution)/shard_map/ppermute | solution.py:531
  48.0 10.4 %collective-permute-start.8 = (f32[3,128,128]{2,1,0:T(8,128)S(1)}, f32[3,128,128]{2,1,0:T(8,128)S(1)}, u32[]{:S(2)}, u32[]{:S(2)}) collective-permute-start(f32[3,128,128]{2,1,0:T(8,128)S(1)} %get-tuple-element.74), channel_id=1, source_target_pairs={{0,24},{4,28},{8,16},{12,20},{16,8},{20,12},{24,0},{28,4},{1,25},{... | collective-permute-start | bytes 589832 | tf_op jit(solution)/shard_map/ppermute | solution.py:531
  59.6 5.9 %collective-permute-start.9 = (f32[2,128,128]{2,1,0:T(8,128)S(1)}, f32[2,128,128]{2,1,0:T(8,128)S(1)}, u32[]{:S(2)}, u32[]{:S(2)}) collective-permute-start(f32[2,128,128]{2,1,0:T(8,128)S(1)} %get-tuple-element.76), channel_id=1, source_target_pairs={{0,8},{4,12},{8,0},{12,4},{16,24},{20,28},{24,16},{28,20},{1,9},{5... | collective-permute-start | bytes 393224 | tf_op jit(solution)/shard_map/ppermute | solution.py:531
  61.1 7.2 %collective-permute-start.10 = (f32[2,128,128]{2,1,0:T(8,128)S(1)}, f32[2,128,128]{2,1,0:T(8,128)S(1)}, u32[]{:S(2)}, u32[]{:S(2)}) collective-permute-start(f32[2,128,128]{2,1,0:T(8,128)S(1)} %get-tuple-element.77), channel_id=1, source_target_pairs={{0,16},{4,20},{8,24},{12,28},{16,0},{20,4},{24,8},{28,12},{1,17},{... | collective-permute-start | bytes 393224 | tf_op jit(solution)/shard_map/ppermute | solution.py:531
  61.4 6.9 %collective-permute-start.11 = (f32[2,128,128]{2,1,0:T(8,128)S(1)}, f32[2,128,128]{2,1,0:T(8,128)S(1)}, u32[]{:S(2)}, u32[]{:S(2)}) collective-permute-start(f32[2,128,128]{2,1,0:T(8,128)S(1)} %get-tuple-element.78), channel_id=1, source_target_pairs={{0,24},{4,28},{8,16},{12,20},{16,8},{20,12},{24,0},{28,4},{1,25},{... | collective-permute-start | bytes 393224 | tf_op jit(solution)/shard_map/ppermute | solution.py:531
  69.2 2.0 %collective-permute-start.12 = (f32[4,2,128,128]{3,2,1,0:T(8,128)S(1)}, f32[4,2,128,128]{3,2,1,0:T(8,128)S(1)}, u32[]{:S(2)}, u32[]{:S(2)}) collective-permute-start(f32[4,2,128,128]{3,2,1,0:T(8,128)S(1)} %get-tuple-element.79), channel_id=1, source_target_pairs={{0,4},{4,0},{8,12},{12,8},{16,20},{20,16},{24,28},{28,24},{1,5},{5... | collective-permute-start | bytes 1572872 | tf_op jit(solution)/shard_map/ppermute | solution.py:531
  80.3 10.2 %collective-permute-start.16 = (f32[16,2048]{1,0:T(8,128)S(1)}, f32[16,2048]{1,0:T(8,128)S(1)}, u32[]{:S(2)}, u32[]{:S(2)}) collective-permute-start(f32[16,2048]{1,0:T(8,128)S(1)} %get-tuple-element.102), channel_id=1, source_target_pairs={{4,0},{8,4},{12,8},{16,12},{20,16},{24,20},{28,24},{5,1},{9,5},{13... | collective-permute-start | bytes 393224 | tf_op jit(solution)/shard_map/ppermute | solution.py:527
  83.2 32.9 %collective-permute-start.13 = (bf16[64,2048]{1,0:T(8,128)(2,1)S(1)}, bf16[64,2048]{1,0:T(8,128)(2,1)S(1)}, u32[]{:S(2)}, u32[]{:S(2)}) collective-permute-start(bf16[64,2048]{1,0:T(8,128)(2,1)S(1)} %get-tuple-element.98), channel_id=1, source_target_pairs={{0,1},{1,0},{2,3},{3,2},{4,5},{5,4},{6,7},{7,6},{8,9},{9,8},{10,11... | collective-permute-start | bytes 786440 | tf_op jit(solution)/shard_map/ppermute | solution.py:531
  88.0 28.1 %collective-permute-start.14 = (bf16[64,2048]{1,0:T(8,128)(2,1)S(1)}, bf16[64,2048]{1,0:T(8,128)(2,1)S(1)}, u32[]{:S(2)}, u32[]{:S(2)}) collective-permute-start(bf16[64,2048]{1,0:T(8,128)(2,1)S(1)} %get-tuple-element.99), channel_id=1, source_target_pairs={{0,2},{1,3},{2,0},{3,1},{4,6},{5,7},{6,4},{7,5},{8,10},{9,11},{10,... | collective-permute-start | bytes 786440 | tf_op jit(solution)/shard_map/ppermute | solution.py:531
  88.0 28.1 %collective-permute-start.15 = (bf16[64,2048]{1,0:T(8,128)(2,1)S(1)}, bf16[64,2048]{1,0:T(8,128)(2,1)S(1)}, u32[]{:S(2)}, u32[]{:S(2)}) collective-permute-start(bf16[64,2048]{1,0:T(8,128)(2,1)S(1)} %get-tuple-element.100), channel_id=1, source_target_pairs={{0,3},{1,2},{2,1},{3,0},{4,7},{5,6},{6,5},{7,4},{8,11},{9,10},{10,... | collective-permute-start | bytes 786440 | tf_op jit(solution)/shard_map/ppermute | solution.py:531
  90.4 1.3 %collective-permute-start.20 = (f32[4,2048]{1,0:T(4,128)S(1)}, f32[4,2048]{1,0:T(4,128)S(1)}, u32[]{:S(2)}, u32[]{:S(2)}) collective-permute-start(f32[4,2048]{1,0:T(4,128)S(1)} %get-tuple-element.105), channel_id=1, source_target_pairs={{0,4},{4,0},{8,12},{12,8},{16,20},{20,16},{24,28},{28,24},{1,5},{5... | collective-permute-start | bytes 98312 | tf_op jit(solution)/shard_map/ppermute | solution.py:531
  90.5 9.3 %collective-permute-start.19 = (bf16[16,2048]{1,0:T(8,128)(2,1)S(1)}, bf16[16,2048]{1,0:T(8,128)(2,1)S(1)}, u32[]{:S(2)}, u32[]{:S(2)}) collective-permute-start(bf16[16,2048]{1,0:T(8,128)(2,1)S(1)} %add_convert_fusion.refs_7_), channel_id=1, source_target_pairs={{2,3},{6,7},{10,11},{14,15},{18,19},{22,23},{26,27},{30,31}} | collective-permute-start | bytes 196616 | tf_op jit(solution)/shard_map/ppermute | solution.py:693
  91.8 4.0 %collective-permute-start.21 = (f32[4,2048]{1,0:T(4,128)S(1)}, f32[4,2048]{1,0:T(4,128)S(1)}, u32[]{:S(2)}, u32[]{:S(2)}) collective-permute-start(f32[4,2048]{1,0:T(4,128)S(1)} %add.13), channel_id=1, source_target_pairs={{0,8},{4,12},{8,0},{12,4},{16,24},{20,28},{24,16},{28,20},{1,9},{5... | collective-permute-start | bytes 98312 | tf_op jit(solution)/shard_map/ppermute | solution.py:531
  95.8 5.3 %collective-permute-start.22 = (f32[4,2048]{1,0:T(4,128)S(1)}, f32[4,2048]{1,0:T(4,128)S(1)}, u32[]{:S(2)}, u32[]{:S(2)}) collective-permute-start(f32[4,2048]{1,0:T(4,128)S(1)} %add.14), channel_id=1, source_target_pairs={{0,16},{4,20},{8,24},{12,28},{16,0},{20,4},{24,8},{28,12},{1,17},{... | collective-permute-start | bytes 98312 | tf_op jit(solution)/shard_map/ppermute | solution.py:531
  99.8 16.3 %collective-permute-start.18 = (bf16[16,2048]{1,0:T(8,128)(2,1)S(1)}, bf16[16,2048]{1,0:T(8,128)(2,1)S(1)}, u32[]{:S(2)}, u32[]{:S(2)}) collective-permute-start(bf16[16,2048]{1,0:T(8,128)(2,1)S(1)} %add_convert_fusion.refs_7_), channel_id=1, source_target_pairs={{1,3},{5,7},{9,11},{13,15},{17,19},{21,23},{25,27},{29,31}} | collective-permute-start | bytes 196616 | tf_op jit(solution)/shard_map/ppermute | solution.py:693
  101.1 15.0 %collective-permute-start.17 = (bf16[16,2048]{1,0:T(8,128)(2,1)S(1)}, bf16[16,2048]{1,0:T(8,128)(2,1)S(1)}, u32[]{:S(2)}, u32[]{:S(2)}) collective-permute-start(bf16[16,2048]{1,0:T(8,128)(2,1)S(1)} %add_convert_fusion.refs_7_), channel_id=1, source_target_pairs={{0,3},{4,7},{8,11},{12,15},{16,19},{20,23},{24,27},{28,31}} | collective-permute-start | bytes 196616 | tf_op jit(solution)/shard_map/ppermute | solution.py:693
